TPU v7x, 32 devices: a whole 2x2x4 slice. The times are simulated.
32 devices in a mesh: ctx: 2 (over x), shard: 4 (over z), rep: 4 (over y, core).
Axes of the slice: x: 2, y: 2, z: 4, core: 2. Of those that a mesh axis runs over, the one named last changes fastest.
Arguments:
- frames: bfloat16 [16, 1024, 1536], P(('shard', 'rep'), 'ctx'), may hold values from -6 to 6
- text_states: bfloat16 [16, 64, 1536], P(('shard', 'rep')), may hold values from -6 to 6
- first_gain: bfloat16 [1536], P('shard'), may hold values from 0.5 to 1.5
- first_shift: bfloat16 [1536], P('shard'), may hold values from -2 to 2
- self_query: bfloat16 [1536, 1536], P('shard'), may hold values from -0.15625 to 0.15625
- self_key: bfloat16 [1536, 1536], P('shard'), may hold values from -0.15625 to 0.15625
- self_value: bfloat16 [1536, 1536], P('shard'), may hold values from -0.15625 to 0.15625
- self_output: bfloat16 [1536, 1536], P('shard'), may hold values from -0.875 to 0.875
- second_gain: bfloat16 [1536], P('shard'), may hold values from 0.5 to 1.5
- second_shift: bfloat16 [1536], P('shard'), may hold values from -2 to 2
- cross_query: bfloat16 [1536, 1536], P('shard'), may hold values from -0.15625 to 0.15625
- cross_key: bfloat16 [1536, 1536], P('shard'), may hold values from -0.15625 to 0.15625
- cross_value: bfloat16 [1536, 1536], P('shard'), may hold values from -0.15625 to 0.15625
- cross_output: bfloat16 [1536, 1536], P('shard'), may hold values from -0.625 to 0.625
- third_gain: bfloat16 [1536], P('shard'), may hold values from 0.5 to 1.5
- third_shift: bfloat16 [1536], P('shard'), may hold values from -2 to 2
- up_weight: bfloat16 [1536, 6144], P('shard'), may hold values from -0.15625 to 0.15625
- down_weight: bfloat16 [6144, 1536], P('shard'), may hold values from -0.078125 to 0.078125
- cotangent: bfloat16 [16, 1024, 1536], P(('shard', 'rep'), 'ctx'), may hold values from -6 to 6
Outputs:
- mixed: bfloat16 [16, 1024, 1536], P(('shard', 'rep'), 'ctx')
- grad_frames: float32 [16, 1024, 1536], P(('shard', 'rep'), 'ctx')
- grad_text: float32 [16, 64, 1536], P(('shard', 'rep'))
- grad_first_gain: float32 [1536], P('shard')
- grad_first_shift: float32 [1536], P('shard')
- grad_self_query: float32 [1536, 1536], P('shard')
- grad_self_key: float32 [1536, 1536], P('shard')
- grad_self_value: float32 [1536, 1536], P('shard')
- grad_self_output: float32 [1536, 1536], P('shard')
- grad_second_gain: float32 [1536], P('shard')
- grad_second_shift: float32 [1536], P('shard')
- grad_cross_query: float32 [1536, 1536], P('shard')
- grad_cross_key: float32 [1536, 1536], P('shard')
- grad_cross_value: float32 [1536, 1536], P('shard')
- grad_cross_output: float32 [1536, 1536], P('shard')
- grad_third_gain: float32 [1536], P('shard')
- grad_third_shift: float32 [1536], P('shard')
- grad_up_weight: float32 [1536, 6144], P('shard')
- grad_down_weight: float32 [6144, 1536], P('shard')
All inputs are finite; a program needn't handle non-finite values.
Results may differ from a plain program's by a relative error of at most 0.024.
Values may be sent and summed in bfloat16 or wider, within the bound.
No kernel may reach another device: no remote copies, remote signals or barrier semaphores. Data moves between devices by JAX's collectives and lax.ppermute only.
A program may use at most 384 MiB of HBM per device.

v0:
```python
from functools import partial

import jax
import jax.numpy as jnp
from jax import lax
from jax.sharding import PartitionSpec as P

HD = 64
HEAD_GROUP = 6


EPS = 1e-05
NEG = -1e30


def shifted(block, axis, distance):
    devices = range(lax.axis_size(axis))
    route = [(i - distance, i) for i in devices if i - distance in devices]
    return lax.ppermute(block, axis, route)


def layer_norm(hidden, gain, shift):
    mean = jnp.mean(hidden, axis=-1, keepdims=True)
    centred = hidden - mean
    spread = jnp.mean(centred * centred, axis=-1, keepdims=True)
    return centred * lax.rsqrt(spread + EPS) * gain + shift


def product(left, right):
    return jnp.dot(left, right, preferred_element_type=jnp.float32)


def over_rows(left, right):
    return lax.dot_general(
        left, right, (((0,), (0,)), ((), ())), preferred_element_type=jnp.float32
    )


def against(left, right):
    return lax.dot_general(
        left, right, (((1,), (1,)), ((), ())), preferred_element_type=jnp.float32
    )


def to_groups(array, groups):
    clips, length, width = array.shape
    return jnp.moveaxis(array.reshape(clips, length, groups, width // (groups * HD), HD), 2, 0)


def from_groups(array):
    groups, clips, length, inner, depth = array.shape
    return jnp.moveaxis(array, 0, 2).reshape(clips, length, groups * inner * depth)


def norm_backward(hidden, gain, shift, grad_normed):
    unused, pullback = jax.vjp(
        layer_norm, hidden, gain.astype(jnp.float32), shift.astype(jnp.float32)
    )
    return pullback(grad_normed)


def local(
    frames,
    text_states,
    first_gain,
    first_shift,
    self_query,
    self_key,
    self_value,
    self_output,
    second_gain,
    second_shift,
    cross_query,
    cross_key,
    cross_value,
    cross_output,
    third_gain,
    third_shift,
    up_weight,
    down_weight,
    cotangent,
):
    clips, span, width = frames.shape
    texts = text_states.shape[1]
    rows = clips * span
    heads = width // HD
    groups = heads // HEAD_GROUP
    scale = HD ** (-0.5)
    position = lax.axis_index("ctx")
    bf16 = jnp.bfloat16
    f32 = jnp.float32
    query_pos = position * span + jnp.arange(span, dtype=jnp.int32)
    key_pos = (position - 1) * span + jnp.arange(2 * span, dtype=jnp.int32)
    allowed = (key_pos[None, :] >= 0) & (key_pos[None, :] <= query_pos[:, None])

    def self_scores(queries, keys):
        raw = jnp.einsum("bqgd,bkgd->bgqk", queries, keys, preferred_element_type=f32) * scale
        return jnp.where(allowed, raw, NEG)

    def attend_group(parts):
        queries, keys, values = parts
        scores = self_scores(queries, keys)
        top = jnp.max(scores, axis=-1, keepdims=True)
        weights = jnp.exp(scores - top)
        total = jnp.sum(weights, axis=-1, keepdims=True)
        probs = (weights / total).astype(bf16)
        output = jnp.einsum("bgqk,bkgd->bqgd", probs, values, preferred_element_type=f32).astype(
            bf16
        )
        return (output, (top + jnp.log(total))[..., 0])

    def attend_back(parts):
        queries, keys, values, grad_out, log_total = parts
        scores = self_scores(queries, keys)
        probs = jnp.exp(scores - log_total[..., None])
        grad_probs = jnp.einsum("bqgd,bkgd->bgqk", grad_out, values, preferred_element_type=f32)
        delta = jnp.sum(probs * grad_probs, axis=-1, keepdims=True)
        grad_scores = (probs * (grad_probs - delta)).astype(bf16)
        grad_q = (
            jnp.einsum("bgqk,bkgd->bqgd", grad_scores, keys, preferred_element_type=f32) * scale
        ).astype(bf16)
        grad_k = (
            jnp.einsum("bgqk,bqgd->bkgd", grad_scores, queries, preferred_element_type=f32) * scale
        )
        grad_v = jnp.einsum(
            "bgqk,bqgd->bkgd", probs.astype(bf16), grad_out, preferred_element_type=f32
        )
        return (grad_q, grad_k, grad_v)

    frames_flat = frames.reshape(rows, width).astype(f32)
    gain_first, shift_first, query_whole, key_whole, value_whole, output_whole = (
        lax.all_gather(first_gain, "shard", axis=0, tiled=True),
        lax.all_gather(first_shift, "shard", axis=0, tiled=True),
        lax.all_gather(self_query, "shard", axis=0, tiled=True),
        lax.all_gather(self_key, "shard", axis=0, tiled=True),
        lax.all_gather(self_value, "shard", axis=0, tiled=True),
        lax.all_gather(self_output, "shard", axis=0, tiled=True),
    )
    normed_first = layer_norm(frames_flat, gain_first.astype(f32), shift_first.astype(f32)).astype(
        bf16
    )
    queries = product(normed_first, query_whole).astype(bf16).reshape(clips, span, width)
    keys_own = product(normed_first, key_whole).astype(bf16).reshape(clips, span, width)
    values_own = product(normed_first, value_whole).astype(bf16).reshape(clips, span, width)
    keys_prev, values_prev = shifted((keys_own, values_own), "ctx", 1)
    query_groups = to_groups(queries, groups)
    key_groups = to_groups(jnp.concatenate([keys_prev, keys_own], axis=1), groups)
    value_groups = to_groups(jnp.concatenate([values_prev, values_own], axis=1), groups)
    out_groups, log_totals = lax.map(attend_group, (query_groups, key_groups, value_groups))
    attended = from_groups(out_groups).reshape(rows, width)
    hidden_one = frames_flat + product(attended, output_whole)
    gain_second, shift_second, cquery_whole, ckey_whole, cvalue_whole, coutput_whole = (
        lax.all_gather(second_gain, "shard", axis=0, tiled=True),
        lax.all_gather(second_shift, "shard", axis=0, tiled=True),
        lax.all_gather(cross_query, "shard", axis=0, tiled=True),
        lax.all_gather(cross_key, "shard", axis=0, tiled=True),
        lax.all_gather(cross_value, "shard", axis=0, tiled=True),
        lax.all_gather(cross_output, "shard", axis=0, tiled=True),
    )
    normed_second = layer_norm(
        hidden_one, gain_second.astype(f32), shift_second.astype(f32)
    ).astype(bf16)
    text_flat = text_states.reshape(clips * texts, width)
    cross_q = product(normed_second, cquery_whole).astype(bf16).reshape(clips, span, heads, HD)
    cross_k = product(text_flat, ckey_whole).astype(bf16).reshape(clips, texts, heads, HD)
    cross_v = product(text_flat, cvalue_whole).astype(bf16).reshape(clips, texts, heads, HD)
    cross_scores = (
        jnp.einsum("bqhd,bkhd->bhqk", cross_q, cross_k, preferred_element_type=f32) * scale
    )
    cross_top = jnp.max(cross_scores, axis=-1, keepdims=True)
    cross_weights = jnp.exp(cross_scores - cross_top)
    cross_probs = cross_weights / jnp.sum(cross_weights, axis=-1, keepdims=True)
    cross_low = cross_probs.astype(bf16)
    cross_att = jnp.einsum(
        "bhqk,bkhd->bqhd", cross_low, cross_v, preferred_element_type=f32
    ).astype(bf16)
    cross_att = cross_att.reshape(rows, width)
    hidden_two = hidden_one + product(cross_att, coutput_whole)
    gain_third, shift_third, up_whole, down_whole = (
        lax.all_gather(third_gain, "shard", axis=0, tiled=True),
        lax.all_gather(third_shift, "shard", axis=0, tiled=True),
        lax.all_gather(up_weight, "shard", axis=0, tiled=True),
        lax.all_gather(down_weight, "shard", axis=0, tiled=True),
    )
    normed_third = layer_norm(hidden_two, gain_third.astype(f32), shift_third.astype(f32)).astype(
        bf16
    )
    pre_act = product(normed_third, up_whole)
    activated = jax.nn.gelu(pre_act, approximate=False).astype(bf16)
    mixed = (hidden_two + product(activated, down_whole)).astype(bf16).reshape(clips, span, width)
    (
        gain_first,
        shift_first,
        query_whole,
        key_whole,
        value_whole,
        output_whole,
        gain_second,
        shift_second,
        cquery_whole,
        ckey_whole,
        cvalue_whole,
        coutput_whole,
        gain_third,
        shift_third,
        up_whole,
        down_whole,
    ) = (
        lax.all_gather(first_gain, "shard", axis=0, tiled=True),
        lax.all_gather(first_shift, "shard", axis=0, tiled=True),
        lax.all_gather(self_query, "shard", axis=0, tiled=True),
        lax.all_gather(self_key, "shard", axis=0, tiled=True),
        lax.all_gather(self_value, "shard", axis=0, tiled=True),
        lax.all_gather(self_output, "shard", axis=0, tiled=True),
        lax.all_gather(second_gain, "shard", axis=0, tiled=True),
        lax.all_gather(second_shift, "shard", axis=0, tiled=True),
        lax.all_gather(cross_query, "shard", axis=0, tiled=True),
        lax.all_gather(cross_key, "shard", axis=0, tiled=True),
        lax.all_gather(cross_value, "shard", axis=0, tiled=True),
        lax.all_gather(cross_output, "shard", axis=0, tiled=True),
        lax.all_gather(third_gain, "shard", axis=0, tiled=True),
        lax.all_gather(third_shift, "shard", axis=0, tiled=True),
        lax.all_gather(up_weight, "shard", axis=0, tiled=True),
        lax.all_gather(down_weight, "shard", axis=0, tiled=True),
    )
    grad_res = cotangent.reshape(rows, width).astype(f32)
    grad_branch = grad_res.astype(bf16)
    grad_down = over_rows(activated, grad_branch)
    grad_act = against(grad_branch, down_whole)
    unused, gelu_back = jax.vjp(partial(jax.nn.gelu, approximate=False), pre_act)
    grad_pre = gelu_back(grad_act)[0].astype(bf16)
    grad_up = over_rows(normed_third, grad_pre)
    grad_hid, grad_gain_third, grad_shift_third = norm_backward(
        hidden_two, gain_third, shift_third, against(grad_pre, up_whole)
    )
    grad_res = grad_res + grad_hid
    grad_branch = grad_res.astype(bf16)
    grad_coutput = over_rows(cross_att, grad_branch)
    grad_catt = against(grad_branch, coutput_whole).astype(bf16).reshape(clips, span, heads, HD)
    grad_cprobs = jnp.einsum("bqhd,bkhd->bhqk", grad_catt, cross_v, preferred_element_type=f32)
    cross_delta = jnp.sum(cross_probs * grad_cprobs, axis=-1, keepdims=True)
    grad_cscores = (cross_probs * (grad_cprobs - cross_delta)).astype(bf16)
    grad_cq = (
        jnp.einsum("bhqk,bkhd->bqhd", grad_cscores, cross_k, preferred_element_type=f32) * scale
    )
    grad_cq = grad_cq.astype(bf16).reshape(rows, width)
    part_keys = (
        jnp.einsum("bhqk,bqhd->bkhd", grad_cscores, cross_q, preferred_element_type=f32) * scale
    )
    part_values = jnp.einsum("bhqk,bqhd->bkhd", cross_low, grad_catt, preferred_element_type=f32)
    summed_keys, summed_values = (
        lax.psum(part_keys.astype(jnp.bfloat16), "ctx").astype(jnp.float32),
        lax.psum(part_values.astype(jnp.bfloat16), "ctx").astype(jnp.float32),
    )
    grad_ck = summed_keys.astype(bf16).reshape(clips, texts, width)
    grad_cv = summed_values.astype(bf16).reshape(clips, texts, width)
    half = texts // lax.axis_size("ctx")
    start = position * half
    text_part = lax.dynamic_slice_in_dim(text_states, start, half, 1).reshape(clips * half, width)
    grad_ckey = over_rows(
        text_part, lax.dynamic_slice_in_dim(grad_ck, start, half, 1).reshape(clips * half, width)
    )
    grad_cvalue = over_rows(
        text_part, lax.dynamic_slice_in_dim(grad_cv, start, half, 1).reshape(clips * half, width)
    )
    grad_text = against(grad_ck.reshape(clips * texts, width), ckey_whole)
    grad_text = (grad_text + against(grad_cv.reshape(clips * texts, width), cvalue_whole)).reshape(
        clips, texts, width
    )
    grad_cquery = over_rows(normed_second, grad_cq)
    grad_hid, grad_gain_second, grad_shift_second = norm_backward(
        hidden_one, gain_second, shift_second, against(grad_cq, cquery_whole)
    )
    grad_res = grad_res + grad_hid
    grad_branch = grad_res.astype(bf16)
    grad_output = over_rows(attended, grad_branch)
    grad_att = against(grad_branch, output_whole).astype(bf16).reshape(clips, span, width)
    grad_qg, grad_kg, grad_vg = lax.map(
        attend_back,
        (query_groups, key_groups, value_groups, to_groups(grad_att, groups), log_totals),
    )
    grad_queries = from_groups(grad_qg).reshape(rows, width)
    grad_keys_all = from_groups(grad_kg)
    grad_values_all = from_groups(grad_vg)
    back_keys, back_values = (
        shifted(grad_keys_all[:, :span].astype(jnp.bfloat16), "ctx", -1).astype(jnp.float32),
        shifted(grad_values_all[:, :span].astype(jnp.bfloat16), "ctx", -1).astype(jnp.float32),
    )
    grad_keys = (grad_keys_all[:, span:] + back_keys).astype(bf16).reshape(rows, width)
    grad_values = (grad_values_all[:, span:] + back_values).astype(bf16).reshape(rows, width)
    grad_query = over_rows(normed_first, grad_queries)
    grad_key = over_rows(normed_first, grad_keys)
    grad_value = over_rows(normed_first, grad_values)
    grad_normed = (
        against(grad_queries, query_whole)
        + against(grad_keys, key_whole)
        + against(grad_values, value_whole)
    )
    grad_hid, grad_gain_first, grad_shift_first = norm_backward(
        frames_flat, gain_first, shift_first, grad_normed
    )
    grad_frames = (grad_res + grad_hid).reshape(clips, span, width)
    owned = (
        lax.psum_scatter(
            grad_gain_first.astype(jnp.bfloat16), "shard", scatter_dimension=0, tiled=True
        ).astype(jnp.float32),
        lax.psum_scatter(
            grad_shift_first.astype(jnp.bfloat16), "shard", scatter_dimension=0, tiled=True
        ).astype(jnp.float32),
        lax.psum_scatter(
            grad_query.astype(jnp.bfloat16), "shard", scatter_dimension=0, tiled=True
        ).astype(jnp.float32),
        lax.psum_scatter(
            grad_key.astype(jnp.bfloat16), "shard", scatter_dimension=0, tiled=True
        ).astype(jnp.float32),
        lax.psum_scatter(
            grad_value.astype(jnp.bfloat16), "shard", scatter_dimension=0, tiled=True
        ).astype(jnp.float32),
        lax.psum_scatter(
            grad_output.astype(jnp.bfloat16), "shard", scatter_dimension=0, tiled=True
        ).astype(jnp.float32),
        lax.psum_scatter(
            grad_gain_second.astype(jnp.bfloat16), "shard", scatter_dimension=0, tiled=True
        ).astype(jnp.float32),
        lax.psum_scatter(
            grad_shift_second.astype(jnp.bfloat16), "shard", scatter_dimension=0, tiled=True
        ).astype(jnp.float32),
        lax.psum_scatter(
            grad_cquery.astype(jnp.bfloat16), "shard", scatter_dimension=0, tiled=True
        ).astype(jnp.float32),
        lax.psum_scatter(
            grad_ckey.astype(jnp.bfloat16), "shard", scatter_dimension=0, tiled=True
        ).astype(jnp.float32),
        lax.psum_scatter(
            grad_cvalue.astype(jnp.bfloat16), "shard", scatter_dimension=0, tiled=True
        ).astype(jnp.float32),
        lax.psum_scatter(
            grad_coutput.astype(jnp.bfloat16), "shard", scatter_dimension=0, tiled=True
        ).astype(jnp.float32),
        lax.psum_scatter(
            grad_gain_third.astype(jnp.bfloat16), "shard", scatter_dimension=0, tiled=True
        ).astype(jnp.float32),
        lax.psum_scatter(
            grad_shift_third.astype(jnp.bfloat16), "shard", scatter_dimension=0, tiled=True
        ).astype(jnp.float32),
        lax.psum_scatter(
            grad_up.astype(jnp.bfloat16), "shard", scatter_dimension=0, tiled=True
        ).astype(jnp.float32),
        lax.psum_scatter(
            grad_down.astype(jnp.bfloat16), "shard", scatter_dimension=0, tiled=True
        ).astype(jnp.float32),
    )
    (
        own_a,
        own_b,
        own_c,
        own_d,
        own_e,
        own_f,
        own_g,
        own_h,
        own_i,
        own_j,
        own_k,
        own_l,
        own_m,
        own_n,
        own_o,
        own_p,
    ) = owned
    totals = (
        lax.psum(own_a.astype(jnp.bfloat16), ("ctx", "rep")).astype(jnp.float32),
        lax.psum(own_b.astype(jnp.bfloat16), ("ctx", "rep")).astype(jnp.float32),
        lax.psum(own_c.astype(jnp.bfloat16), ("ctx", "rep")).astype(jnp.float32),
        lax.psum(own_d.astype(jnp.bfloat16), ("ctx", "rep")).astype(jnp.float32),
        lax.psum(own_e.astype(jnp.bfloat16), ("ctx", "rep")).astype(jnp.float32),
        lax.psum(own_f.astype(jnp.bfloat16), ("ctx", "rep")).astype(jnp.float32),
        lax.psum(own_g.astype(jnp.bfloat16), ("ctx", "rep")).astype(jnp.float32),
        lax.psum(own_h.astype(jnp.bfloat16), ("ctx", "rep")).astype(jnp.float32),
        lax.psum(own_i.astype(jnp.bfloat16), ("ctx", "rep")).astype(jnp.float32),
        lax.psum(own_j.astype(jnp.bfloat16), ("ctx", "rep")).astype(jnp.float32),
        lax.psum(own_k.astype(jnp.bfloat16), ("ctx", "rep")).astype(jnp.float32),
        lax.psum(own_l.astype(jnp.bfloat16), ("ctx", "rep")).astype(jnp.float32),
        lax.psum(own_m.astype(jnp.bfloat16), ("ctx", "rep")).astype(jnp.float32),
        lax.psum(own_n.astype(jnp.bfloat16), ("ctx", "rep")).astype(jnp.float32),
        lax.psum(own_o.astype(jnp.bfloat16), ("ctx", "rep")).astype(jnp.float32),
        lax.psum(own_p.astype(jnp.bfloat16), ("ctx", "rep")).astype(jnp.float32),
    )
    (
        total_a,
        total_b,
        total_c,
        total_d,
        total_e,
        total_f,
        total_g,
        total_h,
        total_i,
        total_j,
        total_k,
        total_l,
        total_m,
        total_n,
        total_o,
        total_p,
    ) = totals
    return (
        mixed,
        grad_frames,
        grad_text,
        total_a,
        total_b,
        total_c,
        total_d,
        total_e,
        total_f,
        total_g,
        total_h,
        total_i,
        total_j,
        total_k,
        total_l,
        total_m,
        total_n,
        total_o,
        total_p,
    )


def solution(mesh):
    in_specs = (
        P(("shard", "rep"), "ctx", None),
        P(("shard", "rep"), None, None),
        P("shard"),
        P("shard"),
        P("shard", None),
        P("shard", None),
        P("shard", None),
        P("shard", None),
        P("shard"),
        P("shard"),
        P("shard", None),
        P("shard", None),
        P("shard", None),
        P("shard", None),
        P("shard"),
        P("shard"),
        P("shard", None),
        P("shard", None),
        P(("shard", "rep"), "ctx", None),
    )
    out_specs = (
        P(("shard", "rep"), "ctx", None),
        P(("shard", "rep"), "ctx", None),
        P(("shard", "rep"), None, None),
        P("shard"),
        P("shard"),
        P("shard", None),
        P("shard", None),
        P("shard", None),
        P("shard", None),
        P("shard"),
        P("shard"),
        P("shard", None),
        P("shard", None),
        P("shard", None),
        P("shard", None),
        P("shard"),
        P("shard"),
        P("shard", None),
        P("shard", None),
    )
    return jax.shard_map(local, mesh=mesh, in_specs=in_specs, out_specs=out_specs, check_vma=False)
```

profile of v0, /device:TPU:0, one launch (start us, length us, event | category | flops | bytes accessed | tf_op | source)
XLA Modules:
  0.0 3124.1 jit_solution(14684579758798926931)
XLA Ops:
  16.3 14.2 all-gather
  30.5 12.1 all-gather.1
  42.8 12.1 all-gather.2
  55.6 12.1 all-gather.3
  68.3 12.1 all-gather.4
  81.0 12.1 all-gather.5
  93.7 8.6 all-gather.21.cloned.1.call-done
  102.4 6.2 convolution_convert_fusion.13
  112.1 79.7 %all-gather.17.cloned.1.call-done = bf16[1536,1536]{1,0:T(8,128)(2,1)} async-done(((bf16[384,1536]{1,0:T(8,128)(2,1)}), bf16[1536,1536]{1,0:T(8,128)(2,1)}) %all-gather.17.cloned.1.call-update) | async-done | bytes 4718608 | tf_op jit(solution)/shard_map/all_gather | solution.py:136
  191.8 6.2 convolution_convert_fusion.15
  207.9 73.3 %all-gather.19.cloned.1.call-done = bf16[1536,1536]{1,0:T(8,128)(2,1)} async-done(((bf16[384,1536]{1,0:T(8,128)(2,1)}), bf16[1536,1536]{1,0:T(8,128)(2,1)}) %all-gather.19.cloned.1.call-update) | async-done | bytes 4718608 | tf_op jit(solution)/shard_map/all_gather | solution.py:134
  281.3 6.2 convolution_convert_fusion.14
  290.2 80.5 %all-gather.29.cloned.1.call-done = bf16[1536,1536]{1,0:T(8,128)(2,1)} async-done(((bf16[384,1536]{1,0:T(8,128)(2,1)}), bf16[1536,1536]{1,0:T(8,128)(2,1)}) %all-gather.29.cloned.1.call-update) | async-done | bytes 4718608 | tf_op jit(solution)/shard_map/all_gather | solution.py:156
  374.9 85.1 %all-gather.25.cloned.1.call-done = bf16[1536,1536]{1,0:T(8,128)(2,1)} async-done(((bf16[384,1536]{1,0:T(8,128)(2,1)}), bf16[1536,1536]{1,0:T(8,128)(2,1)}) %all-gather.25.cloned.1.call-update) | async-done | bytes 4718608 | tf_op jit(solution)/shard_map/all_gather | solution.py:157
  474.7 55.2 %while.28 = (s32[]{:T(128)}, bf16[4,1,512,6,64]{2,4,3,1,0:T(8,128)(2,1)}, f32[4,1,6,512]{3,2,1,0:T(8,128)}, bf16[4,1,1024,6,64]{2,4,3,1,0:T(8,128)(2,1)}, bf16[4...) while((s32[]{:T(128)}, ...), condition=%wide.region_5.6_spmd.clone, body=%wide.region_2.5_spmd.clone.sunk | while | flops 844297216 | bytes 42317412 | solution.py:149
  482.7 5.7 fusion.209
  496.5 5.7 fusion.209
  510.2 5.7 fusion.209
  524.0 5.7 fusion.209
  529.9 19.4 all-gather.23.cloned.1.call-done
  549.3 6.2 fusion.139
  557.7 81.1 %all-gather.27.cloned.1.call-done = bf16[1536,1536]{1,0:T(8,128)(2,1)} async-done(((bf16[384,1536]{1,0:T(8,128)(2,1)}), bf16[1536,1536]{1,0:T(8,128)(2,1)}) %all-gather.27.cloned.1.call-update) | async-done | bytes 4718608 | tf_op jit(solution)/shard_map/all_gather | solution.py:155
  638.8 7.1 convolution_convert_fusion.12
  654.6 73.6 %all-gather.31.cloned.1.call-done = bf16[1536,1536]{1,0:T(8,128)(2,1)} async-done(((bf16[384,1536]{1,0:T(8,128)(2,1)}), bf16[1536,1536]{1,0:T(8,128)(2,1)}) %all-gather.31.cloned.1.call-update) | async-done | bytes 4718608 | tf_op jit(solution)/shard_map/all_gather | solution.py:158
  728.3 5.2 fusion.141
  736.3 314.7 %all-gather.33.cloned.1.call-done = bf16[1536,6144]{1,0:T(8,128)(2,1)} async-done(((bf16[384,6144]{1,0:T(8,128)(2,1)}), bf16[1536,6144]{1,0:T(8,128)(2,1)}) %all-gather.33.cloned.1.call-update) | async-done | bytes 18874384 | tf_op jit(solution)/shard_map/all_gather | solution.py:182
  1050.9 42.6 %multiply_convert_fusion.1 = (bf16[512,6144]{1,0:T(8,128)(2,1)}, f32[512,6144]{1,0:T(8,128)}, f32[512,6144]{1,0:T(8,128)}) fusion(bf16[1536,6144]{1,0:T(8,128)(2,1)} %all-gather.33.cloned.1.call-done, f32[512,1536]{1,0:T(8,128)} %copy-done.8, f32[1536]{0:T(1024)S(1)} %copy-done.77, f32[1536]{0:T(1024)S(1)} %copy-done.53, f32[512]{0:T(512)S(1)} %fusion.119, ...), kind=kOutput, calls=%fused_computation.67 | convolution fusion | flops 9872080896 | bytes 53493760 | tf_op jit(solution)/shard_map/dot_general | solution.py:30
  1093.5 280.3 %all-gather.35.cloned.1.call-done = bf16[6144,1536]{1,0:T(8,128)(2,1)} async-done(((bf16[1536,1536]{1,0:T(8,128)(2,1)}), bf16[6144,1536]{1,0:T(8,128)(2,1)}) %all-gather.35.cloned.1.call-update) | async-done | bytes 18874384 | tf_op jit(solution)/shard_map/all_gather | solution.py:183
  1373.8 23.8 add_convert_fusion
  1397.6 18.1 multiply_reduce_fusion.1
  1437.4 6.9 multiply_reduce_fusion.2
  1455.5 6.3 convolution_convert_fusion.3
  1464.3 119.8 %while.29 = (s32[]{:T(128)}, bf16[4,1,512,6,64]{2,4,3,1,0:T(8,128)(2,1)}, f32[4,1,1024,6,64]{2,4,3,1,0:T(8,128)}, f32[4,1,1024,6,64]{2,4,3,1,0:T(8,128)}, bf16[4...) while((s32[]{:T(128)}, ...), condition=%wide.region_19.20_spmd.clone, body=%wide.region_17.19_spmd.clone.sunk | while | flops 2062283776 | bytes 110338208 | solution.py:278
  1468.4 8.3 multiply_reduce_fusion.10
  1476.7 7.1 multiply_convert_fusion.5
  1498.4 8.3 multiply_reduce_fusion.10
  1506.7 6.9 multiply_convert_fusion.5
  1528.3 8.3 multiply_reduce_fusion.10
  1536.5 6.9 multiply_convert_fusion.5
  1558.0 8.3 multiply_reduce_fusion.10
  1566.3 6.9 multiply_convert_fusion.5
  1584.1 7.0 convolution_convert_fusion.7
  1592.9 5.6 convolution_convert_fusion.4
  1617.6 36.7 %collective-permute-done.3 = bf16[1,512,1536]{1,2,0:T(8,128)(2,1)S(1)} collective-permute-done((bf16[1,512,1536]{1,2,0:T(8,128)(2,1)S(1)}, bf16[1,512,1536]{1,2,0:T(8,128)(2,1)S(1)}, u32[]{:S(2)}, u32[]{:S(2)}) %collective-permute-start.3) | collective-permute-done | bytes 1572896 | tf_op jit(solution)/shard_map/ppermute | solution.py:19
  1654.3 7.5 convolution_convert_fusion.5
  1665.6 35.9 %collective-permute-done.2 = bf16[1,512,1536]{1,2,0:T(8,128)(2,1)S(1)} collective-permute-done((bf16[1,512,1536]{1,2,0:T(8,128)(2,1)S(1)}, bf16[1,512,1536]{1,2,0:T(8,128)(2,1)S(1)}, u32[]{:S(2)}, u32[]{:S(2)}) %collective-permute-start.2) | collective-permute-done | bytes 1572896 | tf_op jit(solution)/shard_map/ppermute | solution.py:19
  1702.7 7.0 convolution_convert_fusion.6
  1710.3 17.1 convolution_convert_fusion
  1728.8 16.0 convolution_convert_fusion.1
  1745.4 18.3 reduce-scatter.17.cloned.1.call-done
  1763.7 88.1 %reduce-scatter.25.cloned.1.call-done = bf16[384,1536]{1,0:T(8,128)(2,1)} async-done(((bf16[1536,1536]{1,0:T(8,128)(2,1)}), bf16[384,1536]{1,0:T(8,128)(2,1)}) %reduce-scatter.25.cloned.1.call-update) | async-done | bytes 1179664 | tf_op jit(solution)/shard_map/reduce_scatter | solution.py:337
  1851.8 88.1 %reduce-scatter.21.cloned.1.call-done = bf16[384,1536]{1,0:T(8,128)(2,1)} async-done(((bf16[1536,1536]{1,0:T(8,128)(2,1)}), bf16[384,1536]{1,0:T(8,128)(2,1)}) %reduce-scatter.21.cloned.1.call-update) | async-done | bytes 1179664 | tf_op jit(solution)/shard_map/reduce_scatter | solution.py:331
  1939.8 88.1 %reduce-scatter.23.cloned.1.call-done = bf16[384,1536]{1,0:T(8,128)(2,1)} async-done(((bf16[1536,1536]{1,0:T(8,128)(2,1)}), bf16[384,1536]{1,0:T(8,128)(2,1)}) %reduce-scatter.23.cloned.1.call-update) | async-done | bytes 1179664 | tf_op jit(solution)/shard_map/reduce_scatter | solution.py:334
  2027.9 88.1 %reduce-scatter.15.cloned.1.call-done = bf16[384,1536]{1,0:T(8,128)(2,1)} async-done(((bf16[1536,1536]{1,0:T(8,128)(2,1)}), bf16[384,1536]{1,0:T(8,128)(2,1)}) %reduce-scatter.15.cloned.1.call-update) | async-done | bytes 1179664 | tf_op jit(solution)/shard_map/reduce_scatter | solution.py:316
  2116.0 88.2 %reduce-scatter.13.cloned.1.call-done = bf16[384,1536]{1,0:T(8,128)(2,1)} async-done(((bf16[1536,1536]{1,0:T(8,128)(2,1)}), bf16[384,1536]{1,0:T(8,128)(2,1)}) %reduce-scatter.13.cloned.1.call-update) | async-done | bytes 1179664 | tf_op jit(solution)/shard_map/reduce_scatter | solution.py:313
  2204.2 316.7 %reduce-scatter.27.cloned.1.call-done = bf16[384,6144]{1,0:T(8,128)(2,1)} async-done(((bf16[1536,6144]{1,0:T(8,128)(2,1)}), bf16[384,6144]{1,0:T(8,128)(2,1)}) %reduce-scatter.27.cloned.1.call-update) | async-done | bytes 4718608 | tf_op jit(solution)/shard_map/reduce_scatter | solution.py:346
  2520.8 317.3 %reduce-scatter.29.cloned.1.call-done = bf16[1536,1536]{1,0:T(8,128)(2,1)} async-done(((bf16[6144,1536]{1,0:T(8,128)(2,1)}), bf16[1536,1536]{1,0:T(8,128)(2,1)}) %reduce-scatter.29.cloned.1.call-update) | async-done | bytes 4718608 | tf_op jit(solution)/shard_map/reduce_scatter | solution.py:349
  2844.8 16.5 fusion.81
  2865.3 7.0 convolution_add_fusion.2
  2878.6 18.7 all-reduce.8
  2897.8 13.0 all-reduce.6
  2914.3 5.7 add_bitcast_fusion
  2920.0 171.0 %all-reduce.13.cloned.1.call-done = (bf16[384,1536]{1,0:T(8,128)(2,1)}, bf16[384,1536]{1,0:T(8,128)(2,1)}, bf16[384,1536]{1,0:T(8,128)(2,1)}, bf16[384,1536]{1,0...) async-done(((bf16[384,1536]{1,0:T(8,128)(2,1)}, ...) | async-done | bytes 18874384 | tf_op jit(solution)/shard_map/psum | solution.py:374
  3091.0 7.4 convert_element_type.383
  (416 shorter events, 252.6 us)
Async XLA Ops:
  7.2 363.5 %copy-start = (bf16[1,64,1536]{2,1,0:T(8,128)(2,1)S(1)}, bf16[1,64,1536]{2,1,0:T(8,128)(2,1)}, u32[]{:S(2)}) copy-start(bf16[1,64,1536]{2,1,0:T(8,128)(2,1)} %param.24) | copy-start | bytes 589828
  7.2 95.2 %all-gather.21.cloned.1.call-start = ((), (), s32[]{:S(2)}) async-start(), calls=%async_computation.12 | async-start | bytes 5898240 | tf_op jit(solution)/shard_map/all_gather | solution.py:135
  7.9 183.8 %all-gather.17.cloned.1.call-start = ((), (), s32[]{:S(2)}) async-start(), calls=%async_computation.10 | async-start | bytes 5898240 | tf_op jit(solution)/shard_map/all_gather | solution.py:136
  8.7 272.6 %all-gather.19.cloned.1.call-start = ((), (), s32[]{:S(2)}) async-start(), calls=%async_computation.11 | async-start | bytes 5898240 | tf_op jit(solution)/shard_map/all_gather | solution.py:134
  9.4 361.3 %all-gather.29.cloned.1.call-start = ((), (), s32[]{:S(2)}) async-start(), calls=%async_computation.16 | async-start | bytes 5898240 | tf_op jit(solution)/shard_map/all_gather | solution.py:156
  10.0 450.0 %all-gather.25.cloned.1.call-start = ((), (), s32[]{:S(2)}) async-start(), calls=%async_computation.14 | async-start | bytes 5898240 | tf_op jit(solution)/shard_map/all_gather | solution.py:157
  10.6 538.7 %all-gather.23.cloned.1.call-start = ((), (), s32[]{:S(2)}) async-start(), calls=%async_computation.13 | async-start | bytes 5898240 | tf_op jit(solution)/shard_map/all_gather | solution.py:137
  11.2 627.6 %all-gather.27.cloned.1.call-start = ((), (), s32[]{:S(2)}) async-start(), calls=%async_computation.15 | async-start | bytes 5898240 | tf_op jit(solution)/shard_map/all_gather | solution.py:155
  11.9 716.3 %all-gather.31.cloned.1.call-start = ((), (), s32[]{:S(2)}) async-start(), calls=%async_computation.17 | async-start | bytes 5898240 | tf_op jit(solution)/shard_map/all_gather | solution.py:158
  12.7 1038.3 %all-gather.33.cloned.1.call-start = ((), (), s32[]{:S(2)}) async-start(), calls=%async_computation.18 | async-start | bytes 23592960 | tf_op jit(solution)/shard_map/all_gather | solution.py:182
  13.4 17.1 copy-start.86
  13.4 29.3 copy-start.87
  13.4 42.1 %copy-start.88 = (bf16[384]{0:T(512)(128)(2,1)S(1)}, bf16[384]{0:T(512)(128)(2,1)}, u32[]{:S(2)}) copy-start(bf16[384]{0:T(512)(128)(2,1)} %param.32) | copy-start | bytes 2308
  13.5 54.8 %copy-start.89 = (bf16[384]{0:T(512)(128)(2,1)S(1)}, bf16[384]{0:T(512)(128)(2,1)}, u32[]{:S(2)}) copy-start(bf16[384]{0:T(512)(128)(2,1)} %param.37) | copy-start | bytes 2308
  13.5 67.6 %copy-start.90 = (bf16[384]{0:T(512)(128)(2,1)S(1)}, bf16[384]{0:T(512)(128)(2,1)}, u32[]{:S(2)}) copy-start(bf16[384]{0:T(512)(128)(2,1)} %param.38) | copy-start | bytes 2308
  13.5 1360.4 %all-gather.35.cloned.1.call-start = ((), (), s32[]{:S(2)}) async-start(), calls=%async_computation.19 | async-start | bytes 23592960 | tf_op jit(solution)/shard_map/all_gather | solution.py:183
  14.1 1590.7 %all-reduce.15.cloned.1.call-start = ((), (), s32[]{:S(2)}) async-start(), calls=%async_computation.31 | async-start | bytes 1572864 | tf_op jit(solution)/shard_map/psum | solution.py:252
  15.1 266.2 %copy-start.57 = (f32[512]{0:T(512)}, f32[512]{0:T(512)S(1)}, u32[]{:S(2)}) copy-start(f32[512]{0:T(512)S(1)} %broadcast_multiply_fusion.2) | copy-start | bytes 6148
  15.7 265.6 %copy-start.69 = (f32[512]{0:T(512)}, f32[512]{0:T(512)S(1)}, u32[]{:S(2)}) copy-start(f32[512]{0:T(512)S(1)} %fusion.117) | copy-start | bytes 6148
  30.5 250.7 %copy-start.51 = (f32[1536]{0:T(1024)}, f32[1536]{0:T(1024)S(1)}, u32[]{:S(2)}) copy-start(f32[1536]{0:T(1024)S(1)} %reshape.507) | copy-start | bytes 18436
  42.7 238.5 %copy-start.75 = (f32[1536]{0:T(1024)}, f32[1536]{0:T(1024)S(1)}, u32[]{:S(2)}) copy-start(f32[1536]{0:T(1024)S(1)} %reshape.508) | copy-start | bytes 18436
  108.6 355.7 %collective-permute-start.1 = (bf16[1,512,1536]{2,1,0:T(8,128)(2,1)}, bf16[1,512,1536]{2,1,0:T(8,128)(2,1)S(1)}, u32[]{:S(2)}, u32[]{:S(2)}) collective-permute-start(bf16[1,512,1536]{2,1,0:T(8,128)(2,1)} %bitcast.9), channel_id=1, source_target_pairs={{0,16},{1,17},{2,18},{3,19},{4,20},{5,21},{6,22},{7,23},{8,24},{9,... | collective-permute-start | bytes 4718600 | tf_op jit(solution)/shard_map/ppermute | solution.py:19
  198.0 267.9 %collective-permute-start = (bf16[1,512,1536]{2,1,0:T(8,128)(2,1)}, bf16[1,512,1536]{2,1,0:T(8,128)(2,1)}, u32[]{:S(2)}, u32[]{:S(2)}) collective-permute-start(bf16[1,512,1536]{2,1,0:T(8,128)(2,1)} %bitcast.1), channel_id=1, source_target_pairs={{0,16},{1,17},{2,18},{3,19},{4,20},{5,21},{6,22},{7,23},{8,24},{9,... | collective-permute-start | bytes 4718600 | tf_op jit(solution)/shard_map/ppermute | solution.py:19
  529.9 25.7 copy-start.1
  529.9 25.7 copy-start.43
  529.9 25.7 copy-start.45
  529.9 25.7 copy-start.49
  555.6 83.2 %copy-start.55 = (f32[1536]{0:T(1024)S(1)}, f32[1536]{0:T(1024)}, u32[]{:S(2)}) copy-start(f32[1536]{0:T(1024)} %reshape.509) | copy-start | bytes 18436
  555.6 83.2 %copy-start.79 = (f32[1536]{0:T(1024)S(1)}, f32[1536]{0:T(1024)}, u32[]{:S(2)}) copy-start(f32[1536]{0:T(1024)} %reshape.510) | copy-start | bytes 18436
  555.6 83.2 %copy-start.61 = (f32[512]{0:T(512)}, f32[512]{0:T(512)S(1)}, u32[]{:S(2)}) copy-start(f32[512]{0:T(512)S(1)} %broadcast_multiply_fusion.1) | copy-start | bytes 6148
  557.7 81.1 %copy-start.65 = (f32[512]{0:T(512)}, f32[512]{0:T(512)S(1)}, u32[]{:S(2)}) copy-start(f32[512]{0:T(512)S(1)} %multiply_reduce_fusion.7) | copy-start | bytes 6148
  557.7 81.1 %copy-start.73 = (f32[512]{0:T(512)}, f32[512]{0:T(512)S(1)}, u32[]{:S(2)}) copy-start(f32[512]{0:T(512)S(1)} %fusion.118) | copy-start | bytes 6148
  650.7 77.6 %copy-start.4 = (f32[512,1536]{1,0:T(8,128)S(1)}, f32[512,1536]{1,0:T(8,128)}, u32[]{:S(2)}) copy-start(f32[512,1536]{1,0:T(8,128)} %copy-done.3) | copy-start | bytes 9437188
  733.5 317.4 %copy-start.53 = (f32[1536]{0:T(1024)S(1)}, f32[1536]{0:T(1024)}, u32[]{:S(2)}) copy-start(f32[1536]{0:T(1024)} %reshape.511) | copy-start | bytes 18436
  733.5 317.4 %copy-start.77 = (f32[1536]{0:T(1024)S(1)}, f32[1536]{0:T(1024)}, u32[]{:S(2)}) copy-start(f32[1536]{0:T(1024)} %reshape.512) | copy-start | bytes 18436
  733.5 682.2 %copy-start.59 = (f32[512]{0:T(512)}, f32[512]{0:T(512)S(1)}, u32[]{:S(2)}) copy-start(f32[512]{0:T(512)S(1)} %broadcast_multiply_fusion) | copy-start | bytes 6148
  736.3 679.5 %copy-start.71 = (f32[512]{0:T(512)}, f32[512]{0:T(512)S(1)}, u32[]{:S(2)}) copy-start(f32[512]{0:T(512)S(1)} %fusion.119) | copy-start | bytes 6148
  1373.8 23.8 copy-start.9
  1397.6 18.1 copy-start.68
  1455.4 289.9 %reduce-scatter.19.cloned.1.call-start = ((), (), s32[]{:S(2)}) async-start(), calls=%async_computation.24 | async-start | bytes 5898240 | tf_op jit(solution)/shard_map/reduce_scatter | solution.py:328
  1461.8 283.6 %reduce-scatter.11.cloned.1.call-start = ((), (), s32[]{:S(2)}) async-start(), calls=%async_computation.20 | async-start | bytes 5898240 | tf_op jit(solution)/shard_map/reduce_scatter | solution.py:310
  1464.2 119.8 %copy-start.52 = (f32[1536]{0:T(1024)S(1)}, f32[1536]{0:T(1024)}, u32[]{:S(2)}) copy-start(f32[1536]{0:T(1024)} %copy-done.51) | copy-start | bytes 18436
  1464.2 119.8 %copy-start.58 = (f32[512]{0:T(512)S(1)}, f32[512]{0:T(512)}, u32[]{:S(2)}) copy-start(f32[512]{0:T(512)} %copy-done.57) | copy-start | bytes 6148
  1464.2 119.8 %copy-start.70 = (f32[512]{0:T(512)S(1)}, f32[512]{0:T(512)}, u32[]{:S(2)}) copy-start(f32[512]{0:T(512)} %copy-done.69) | copy-start | bytes 6148
  1464.3 119.8 %copy-start.76 = (f32[1536]{0:T(1024)S(1)}, f32[1536]{0:T(1024)}, u32[]{:S(2)}) copy-start(f32[1536]{0:T(1024)} %copy-done.75) | copy-start | bytes 18436
  1591.1 172.7 %reduce-scatter.17.cloned.1.call-start = ((), (), s32[]{:S(2)}) async-start(), calls=%async_computation.23 | async-start | bytes 5898240 | tf_op jit(solution)/shard_map/reduce_scatter | solution.py:319
  1598.6 253.2 %reduce-scatter.25.cloned.1.call-start = ((), (), s32[]{:S(2)}) async-start(), calls=%async_computation.27 | async-start | bytes 5898240 | tf_op jit(solution)/shard_map/reduce_scatter | solution.py:337
  1604.7 335.2 %reduce-scatter.21.cloned.1.call-start = ((), (), s32[]{:S(2)}) async-start(), calls=%async_computation.25 | async-start | bytes 5898240 | tf_op jit(solution)/shard_map/reduce_scatter | solution.py:331
  1609.4 418.5 %reduce-scatter.23.cloned.1.call-start = ((), (), s32[]{:S(2)}) async-start(), calls=%async_computation.26 | async-start | bytes 5898240 | tf_op jit(solution)/shard_map/reduce_scatter | solution.py:334
  1614.0 40.3 %copy-start.7 = (bf16[1,512,1536]{2,1,0:T(8,128)(2,1)S(1)}, bf16[1,512,1536]{2,1,0:T(8,128)(2,1)}, u32[]{:S(2)}) copy-start(bf16[1,512,1536]{2,1,0:T(8,128)(2,1)} %param.23) | copy-start | bytes 4718596
  1614.1 501.9 %reduce-scatter.15.cloned.1.call-start = ((), (), s32[]{:S(2)}) async-start(), calls=%async_computation.22 | async-start | bytes 5898240 | tf_op jit(solution)/shard_map/reduce_scatter | solution.py:316
  1616.3 38.0 %collective-permute-start.3 = (bf16[1,512,1536]{1,2,0:T(8,128)(2,1)S(1)}, bf16[1,512,1536]{1,2,0:T(8,128)(2,1)S(1)}, u32[]{:S(2)}, u32[]{:S(2)}) collective-permute-start(bf16[1,512,1536]{1,2,0:T(8,128)(2,1)S(1)} %slice.38), channel_id=1, source_target_pairs={{16,0},{17,1},{18,2},{19,3},{20,4},{21,5},{22,6},{23,7},{24,8},{25... | collective-permute-start | bytes 4718600 | tf_op jit(solution)/shard_map/ppermute | solution.py:19
  1661.9 542.3 %reduce-scatter.13.cloned.1.call-start = ((), (), s32[]{:S(2)}) async-start(), calls=%async_computation.21 | async-start | bytes 5898240 | tf_op jit(solution)/shard_map/reduce_scatter | solution.py:313
  1664.3 37.2 %collective-permute-start.2 = (bf16[1,512,1536]{1,2,0:T(8,128)(2,1)S(1)}, bf16[1,512,1536]{1,2,0:T(8,128)(2,1)S(1)}, u32[]{:S(2)}, u32[]{:S(2)}) collective-permute-start(bf16[1,512,1536]{1,2,0:T(8,128)(2,1)S(1)} %slice.39), channel_id=1, source_target_pairs={{16,0},{17,1},{18,2},{19,3},{20,4},{21,5},{22,6},{23,7},{24,8},{25... | collective-permute-start | bytes 4718600 | tf_op jit(solution)/shard_map/ppermute | solution.py:19
  1709.7 811.2 %reduce-scatter.27.cloned.1.call-start = ((), (), s32[]{:S(2)}) async-start(), calls=%async_computation.28 | async-start | bytes 23592960 | tf_op jit(solution)/shard_map/reduce_scatter | solution.py:346
  1727.5 1110.6 %reduce-scatter.29.cloned.1.call-start = ((), (), s32[]{:S(2)}) async-start(), calls=%async_computation.29 | async-start | bytes 23592960 | tf_op jit(solution)/shard_map/reduce_scatter | solution.py:349
  1744.9 1346.1 %all-reduce.13.cloned.1.call-start = ((), (), s32[]{:S(2)}) async-start(), calls=%async_computation.30 | async-start | bytes 37748736 | tf_op jit(solution)/shard_map/psum | solution.py:374
  2840.0 21.3 slice-start
  2840.0 22.9 slice-start.2
  2844.8 16.6 slice-start.1
  2844.8 16.6 copy-start.30
  2844.8 18.1 slice-start.3
  2863.0 9.4 slice-start.6
  2863.0 9.4 slice-start.8
  (71 other events, 206.3 us)
Sparse Core Ops, SparseCore 0:
  9.6 92.7 all-gather.20
  103.9 87.7 all-gather.16
  193.4 87.8 all-gather.18
  282.7 87.9 all-gather.28
  372.1 87.8 all-gather.24
  461.4 87.8 all-gather.22
  550.9 87.8 all-gather.26
  640.4 87.8 all-gather.30
  729.9 321.0 all-gather.32
  1052.4 321.4 all-gather.34
  1455.6 33.3 all-reduce.14
  1491.2 85.2 reduce-scatter.18
  1591.2 84.4 reduce-scatter.10
  1677.9 85.7 reduce-scatter.16
  1766.0 85.7 reduce-scatter.24
  1854.0 85.7 reduce-scatter.20
  1942.1 85.7 reduce-scatter.22
  2030.2 85.7 reduce-scatter.14
  2118.4 85.7 reduce-scatter.12
  2206.5 314.2 reduce-scatter.26
  2523.2 314.8 reduce-scatter.28
  2844.8 246.1 all-reduce.12
where the time goes:
time: 3130 us; the launch traced here: 3120 us
  waiting for transfers between devices  2440 us (78%)
  matrix products  394 us (13%)
  blocking collectives  106 us (3%)
  other arithmetic  97 us (3%)
  local copies, waits for them, and re-layouts  58.4 us (2%)
    reduce_scatter x1, waiting for transfers between devices, local(): lax.psum_scatter(grad_down.astype(jnp.bfloat16), 'shard', scatter_dimensi...  317 us
    reduce_scatter x1, waiting for transfers between devices, local(): lax.psum_scatter(grad_up.astype(jnp.bfloat16), 'shard', scatter_dimension...  317 us
    all_gather x1, waiting for transfers between devices, local(): lax.all_gather(up_weight, 'shard', axis=0, tiled=True)  315 us
    all_gather x1, waiting for transfers between devices, local(): lax.all_gather(down_weight, 'shard', axis=0, tiled=True)  280 us
    psum x1, waiting for transfers between devices, local(): lax.psum(own_c.astype(jnp.bfloat16), ('ctx', 'rep')).astype(jnp.float32)  171 us
    dot_general x10, matrix products, product(): return jnp.dot(left, right, preferred_element_type=jnp.float32)  103 us
    reduce_scatter x1, waiting for transfers between devices, local(): lax.psum_scatter(grad_key.astype(jnp.bfloat16), 'shard', scatter_dimensio...  88.2 us
    reduce_scatter x1, waiting for transfers between devices, local(): lax.psum_scatter(grad_value.astype(jnp.bfloat16), 'shard', scatter_dimens...  88.1 us
  transfers between devices with their start and end apart: 26, of which 21 were waited for; matrix products, arithmetic and copies ran while one was open for 14% of the time, Pallas kernels for 0%

commit v1 on v0

v1 whole, which is shorter than its diff:
```python
import math

import jax
import jax.numpy as jnp
from jax import lax
from jax.experimental import pallas as pl
from jax.experimental.pallas import tpu as pltpu
from jax.sharding import PartitionSpec as P

HD = 64
EPS = 1e-05
NEG = -1e30
BF16 = jnp.bfloat16
F32 = jnp.float32
VMEM_LIMIT = 48 * 1024 * 1024
EVERY = ("shard", "ctx", "rep")


def product(left, right):
    return jnp.dot(left, right, preferred_element_type=F32)


def over_rows(left, right):
    return lax.dot_general(left, right, (((0,), (0,)), ((), ())), preferred_element_type=F32)


def against(left, right):
    return lax.dot_general(left, right, (((1,), (1,)), ((), ())), preferred_element_type=F32)


def xor_permute(array, axis, bit):
    return lax.ppermute(array, axis, [(i, i ^ bit) for i in range(lax.axis_size(axis))])


def swap_ctx(array):
    return xor_permute(array, "ctx", 1)


def swap_row(array):
    return xor_permute(array, "rep", 2)


def swap_core(array):
    return xor_permute(array, "rep", 1)


def shifted(block, axis, distance):
    devices = range(lax.axis_size(axis))
    route = [(i - distance, i) for i in devices if i - distance in devices]
    return lax.ppermute(block, axis, route)


def pick(array, index, axis):
    return lax.dynamic_index_in_dim(array, index, axis, keepdims=False)


def both(own):
    return jnp.concatenate([own, swap_core(own)], axis=0)


def pair_sum(left, right, multiply):
    half = left.shape[0] // 2
    other = swap_core(multiply(left[half:], right).astype(BF16))
    return multiply(left[:half], right) + other.astype(F32)


def nt(left, right):
    return lax.dot_general(left, right, (((1,), (1,)), ((), ())), preferred_element_type=F32)


def tn(left, right):
    return lax.dot_general(left, right, (((0,), (0,)), ((), ())), preferred_element_type=F32)


def nn(left, right):
    return lax.dot_general(left, right, (((1,), (0,)), ((), ())), preferred_element_type=F32)


def query_block(span):
    return math.gcd(span, 256)


def key_chunks(causal, block, index):
    if not causal:
        return [(0, None, "none")]
    return [(0, None, "earlier"), (1, (index + 1) * block, "own")]


def masked(scores, mode, position, block, index):
    if mode == "earlier":
        return jnp.where(position > 0, scores, NEG)
    if mode == "own":
        row = lax.broadcasted_iota(jnp.int32, scores.shape, 0)
        column = lax.broadcasted_iota(jnp.int32, scores.shape, 1) + index * block
        return jnp.where(row <= column, scores, NEG)
    return scores


def attend_kernel(causal, position_ref, q_ref, k_ref, v_ref, o_ref, log_ref):
    position = position_ref[0]
    span = q_ref.shape[1]
    block = query_block(span)
    low = lax.broadcasted_iota(jnp.int32, (block, 2 * HD), 1) < HD
    for index in range(span // block):
        rows = pl.ds(index * block, block)
        queries = q_ref[0, rows, :] * BF16(HD ** -0.5)
        parts = []
        for head in range(2):
            side = jnp.where(low == (head == 0), queries, jnp.zeros_like(queries))
            scores = []
            for part, extent, mode in key_chunks(causal, block, index):
                keys = k_ref[part, 0, :extent, :]
                scores.append(masked(nt(keys, side), mode, position, block, index))
            top = scores[0].max(axis=0, keepdims=True)
            for other in scores[1:]:
                top = jnp.maximum(top, other.max(axis=0, keepdims=True))
            weights = [jnp.exp(each - top) for each in scores]
            total = sum(each.sum(axis=0, keepdims=True) for each in weights)
            inverse = 1.0 / total
            out = None
            for weight, (part, extent, mode) in zip(weights, key_chunks(causal, block, index)):
                term = tn(v_ref[part, 0, :extent, :], (weight * inverse).astype(BF16))
                out = term if out is None else out + term
            parts.append(out)
            log_ref[0, 0, head : head + 1, rows] = top + jnp.log(total)
        upper = lax.broadcasted_iota(jnp.int32, parts[0].shape, 0) < HD
        o_ref[0, rows, :] = jnp.where(upper, parts[0], parts[1]).T.astype(BF16)


def attend_back_kernel(
    causal, position_ref, q_ref, k_ref, v_ref, o_ref, g_ref, log_ref, dq_ref, dk_ref, dv_ref, dk_acc, dv_acc
):
    position = position_ref[0]
    span = q_ref.shape[1]
    block = query_block(span)
    low = lax.broadcasted_iota(jnp.int32, (block, 2 * HD), 1) < HD
    dk_acc[...] = jnp.zeros_like(dk_acc)
    dv_acc[...] = jnp.zeros_like(dv_acc)
    for index in range(span // block):
        rows = pl.ds(index * block, block)
        queries = q_ref[0, rows, :] * BF16(HD ** -0.5)
        grads = g_ref[0, rows, :]
        flat = (grads.astype(F32) * o_ref[0, rows, :].astype(F32)).T
        parts = []
        for head in range(2):
            mine = low == (head == 0)
            side = jnp.where(mine, queries, jnp.zeros_like(queries))
            grad = jnp.where(mine, grads, jnp.zeros_like(grads))
            delta = flat[head * HD : (head + 1) * HD].sum(axis=0, keepdims=True)
            log_total = log_ref[0, 0, head : head + 1, rows]
            dq = None
            for part, extent, mode in key_chunks(causal, block, index):
                keys = k_ref[part, 0, :extent, :]
                scores = masked(nt(keys, side), mode, position, block, index)
                probs = jnp.exp(scores - log_total)
                grad_probs = nt(v_ref[part, 0, :extent, :], grad)
                grad_scores = (probs * (grad_probs - delta)).astype(BF16)
                dk_acc[part, :extent, :] += nn(grad_scores, side)
                dv_acc[part, :extent, :] += nn(probs.astype(BF16), grad)
                term = tn(keys, grad_scores)
                dq = term if dq is None else dq + term
            parts.append(dq)
        upper = lax.broadcasted_iota(jnp.int32, parts[0].shape, 0) < HD
        dq_ref[0, rows, :] = (jnp.where(upper, parts[0], parts[1]).T * HD ** -0.5).astype(BF16)
    dk_ref[:, 0] = dk_acc[...].astype(BF16)
    dv_ref[:, 0] = dv_acc[...].astype(BF16)


def attend(position, queries, keys, values, key_base, value_base, causal):
    clips, span, width = queries.shape
    parts, unused, length, unused = keys.shape
    pair = 2 * HD
    pairs = width // pair
    work = 2 * clips * span * length * parts * width
    return pl.pallas_call(
        lambda *refs: attend_kernel(causal, *refs),
        grid=(clips, pairs),
        in_specs=[
            pl.BlockSpec(memory_space=pltpu.SMEM),
            pl.BlockSpec((1, span, pair), lambda b, j: (b, 0, j)),
            pl.BlockSpec((parts, 1, length, pair), lambda b, j: (0, b, 0, key_base + j)),
            pl.BlockSpec((parts, 1, length, pair), lambda b, j: (0, b, 0, value_base + j)),
        ],
        out_specs=[
            pl.BlockSpec((1, span, pair), lambda b, j: (b, 0, j)),
            pl.BlockSpec((1, 1, 2, span), lambda b, j: (b, j, 0, 0)),
        ],
        out_shape=[
            jax.ShapeDtypeStruct((clips, span, width), BF16),
            jax.ShapeDtypeStruct((clips, pairs, 2, span), F32),
        ],
        compiler_params=pltpu.CompilerParams(vmem_limit_bytes=VMEM_LIMIT),
        cost_estimate=pl.CostEstimate(flops=2 * 2 * work, bytes_accessed=8 * clips * span * width, transcendentals=work // (2 * HD)),
    )(position, queries, keys, values)


def attend_back(position, queries, keys, values, out, grad, logs, key_base, value_base, causal):
    clips, span, width = queries.shape
    parts, unused, length, unused = keys.shape
    pair = 2 * HD
    pairs = width // pair
    work = 2 * clips * span * length * parts * width
    row_spec = pl.BlockSpec((1, span, pair), lambda b, j: (b, 0, j))
    return pl.pallas_call(
        lambda *refs: attend_back_kernel(causal, *refs),
        grid=(clips, pairs),
        in_specs=[
            pl.BlockSpec(memory_space=pltpu.SMEM),
            row_spec,
            pl.BlockSpec((parts, 1, length, pair), lambda b, j: (0, b, 0, key_base + j)),
            pl.BlockSpec((parts, 1, length, pair), lambda b, j: (0, b, 0, value_base + j)),
            row_spec,
            row_spec,
            pl.BlockSpec((1, 1, 2, span), lambda b, j: (b, j, 0, 0)),
        ],
        out_specs=[
            row_spec,
            pl.BlockSpec((parts, 1, length, pair), lambda b, j: (0, b, 0, j)),
            pl.BlockSpec((parts, 1, length, pair), lambda b, j: (0, b, 0, j)),
        ],
        out_shape=[
            jax.ShapeDtypeStruct((clips, span, width), BF16),
            jax.ShapeDtypeStruct((parts, clips, length, width), BF16),
            jax.ShapeDtypeStruct((parts, clips, length, width), BF16),
        ],
        scratch_shapes=[
            pltpu.VMEM((parts, length, pair), F32),
            pltpu.VMEM((parts, length, pair), F32),
        ],
        compiler_params=pltpu.CompilerParams(vmem_limit_bytes=VMEM_LIMIT),
        cost_estimate=pl.CostEstimate(flops=2 * 5 * work, bytes_accessed=20 * clips * span * width, transcendentals=work // (2 * HD)),
    )(position, queries, keys, values, out, grad, logs)


def strip_halves(block, strips, core):
    size = block.shape[-1] // (2 * strips)
    return [block[..., (2 * j + core) * size : (2 * j + core + 1) * size] for j in range(strips)]


class Place:
    def __init__(self, width):
        self.shards = lax.axis_size("shard")
        self.ctx = lax.axis_index("ctx")
        self.z = lax.axis_index("shard")
        rep = lax.axis_index("rep")
        self.core = rep % 2
        self.y = rep // 2
        self.staged = (
            self.shards == 4
            and lax.axis_size("ctx") == 2
            and lax.axis_size("rep") == 4
            and (width // self.shards) % (2 * HD) == 0
            and (width // self.shards) % 128 == 0
        )
        self.strips = self.shards if self.staged else 1
        self.spot = jnp.stack([self.z, self.ctx * 2 + self.y, self.core]).astype(jnp.int32)

    def own_columns(self, array):
        rows, width = array.shape
        return lax.dynamic_slice_in_dim(array, self.core * (width // 2), width // 2, 1)

    def own_rows(self, array):
        rows, width = array.shape
        return lax.dynamic_slice_in_dim(array, self.core * (rows // 2), rows // 2, 0)


    def unit_shape(self, batch):
        kind, shards = batch
        if kind == "columns":
            return shards[0].shape[0], sum(s.shape[1] // 2 for s in shards)
        return shards[0].shape[0] // 2, sum(s.shape[1] for s in shards)

    def first_pieces(self, batches):
        shards = [s for kind, each in batches for s in each]
        shapes = [(rows // 4, width) for rows, width in map(self.unit_shape, batches)]

        def spec(kind, quarter, width):
            if kind == "columns":
                return pl.BlockSpec((quarter, width), lambda i, at: (at[1], 0))
            return pl.BlockSpec((quarter, width), lambda i, at: (at[2] * 4 + at[1], 0))

        def kernel(at, *refs):
            ins, outs = list(refs[: len(shards)]), refs[len(shards) :]
            for core in range(2):

                @pl.when(at[2] == core)
                def unused():
                    rest = list(ins)
                    for (kind, each), out in zip(batches, outs):
                        edge = 0
                        for shard in each:
                            block = rest.pop(0)
                            parts = strip_halves(block, self.strips, core) if kind == "columns" else [block[...]]
                            for part in parts:
                                out[:, edge : edge + part.shape[-1]] = part
                                edge += part.shape[-1]

        return pl.pallas_call(
            kernel,
            grid_spec=pltpu.PrefetchScalarGridSpec(
                num_scalar_prefetch=1,
                grid=(1,),
                in_specs=[
                    spec(kind, self.unit_shape((kind, each))[0] // 4, s.shape[1]) for kind, each in batches for s in each
                ],
                out_specs=[pl.BlockSpec(shape, lambda i, at: (0, 0)) for shape in shapes],
            ),
            out_shape=[jax.ShapeDtypeStruct(shape, BF16) for shape in shapes],
            compiler_params=pltpu.CompilerParams(vmem_limit_bytes=VMEM_LIMIT),
        )(self.spot, *shards)

    def exchange_z(self, mine):
        return jnp.stack([xor_permute(mine, "shard", k) for k in range(1, 4)])

    def exchange_plane(self, from_z):
        half = from_z.shape[-1] // 2
        from_x = swap_ctx(from_z)
        from_y = swap_row(from_z)
        return from_z, from_y, from_x, swap_row(from_x[..., :half]), swap_ctx(from_y[..., half:])

    def assemble(self, batch, received, splits=()):
        kind, shards = batch
        rows, width = self.unit_shape(batch)
        quarter, half = rows // 4, width // 2
        edges = [0, *splits, width]
        spans = list(zip(edges[:-1], edges[1:]))
        count = len(shards)

        def step(turn):
            def index(s, k, at):
                now = jnp.maximum(k, 1) - 1
                return (jnp.where(s == turn, now, jnp.where(s < turn, 0, 2)), 0, 0)

            return index

        def own(s, k, at):
            spot = lax.bitwise_xor(at[1], s)
            return (spot, 0) if kind == "columns" else (at[2] * 4 + spot, 0)

        def target(s, k, at):
            return (lax.bitwise_xor(at[0], k) * 4 + lax.bitwise_xor(at[1], s), 0)

        def kernel(at, *refs):
            ins, (z_ref, y_ref, x_ref, xy_ref, yx_ref), outs = refs[:count], refs[count : count + 5], refs[count + 5 :]
            s, k = pl.program_id(0), pl.program_id(1)

            def put(parts):
                edge = 0
                for part in parts:
                    end = edge + part.shape[-1]
                    for (a, b), out in zip(spans, outs):
                        low, high = max(a, edge), min(b, end)
                        if low < high:
                            out[:, low - a : high - a] = part[:, low - edge : high - edge]
                    edge = end

            for core in range(2):

                @pl.when((k == 0) & (at[2] == core))
                def unused():
                    parts = []
                    for block in ins:
                        parts += strip_halves(block, self.strips, core) if kind == "columns" else [block[...]]
                    put(parts)

            for turn, ref in ((0, z_ref), (1, y_ref), (2, x_ref)):

                @pl.when((k > 0) & (s == turn))
                def unused(ref=ref):
                    put([ref[0]])

            @pl.when((k > 0) & (s == 3))
            def unused():
                put([xy_ref[0], yx_ref[0]])

        return pl.pallas_call(
            kernel,
            grid_spec=pltpu.PrefetchScalarGridSpec(
                num_scalar_prefetch=1,
                grid=(4, 4),
                in_specs=[pl.BlockSpec((quarter, s.shape[1]), own) for s in shards]
                + [pl.BlockSpec((1, quarter, width), step(turn)) for turn in range(3)]
                + [pl.BlockSpec((1, quarter, half), step(3))] * 2,
                out_specs=[pl.BlockSpec((quarter, b - a), target) for a, b in spans],
            ),
            out_shape=[jax.ShapeDtypeStruct((4 * rows, b - a), BF16) for a, b in spans],
            compiler_params=pltpu.CompilerParams(vmem_limit_bytes=VMEM_LIMIT),
            cost_estimate=pl.CostEstimate(flops=0, bytes_accessed=16 * rows * width, transcendentals=0),
        )(self.spot, *shards, *received)

    def gather_plain(self, batch, splits=()):
        kind, shards = batch
        whole = [lax.all_gather(s, "shard", axis=0, tiled=True) for s in shards]
        parts = [self.own_columns(w) if kind == "columns" else self.own_rows(w) for w in whole]
        joined = jnp.concatenate(parts, axis=1)
        edges = [0, *splits, joined.shape[1]]
        return [joined[:, a:b] for a, b in zip(edges[:-1], edges[1:])]


    def total(self, grad):
        rows, width = grad.shape[0] // 4, grad.shape[1]
        quarter, half = rows // 4, width // 2
        x, y = self.ctx, self.y
        pieces = grad.reshape(4, 2, 2, quarter, width)
        first, second = pieces[..., :half], pieces[..., half:]

        def plus(left, right):
            return (left.astype(F32) + right.astype(F32)).astype(BF16)

        kept_a = plus(pick(first, x, 1), swap_ctx(pick(first, 1 - x, 1)))
        kept_b = plus(pick(second, y, 2), swap_row(pick(second, 1 - y, 2)))
        kept_a = plus(pick(kept_a, y, 1), swap_row(pick(kept_a, 1 - y, 1)))
        kept_b = plus(pick(kept_b, x, 1), swap_ctx(pick(kept_b, 1 - x, 1)))
        kept = jnp.concatenate([kept_a, kept_b], axis=-1)
        summed = pick(kept, self.z, 0).astype(F32)
        for k in range(1, 4):
            summed = summed + xor_permute(pick(kept, self.z ^ k, 0), "shard", k).astype(F32)
        return lax.all_gather(summed.astype(BF16), ("ctx", "rep"), axis=0, tiled=False)

    def all_sum(self, array):
        array = lax.psum_scatter(array, "shard", scatter_dimension=0, tiled=True)
        return lax.psum(array, ("ctx", "rep"))

    def scatter_columns(self, grad, count):
        rows, width = grad.shape
        each = width // count
        if not self.staged:
            outs = []
            for i in range(count):
                whole = jnp.zeros((rows, 2 * each), BF16)
                part = grad[:, i * each : (i + 1) * each]
                whole = lax.dynamic_update_slice_in_dim(whole, part, self.core * each, 1)
                outs.append(self.all_sum(whole).astype(F32))
            return outs
        total = self.total(grad)
        quarter = total.shape[1]
        total = total.reshape(4, 2, quarter, width)
        strips = self.strips
        size = each // strips

        def kernel(in_ref, *outs):
            for i, out in enumerate(outs):
                for j in range(strips):
                    for core in range(2):
                        edge = i * each + j * size
                        out[:, (2 * j + core) * size : (2 * j + core + 1) * size] = in_ref[
                            0, core, :, edge : edge + size
                        ].astype(F32)

        return pl.pallas_call(
            kernel,
            grid=(4,),
            in_specs=[pl.BlockSpec((1, 2, quarter, width), lambda p: (p, 0, 0, 0))],
            out_specs=[pl.BlockSpec((quarter, 2 * each), lambda p: (p, 0))] * count,
            out_shape=[jax.ShapeDtypeStruct((4 * quarter, 2 * each), F32)] * count,
            compiler_params=pltpu.CompilerParams(vmem_limit_bytes=VMEM_LIMIT),
        )(total)

    def scatter_rows(self, grad):
        if not self.staged:
            rows, width = grad.shape
            whole = jnp.zeros((2 * rows, width), BF16)
            whole = lax.dynamic_update_slice_in_dim(whole, grad, self.core * rows, 0)
            return self.all_sum(whole).astype(F32)
        total = self.total(grad)
        unused, quarter, width = total.shape

        def kernel(in_ref, out_ref):
            out_ref[...] = in_ref[0].astype(F32)

        return pl.pallas_call(
            kernel,
            grid=(2, 4),
            in_specs=[pl.BlockSpec((1, quarter, width), lambda c, p: (p * 2 + c, 0, 0))],
            out_specs=pl.BlockSpec((quarter, width), lambda c, p: (c * 4 + p, 0)),
            out_shape=jax.ShapeDtypeStruct((8 * quarter, width), F32),
            compiler_params=pltpu.CompilerParams(vmem_limit_bytes=VMEM_LIMIT),
        )(total)


def layer_norm(hidden, gain, shift):
    mean = jnp.mean(hidden, axis=-1, keepdims=True)
    centred = hidden - mean
    spread = jnp.mean(centred * centred, axis=-1, keepdims=True)
    return centred * lax.rsqrt(spread + EPS) * gain + shift


def norm_backward(hidden, gain, grad):
    mean = jnp.mean(hidden, axis=-1, keepdims=True)
    centred = hidden - mean
    inverse = lax.rsqrt(jnp.mean(centred * centred, axis=-1, keepdims=True) + EPS)
    unit = centred * inverse
    scaled = grad * gain
    grad_hidden = inverse * (
        scaled - jnp.mean(scaled, axis=-1, keepdims=True) - unit * jnp.mean(scaled * unit, axis=-1, keepdims=True)
    )
    return grad_hidden, jnp.sum(grad * unit, axis=0), jnp.sum(grad, axis=0)


def gelu_parts(pre):
    phi = 0.5 * lax.erfc(-pre * (0.5 ** 0.5))
    slope = phi + pre * jnp.exp(-0.5 * pre * pre) * ((2.0 * math.pi) ** -0.5)
    return pre * phi, slope


def local(
    frames,
    text_states,
    first_gain,
    first_shift,
    self_query,
    self_key,
    self_value,
    self_output,
    second_gain,
    second_shift,
    cross_query,
    cross_key,
    cross_value,
    cross_output,
    third_gain,
    third_shift,
    up_weight,
    down_weight,
    cotangent,
):
    clips, span, width = frames.shape
    texts = text_states.shape[1]
    rows = clips * span
    place = Place(width)
    position = place.ctx.astype(jnp.int32).reshape(1)
    half = width // 2
    pairs = half // (2 * HD)

    batches = [
        ("columns", [self_query, self_key, self_value]),
        ("rows", [self_output]),
        ("columns", [cross_query, cross_key, cross_value]),
        ("rows", [cross_output]),
        ("columns", [up_weight]),
        ("rows", [down_weight]),
    ]
    cuts = [[half], [], [half], [], [], []]
    if place.staged:
        pieces = place.first_pieces(batches)
        from_z = [place.exchange_z(piece) for piece in pieces]
        weights = [
            place.assemble(batch, place.exchange_plane(each), cut) for batch, each, cut in zip(batches, from_z, cuts)
        ]
    else:
        weights = [place.gather_plain(batch, cut) for batch, cut in zip(batches, cuts)]
    (w_query, w_key_value), (w_out,), (w_cross_query, w_cross_kv), (w_cross_out,), (w_up,), (w_down,) = weights
    norms = jnp.stack([first_gain, first_shift, second_gain, second_shift, third_gain, third_shift])
    norms = lax.all_gather(norms, "shard", axis=1, tiled=True).astype(F32)
    gain_one, shift_one, gain_two, shift_two, gain_three, shift_three = (norms[i] for i in range(6))

    frames_own = frames.reshape(rows, width)
    frames_before = shifted(frames_own, "ctx", 1)
    frames_all = jnp.concatenate([both(frames_before), both(frames_own)], axis=0)
    normed_one = layer_norm(frames_all.astype(F32), gain_one, shift_one).astype(BF16)
    normed_own = normed_one[2 * rows :]
    queries = product(normed_own, w_query).astype(BF16).reshape(2 * clips, span, half)
    key_values = product(normed_one, w_key_value).astype(BF16).reshape(2, 2 * clips, span, width)
    attended, logs = attend(position, queries, key_values, key_values, 0, pairs, True)
    attended = attended.reshape(2 * rows, half)
    hidden_zero = frames_own.astype(F32)
    hidden_one = hidden_zero + pair_sum(attended, w_out, product)

    normed_two = both(layer_norm(hidden_one, gain_two, shift_two).astype(BF16))
    text = both(text_states.reshape(clips * texts, width))
    cross_q = product(normed_two, w_cross_query).astype(BF16).reshape(2 * clips, span, half)
    cross_kv = product(text, w_cross_kv).astype(BF16).reshape(1, 2 * clips, texts, width)
    cross_att, cross_logs = attend(position, cross_q, cross_kv, cross_kv, 0, pairs, False)
    cross_att = cross_att.reshape(2 * rows, half)
    hidden_two = hidden_one + pair_sum(cross_att, w_cross_out, product)

    normed_three = both(layer_norm(hidden_two, gain_three, shift_three).astype(BF16))
    pre_act = product(normed_three, w_up)
    activated, slope = gelu_parts(pre_act)
    activated = activated.astype(BF16)
    mixed = (hidden_two + pair_sum(activated, w_down, product)).astype(BF16).reshape(clips, span, width)

    cotangent_own = cotangent.reshape(rows, width)
    grad_branch = both(cotangent_own)
    grad_pre = (against(grad_branch, w_down) * slope).astype(BF16)
    grad_down = over_rows(activated, grad_branch).astype(BF16)
    grad_up = over_rows(normed_three, grad_pre).astype(BF16)
    grad_hid, grad_gain_three, grad_shift_three = norm_backward(
        hidden_two, gain_three, pair_sum(grad_pre, w_up, against)
    )
    grad_res = cotangent_own.astype(F32) + grad_hid

    grad_branch = both(grad_res.astype(BF16))
    grad_cross_out = over_rows(cross_att, grad_branch).astype(BF16)
    grad_catt = against(grad_branch, w_cross_out).astype(BF16).reshape(2 * clips, span, half)
    grad_cq, part_ck, part_cv = attend_back(
        position, cross_q, cross_kv, cross_kv, cross_att.reshape(2 * clips, span, half), grad_catt, cross_logs, 0, pairs, False
    )
    grad_cq = grad_cq.reshape(2 * rows, half)
    part = jnp.concatenate([part_ck, part_cv], axis=-1).reshape(2 * clips, texts, width)
    grad_ckv = (part.astype(F32) + swap_ctx(part).astype(F32)).astype(BF16)
    share = texts // lax.axis_size("ctx")
    start = place.ctx * share

    def part_rows(array):
        array = array.reshape(2 * clips, texts, width)
        return lax.dynamic_slice_in_dim(array, start, share, 1).reshape(2 * clips * share, width)

    grad_cross_kv = over_rows(part_rows(text), part_rows(grad_ckv)).astype(BF16)
    grad_text = pair_sum(grad_ckv.reshape(2 * clips * texts, width), w_cross_kv, against).reshape(clips, texts, width)
    grad_cross_query = over_rows(normed_two, grad_cq).astype(BF16)
    grad_hid, grad_gain_two, grad_shift_two = norm_backward(
        hidden_one, gain_two, pair_sum(grad_cq, w_cross_query, against)
    )
    grad_res = grad_res + grad_hid

    grad_branch = both(grad_res.astype(BF16))
    grad_out = over_rows(attended, grad_branch).astype(BF16)
    grad_att = against(grad_branch, w_out).astype(BF16).reshape(2 * clips, span, half)
    grad_q, grad_k, grad_v = attend_back(
        position,
        queries,
        key_values,
        key_values,
        attended.reshape(2 * clips, span, half),
        grad_att,
        logs,
        0,
        pairs,
        True,
    )
    grad_q = grad_q.reshape(2 * rows, half)
    grad_k = grad_k.reshape(4 * rows, half)
    grad_v = grad_v.reshape(4 * rows, half)
    grad_query = over_rows(normed_own, grad_q).astype(BF16)
    grad_kv = jnp.concatenate([grad_k, grad_v], axis=1)
    grad_key_value = over_rows(normed_one, grad_kv).astype(BF16)
    grad_normed_before = pair_sum(grad_kv[: 2 * rows], w_key_value, against)
    returned = shifted(grad_normed_before.astype(BF16), "ctx", -1)
    grad_normed = pair_sum(grad_q, w_query, against) + pair_sum(grad_kv[2 * rows :], w_key_value, against)
    grad_hid, grad_gain_one, grad_shift_one = norm_backward(
        hidden_zero, gain_one, grad_normed + returned.astype(F32)
    )
    grad_frames = (grad_res + grad_hid).reshape(clips, span, width)

    total_down = place.scatter_rows(grad_down)
    (total_up,) = place.scatter_columns(grad_up, 1)
    total_cross_out = place.scatter_rows(grad_cross_out)
    total_cross_key, total_cross_value = place.scatter_columns(grad_cross_kv, 2)
    (total_cross_query,) = place.scatter_columns(grad_cross_query, 1)
    total_out = place.scatter_rows(grad_out)
    total_key, total_value = place.scatter_columns(grad_key_value, 2)
    (total_query,) = place.scatter_columns(grad_query, 1)
    small = jnp.stack(
        [grad_gain_one, grad_shift_one, grad_gain_two, grad_shift_two, grad_gain_three, grad_shift_three]
    )
    small = lax.psum(small, EVERY)
    share = width // place.shards
    small = lax.dynamic_slice_in_dim(small, place.z * share, share, 1)
    return (
        mixed,
        grad_frames,
        grad_text,
        small[0],
        small[1],
        total_query,
        total_key,
        total_value,
        total_out,
        small[2],
        small[3],
        total_cross_query,
        total_cross_key,
        total_cross_value,
        total_cross_out,
        small[4],
        small[5],
        total_up,
        total_down,
    )


def solution(mesh):
    rows = P(("shard", "rep"), "ctx", None)
    vector = P("shard")
    weight = P("shard", None)
    block = (vector, vector, weight, weight, weight, weight)
    in_specs = (rows, P(("shard", "rep"), None, None), *block, *block, vector, vector, weight, weight, rows)
    out_specs = (rows, rows, P(("shard", "rep"), None, None), *block, *block, vector, vector, weight, weight)
    return jax.shard_map(local, mesh=mesh, in_specs=in_specs, out_specs=out_specs, check_vma=False)
```

time: 3130 us -> 1520 us (0.49)
  waiting for transfers between devices: 2440 us -> 670 us
  starting transfers between devices: 12.3 us -> 205 us
  Pallas kernels: 0 us -> 169 us
  matrix products: 394 us -> 247 us
  blocking collectives: 106 us -> 53.2 us
    all_gather x10 -> x8, waiting for transfers between devices: 1100 us -> 0.03 us  [total(): lax.all_gather(summed.astype(BF16), ('ctx', 'rep'), axis=0, tiled=False)]
    reduce_scatter x10 -> x0, waiting for transfers between devices: 1090 us -> none  [the longest x1 317 us: local(): lax.psum_scatter(grad_down.astype(jnp.bfloat16), 'shard', scatter_dimensi...]
    ppermute x0 -> x116, waiting for transfers between devices: none -> 661 us  [xor_permute(): lax.ppermute(array, axis, [(i, i ^ bit) for i in range(lax.axis_size(axis...]
    ppermute x0 -> x116, starting transfers between devices: none -> 196 us  [xor_permute(): lax.ppermute(array, axis, [(i, i ^ bit) for i in range(lax.axis_size(axis...]
    psum x2 -> x0, waiting for transfers between devices: 171 us -> none  [the longest x1 171 us: local(): lax.psum(own_c.astype(jnp.bfloat16), ('ctx', 'rep')).astype(jnp.float32)]
    pallas_call x0 -> x19, Pallas kernels: none -> 169 us  [the longest x6 50.9 us: assemble(): pl.pallas_call(kernel, grid_spec=pltpu.PrefetchScalarGridSpec(num_scalar_...]
    dot_general x43 -> x11, matrix products: 237 us -> 94.6 us  [product(): return jnp.dot(left, right, preferred_element_type=F32)]
    ppermute x4 -> x2, waiting for transfers between devices: 72.6 us -> 8.21 us  [shifted(): return lax.ppermute(block, axis, route)]
  transfers between devices with their start and end apart: 26 -> 126, of which waited for: 21 -> 56; matrix products, arithmetic and copies ran while one was open for 14% -> 18% of each run, Pallas kernels for 0% -> 7%
where the time goes in v1:
time: 1520 us; the launch traced here: 1510 us
  waiting for transfers between devices  670 us (44%)
  matrix products  247 us (16%)
  starting transfers between devices  205 us (13%)
  Pallas kernels  169 us (11%)
  local copies, waits for them, and re-layouts  83.7 us (6%)
  other arithmetic  69.6 us (5%)
  blocking collectives  53.2 us (4%)
  between operations  16.6 us (1%)
    ppermute x116, waiting for transfers between devices, xor_permute(): lax.ppermute(array, axis, [(i, i ^ bit) for i in range(lax.axis_size(axis...  661 us
    ppermute x116, starting transfers between devices, xor_permute(): lax.ppermute(array, axis, [(i, i ^ bit) for i in range(lax.axis_size(axis...  196 us
    dot_general x11, matrix products, product(): return jnp.dot(left, right, preferred_element_type=F32)  94.6 us
    dot_general x15, matrix products, against(): lax.dot_general(left, right, (((1,), (1,)), ((), ())), preferred_element_...  93.1 us
    dot_general x8, matrix products, over_rows(): lax.dot_general(left, right, (((0,), (0,)), ((), ())), preferred_element_...  59.7 us
    pallas_call x6, Pallas kernels, assemble(): pl.pallas_call(kernel, grid_spec=pltpu.PrefetchScalarGridSpec(num_scalar_...  50.9 us
    pallas_call x2, Pallas kernels, attend_back(): pl.pallas_call(lambda *refs: attend_back_kernel(causal, *refs), grid=(cli...  49.7 us
    pallas_call x2, Pallas kernels, attend(): pl.pallas_call(lambda *refs: attend_kernel(causal, *refs), grid=(clips, p...  41.3 us
  transfers between devices with their start and end apart: 126, of which 56 were waited for; matrix products, arithmetic and copies ran while one was open for 18% of the time, Pallas kernels for 7%

profile of v1, /device:TPU:0, one launch (start us, length us, event | category | flops | bytes accessed | tf_op | source)
XLA Modules:
  0.0 1513.5 jit_solution(8239307422961659667)
XLA Ops:
  7.2 6.0 collective-permute-start
  24.2 10.6 collective-permute-done.5
  34.8 26.1 %collective-permute-done.4 = bf16[96,2304]{1,0:T(8,128)(2,1)S(1)} collective-permute-done((bf16[96,2304]{1,0:T(8,128)(2,1)S(1)}, bf16[96,2304]{1,0:T(8,128)(2,1)S(1)}, u32[]{:S(2)}, u32[]{:S(2)}) %collective-permute-start.4) | collective-permute-done | bytes 442400 | tf_op jit(solution)/shard_map/ppermute | solution.py:32
  83.7 9.5 collective-permute-done.7.refs_5_
  109.4 11.2 collective-permute-done.15.refs_4_
  125.9 13.6 all_gather.51
  145.8 11.4 shard_map.331
  166.0 7.3 fusion.5
  176.0 12.3 convolution_convert_fusion.2
  188.3 31.8 %shard_map.332 = (bf16[2,512,768]{2,1,0:T(8,128)(2,1)S(1)}, f32[2,6,2,512]{3,2,1,0:T(2,128)S(1)}) custom-call(s32[1]{0:T(128)} %bitcast.1.refs_0_, bf16[2,512,768]{2,1,0:T(8,128)(2,1)S(1)} %bitcast.458, bf16[2,2,512,1536]{3,2,1,0:T(8,128)(2,1)} %bitcast.517, bf16[2,2,512,1536]{3,2,1,0:T(8,128)(2,1)} %bitcast.518), custom_call_target="tpu_custom_call" | custom-call | flops 6442450944 | bytes 6291456 | tf_op jit(solution)/shard_map/pallas_call | solution.py:175
  228.1 8.4 collective-permute-done.21
  236.6 17.6 %collective-permute-start.28 = (bf16[48,1536]{1,0:T(8,128)(2,1)S(1)}, bf16[48,1536]{1,0:T(8,128)(2,1)S(1)}, u32[]{:S(2)}, u32[]{:S(2)}) collective-permute-start(bf16[48,1536]{1,0:T(8,128)(2,1)S(1)} %get-tuple-element.52), channel_id=1, source_target_pairs={{0,8},{4,12},{8,0},{12,4},{1,9},{5,13},{9,1},{13,5},{2,10},{6,14},... | collective-permute-start | bytes 442376 | tf_op jit(solution)/shard_map/ppermute | solution.py:32
  254.2 14.9 collective-permute-done.20
  279.8 21.6 %collective-permute-done.23.refs_5_ = bf16[3,96,2304]{2,1,0:T(8,128)(2,1)S(1)} collective-permute-done((bf16[3,96,2304]{2,1,0:T(8,128)(2,1)S(1)}, bf16[3,96,2304]{2,1,0:T(8,128)(2,1)S(1)}, u32[]{:S(2)}, u32[]{:S(2)}) %collective-permute-start.23) | collective-permute-done | bytes 1327136 | tf_op jit(solution)/shard_map/ppermute | solution.py:32
  304.6 6.3 collective-permute-done.31.refs_3_
  313.1 15.1 collective-permute-done.32.refs_4_
  330.2 10.2 shard_map.334
  348.5 9.5 shard_map.335
  366.6 11.4 collective-permute-done.45
  378.0 26.6 %collective-permute-start.37 = (bf16[96,3072]{1,0:T(8,128)(2,1)S(1)}, bf16[96,3072]{1,0:T(8,128)(2,1)S(1)}, u32[]{:S(2)}, u32[]{:S(2)}) collective-permute-start(bf16[96,3072]{1,0:T(8,128)(2,1)S(1)} %copy-done.34), channel_id=1, source_target_pairs={{0,8},{4,12},{8,0},{12,4},{1,9},{5,13},{9,1},{13,5},{2,10},{6,14},... | collective-permute-start | bytes 1769480 | tf_op jit(solution)/shard_map/ppermute | solution.py:32
  404.6 35.6 %collective-permute-done.44 = bf16[192,1536]{1,0:T(8,128)(2,1)S(1)} collective-permute-done((bf16[192,1536]{1,0:T(8,128)(2,1)S(1)}, bf16[192,1536]{1,0:T(8,128)(2,1)S(1)}, u32[]{:S(2)}, u32[]{:S(2)}) %collective-permute-start.44) | collective-permute-done | bytes 589856 | tf_op jit(solution)/shard_map/ppermute | solution.py:32
  443.5 21.4 %collective-permute-done.37 = bf16[96,3072]{1,0:T(8,128)(2,1)S(1)} collective-permute-done((bf16[96,3072]{1,0:T(8,128)(2,1)S(1)}, bf16[96,3072]{1,0:T(8,128)(2,1)S(1)}, u32[]{:S(2)}, u32[]{:S(2)}) %collective-permute-start.37) | collective-permute-done | bytes 589856 | tf_op jit(solution)/shard_map/ppermute | solution.py:32
  474.2 43.4 %collective-permute-done.40.refs_3_ = bf16[3,96,3072]{2,1,0:T(8,128)(2,1)S(1)} collective-permute-done((bf16[3,96,3072]{2,1,0:T(8,128)(2,1)S(1)}, bf16[3,96,3072]{2,1,0:T(8,128)(2,1)S(1)}, u32[]{:S(2)}, u32[]{:S(2)}) %collective-permute-start.40) | collective-permute-done | bytes 1769504 | tf_op jit(solution)/shard_map/ppermute | solution.py:32
  522.2 18.1 %collective-permute-done.41.refs_4_ = bf16[3,96,1536]{2,1,0:T(8,128)(2,1)S(1)} collective-permute-done((bf16[3,96,1536]{2,1,0:T(8,128)(2,1)S(1)}, bf16[3,96,1536]{2,1,0:T(8,128)(2,1)S(1)}, u32[]{:S(2)}, u32[]{:S(2)}) %collective-permute-start.41) | collective-permute-done | bytes 884768 | tf_op jit(solution)/shard_map/ppermute | solution.py:32
  542.6 12.6 shard_map.337
  557.7 11.6 shard_map.338
  569.3 42.0 %multiply_convert_fusion = (bf16[1024,3072]{1,0:T(8,128)(2,1)}, f32[1024,3072]{1,0:T(8,128)}, f32[1024,3072]{1,0:T(8,128)}) fusion(bf16[1536,3072]{1,0:T(8,128)(2,1)} %shard_map.337, bf16[512,1536]{1,0:T(8,128)(2,1)} %collective-permute-done.35, bf16[512,1536]{1,0:T(8,128)(2,1)} %add_convert_fusion), kind=kOutput, calls=%fused_computation.18 | convolution fusion | flops 9874440192 | bytes 44040192 | tf_op jit(solution)/shard_map/dot_general | solution.py:20
  612.5 19.3 %fusion.13 = bf16[1024,3072]{1,0:T(8,128)(2,1)} fusion(f32[1024,3072]{1,0:T(8,128)} %get-tuple-element.96, f32[1024,3072]{1,0:T(8,128)} %get-tuple-element.173, bf16[3072,1536]{1,0:T(8,128)(2,1)} %shard_map.338, bf16[512,1536]{1,0:T(8,128)(2,1)S(1)} %collective-permute-done.51, bf16[512,1536]{1,0:T(8,128)(2,1)S(1)} %bitcast.481), kind=kOutput, calls=%fused_computation.17 | convolution fusion | flops 9691987968 | bytes 44040192 | tf_op jit(solution)/shard_map/dot_general | solution.py:28
  631.8 10.5 fusion.53
  646.1 12.4 multiply_reduce_fusion
  661.1 15.3 %convolution_convert_fusion.1 = bf16[1536,3072]{1,0:T(8,128)(2,1)} fusion(bf16[1024,3072]{1,0:T(8,128)(2,1)} %fusion.13, bf16[512,1536]{1,0:T(8,128)(2,1)} %collective-permute-done.35, bf16[512,1536]{1,0:T(8,128)(2,1)} %add_convert_fusion), kind=kOutput, calls=%fused_computation.34 | convolution fusion | flops 9674686464 | bytes 18874368 | tf_op jit(solution)/shard_map/dot_general | solution.py:24
  676.4 8.4 fusion.236
  689.8 13.5 shard_map.339
  729.8 8.1 collective-permute-done.97
  750.7 23.9 %collective-permute-done.98 = bf16[4,48,768]{2,1,0:T(8,128)(2,1)S(1)} collective-permute-done((bf16[4,48,768]{2,1,0:T(8,128)(2,1)S(1)}, bf16[4,48,768]{2,1,0:T(8,128)(2,1)S(1)}, u32[]{:S(2)}, u32[]{:S(2)}) %collective-permute-start.98) | collective-permute-done | bytes 294944 | tf_op jit(solution)/shard_map/ppermute | solution.py:32
  774.8 11.2 collective-permute-start.101
  791.4 8.1 collective-permute-done.102
  823.0 6.7 collective-permute-done.88
  848.4 36.2 %shard_map.340 = (bf16[2,512,768]{2,1,0:T(8,128)(2,1)S(1)}, bf16[2,2,512,768]{3,2,1,0:T(8,128)(2,1)}, bf16[2,2,512,768]{3,2,1,0:T(8,128)(2,1)}) custom-call(s32[1]{0:T(128)} %bitcast.1.refs_0_, bf16[2,512,768]{2,1,0:T(8,128)(2,1)S(1)} %bitcast.459, bf16[2,2,512,1536]{3,2,1,0:T(8,128)(2,1)} %bitcast.519, bf16[2,2,512,1536]{3,2,1,0:T(8,128)(2,1)} %bitcast.520, ...), custom_call_target="tpu_custom_call" | custom-call | flops 16106127360 | bytes 15728640 | tf_op jit(solution)/shard_map/pallas_call | solution.py:204
  888.7 5.9 collective-permute-done.78
  917.8 6.1 collective-permute-done.81
  931.8 24.5 %collective-permute-done.65 = bf16[4,96,384]{2,1,0:T(8,128)(2,1)S(1)} collective-permute-done((bf16[4,96,384]{2,1,0:T(8,128)(2,1)S(1)}, bf16[4,96,384]{2,1,0:T(8,128)(2,1)S(1)}, u32[]{:S(2)}, u32[]{:S(2)}) %collective-permute-start.65) | collective-permute-done | bytes 294944 | tf_op jit(solution)/shard_map/ppermute | solution.py:32
  987.6 8.1 collective-permute-done.95
  996.6 42.5 %collective-permute-done.104 = bf16[4,2,96,1536]{3,2,0,1:T(8,128)(2,1)} collective-permute-done((bf16[4,2,96,1536]{3,2,0,1:T(8,128)(2,1)}, bf16[4,2,96,1536]{3,2,0,1:T(8,128)(2,1)}, u32[]{:S(2)}, u32[]{:S(2)}) %collective-permute-start.104) | collective-permute-done | bytes 2359328 | tf_op jit(solution)/shard_map/ppermute | solution.py:32
  1042.4 13.1 collective-permute-done.107
  1063.6 12.0 collective-permute-done.108
  1075.6 22.2 %collective-permute-done.109 = bf16[96,3072]{1,0:T(8,128)(2,1)S(1)} collective-permute-done((bf16[96,3072]{1,0:T(8,128)(2,1)S(1)}, bf16[96,3072]{1,0:T(8,128)(2,1)S(1)}, u32[]{:S(2)}, u32[]{:S(2)}) %collective-permute-start.109) | collective-permute-done | bytes 589856 | tf_op jit(solution)/shard_map/ppermute | solution.py:32
  1099.0 14.8 convolution_convert_fusion
  1113.8 7.1 fusion.235
  1129.6 51.8 %collective-permute-done.113 = bf16[4,2,192,768]{3,2,0,1:T(8,128)(2,1)S(1)} collective-permute-done((bf16[4,2,192,768]{3,2,0,1:T(8,128)(2,1)S(1)}, bf16[4,2,192,768]{3,2,0,1:T(8,128)(2,1)S(1)}, u32[]{:S(2)}, u32[]{:S(2)}) %collective-permute-start.113) | collective-permute-done | bytes 2359328 | tf_op jit(solution)/shard_map/ppermute | solution.py:32
  1195.4 15.2 %collective-permute-done.114 = bf16[4,192,768]{2,1,0:T(8,128)(2,1)} collective-permute-done((bf16[4,192,768]{2,1,0:T(8,128)(2,1)}, bf16[4,192,768]{2,1,0:T(8,128)(2,1)}, u32[]{:S(2)}, u32[]{:S(2)}) %collective-permute-start.114) | collective-permute-done | bytes 1179680 | tf_op jit(solution)/shard_map/ppermute | solution.py:32
  1214.3 12.3 collective-permute-start.115
  1232.9 14.5 collective-permute-done.115
  1247.4 21.7 %collective-permute-done.116 = bf16[192,1536]{1,0:T(8,128)(2,1)S(1)} collective-permute-done((bf16[192,1536]{1,0:T(8,128)(2,1)S(1)}, bf16[192,1536]{1,0:T(8,128)(2,1)S(1)}, u32[]{:S(2)}, u32[]{:S(2)}) %collective-permute-start.116) | collective-permute-done | bytes 589856 | tf_op jit(solution)/shard_map/ppermute | solution.py:32
  1270.4 10.4 fusion.50
  1285.3 12.4 convolution_convert_fusion.3
  1307.3 32.3 %collective-permute-done.71 = bf16[4,2,96,768]{3,2,0,1:T(8,128)(2,1)S(1)} collective-permute-done((bf16[4,2,96,768]{3,2,0,1:T(8,128)(2,1)S(1)}, bf16[4,2,96,768]{3,2,0,1:T(8,128)(2,1)S(1)}, u32[]{:S(2)}, u32[]{:S(2)}) %collective-permute-start.71) | collective-permute-done | bytes 1179680 | tf_op jit(solution)/shard_map/ppermute | solution.py:32
  1345.8 8.7 collective-permute-done.72
  1371.2 12.7 collective-permute-done.74
  1386.4 12.0 fusion.59
  1409.2 7.4 convolution_add_fusion.5
  1424.2 8.2 collective-permute-done.59
  1438.3 39.5 %psum.7 = f32[6,1536]{1,0:T(8,128)S(1)} all-reduce(f32[6,1536]{1,0:T(8,128)S(1)} %stack.167), channel_id=1, replica_groups=mesh['ctx'=2,'shard'=4,'rep'=4] {'shard','ctx','rep'}, use_global_device_ids=true, to_apply=%region_20.21 | all-reduce | flops 9216 | bytes 73728 | tf_op jit(solution)/shard_map/psum | solution.py:657
  1478.5 5.9 fusion.37
  (673 shorter events, 435.4 us)
Async XLA Ops:
  7.2 1393.7 %all-gather.27.cloned.1.call-start = ((), (), s32[]{:S(2)}) async-start(), calls=%async_computation.5 | async-start | bytes 1327104 | tf_op jit(solution)/shard_map/all_gather | solution.py:418
  7.2 63.6 %collective-permute-start = (bf16[512,1536]{1,0:T(8,128)(2,1)}, bf16[512,1536]{1,0:T(8,128)(2,1)}, u32[]{:S(2)}, u32[]{:S(2)}) collective-permute-start(bf16[512,1536]{1,0:T(8,128)(2,1)} %bitcast), channel_id=1, source_target_pairs={{0,16},{1,17},{2,18},{3,19},{4,20},{5,21},{6,22},{7,23},{8,24},{9,... | collective-permute-start | bytes 4718600 | tf_op jit(solution)/shard_map/ppermute | solution.py:50
  23.4 37.5 %collective-permute-start.4 = (bf16[96,2304]{1,0:T(8,128)(2,1)S(1)}, bf16[96,2304]{1,0:T(8,128)(2,1)S(1)}, u32[]{:S(2)}, u32[]{:S(2)}) collective-permute-start(bf16[96,2304]{1,0:T(8,128)(2,1)S(1)} %get-tuple-element.43), channel_id=1, source_target_pairs={{0,8},{4,12},{8,0},{12,4},{1,9},{5,13},{9,1},{13,5},{2,10},{6,14},... | collective-permute-start | bytes 1327112 | tf_op jit(solution)/shard_map/ppermute | solution.py:32
  23.4 37.5 %collective-permute-start.3 = (bf16[96,2304]{1,0:T(8,128)(2,1)S(1)}, bf16[96,2304]{1,0:T(8,128)(2,1)S(1)}, u32[]{:S(2)}, u32[]{:S(2)}) collective-permute-start(bf16[96,2304]{1,0:T(8,128)(2,1)S(1)} %get-tuple-element.43), channel_id=1, source_target_pairs={{0,4},{4,0},{8,12},{12,8},{1,5},{5,1},{9,13},{13,9},{2,6},{6,2},{1... | collective-permute-start | bytes 1327112 | tf_op jit(solution)/shard_map/ppermute | solution.py:32
  61.1 32.1 %collective-permute-start.7 = (bf16[3,96,2304]{2,1,0:T(8,128)(2,1)S(1)}, bf16[3,96,2304]{2,1,0:T(8,128)(2,1)S(1)}, u32[]{:S(2)}, u32[]{:S(2)}) collective-permute-start(bf16[3,96,2304]{2,1,0:T(8,128)(2,1)S(1)} %pad_maximum_fusion.26.refs_3_), channel_id=1, source_target_pairs={{0,16},{16,0},{1,17},{17,1},{2,18},{18,2},{3,19},{19,3},{4,20},{20... | collective-permute-start | bytes 3981320 | tf_op jit(solution)/shard_map/ppermute | solution.py:32
  61.2 34.5 %collective-permute-start.6 = (bf16[3,96,2304]{2,1,0:T(8,128)(2,1)S(1)}, bf16[3,96,2304]{2,1,0:T(8,128)(2,1)S(1)}, u32[]{:S(2)}, u32[]{:S(2)}) collective-permute-start(bf16[3,96,2304]{2,1,0:T(8,128)(2,1)S(1)} %pad_maximum_fusion.26.refs_3_), channel_id=1, source_target_pairs={{0,2},{1,3},{2,0},{3,1},{4,6},{5,7},{6,4},{7,5},{8,10},{9,11},{10,... | collective-permute-start | bytes 3981320 | tf_op jit(solution)/shard_map/ppermute | solution.py:32
  70.9 86.4 %collective-permute-start.2 = (bf16[512,1536]{1,0:T(8,128)(2,1)}, bf16[512,1536]{1,0:T(8,128)(2,1)}, u32[]{:S(2)}, u32[]{:S(2)}) collective-permute-start(bf16[512,1536]{1,0:T(8,128)(2,1)} %bitcast), channel_id=1, source_target_pairs={{0,1},{1,0},{2,3},{3,2},{4,5},{5,4},{6,7},{7,6},{8,9},{9,8},{10,11... | collective-permute-start | bytes 4718600 | tf_op jit(solution)/shard_map/ppermute | solution.py:32
  70.9 86.4 %collective-permute-start.1 = (bf16[512,1536]{1,0:T(8,128)(2,1)}, bf16[512,1536]{1,0:T(8,128)(2,1)}, u32[]{:S(2)}, u32[]{:S(2)}) collective-permute-start(bf16[512,1536]{1,0:T(8,128)(2,1)} %collective-permute-done), channel_id=1, source_target_pairs={{0,1},{1,0},{2,3},{3,2},{4,5},{5,4},{6,7},{7,6},{8,9},{9,8},{10,11... | collective-permute-start | bytes 4718600 | tf_op jit(solution)/shard_map/ppermute | solution.py:32
  95.7 50.1 %collective-permute-start.8 = (bf16[3,96,1152]{2,1,0:T(8,128)(2,1)}, bf16[3,96,1152]{2,1,0:T(8,128)(2,1)}, u32[]{:S(2)}, u32[]{:S(2)}) collective-permute-start(bf16[3,96,1152]{2,1,0:T(8,128)(2,1)} %slice.285), channel_id=1, source_target_pairs={{0,2},{1,3},{2,0},{3,1},{4,6},{5,7},{6,4},{7,5},{8,10},{9,11},{10,... | collective-permute-start | bytes 1990664 | tf_op jit(solution)/shard_map/ppermute | solution.py:32
  100.8 45.0 %collective-permute-start.9 = (bf16[3,96,1152]{2,1,0:T(8,128)(2,1)}, bf16[3,96,1152]{2,1,0:T(8,128)(2,1)}, u32[]{:S(2)}, u32[]{:S(2)}) collective-permute-start(bf16[3,96,1152]{2,1,0:T(8,128)(2,1)} %slice.286), channel_id=1, source_target_pairs={{0,16},{16,0},{1,17},{17,1},{2,18},{18,2},{3,19},{19,3},{4,20},{20... | collective-permute-start | bytes 1990664 | tf_op jit(solution)/shard_map/ppermute | solution.py:32
  221.5 48.4 %collective-permute-start.17 = (bf16[512,1536]{1,0:T(8,128)(2,1)S(1)}, bf16[512,1536]{1,0:T(8,128)(2,1)S(1)}, u32[]{:S(2)}, u32[]{:S(2)}) collective-permute-start(bf16[512,1536]{1,0:T(8,128)(2,1)S(1)} %convolution_convert_fusion.13), channel_id=1, source_target_pairs={{0,1},{1,0},{2,3},{3,2},{4,5},{5,4},{6,7},{7,6},{8,9},{9,8},{10,11... | collective-permute-start | bytes 4718600 | tf_op jit(solution)/shard_map/ppermute | solution.py:32
  223.7 45.4 %collective-permute-start.20 = (bf16[96,2304]{1,0:T(8,128)(2,1)S(1)}, bf16[96,2304]{1,0:T(8,128)(2,1)S(1)}, u32[]{:S(2)}, u32[]{:S(2)}) collective-permute-start(bf16[96,2304]{1,0:T(8,128)(2,1)S(1)} %copy-done.38), channel_id=1, source_target_pairs={{0,8},{4,12},{8,0},{12,4},{1,9},{5,13},{9,1},{13,5},{2,10},{6,14},... | collective-permute-start | bytes 1327112 | tf_op jit(solution)/shard_map/ppermute | solution.py:32
  223.7 45.4 %collective-permute-start.19 = (bf16[96,2304]{1,0:T(8,128)(2,1)S(1)}, bf16[96,2304]{1,0:T(8,128)(2,1)S(1)}, u32[]{:S(2)}, u32[]{:S(2)}) collective-permute-start(bf16[96,2304]{1,0:T(8,128)(2,1)S(1)} %copy-done.38), channel_id=1, source_target_pairs={{0,4},{4,0},{8,12},{12,8},{1,5},{5,1},{9,13},{13,9},{2,6},{6,2},{1... | collective-permute-start | bytes 1327112 | tf_op jit(solution)/shard_map/ppermute | solution.py:32
  226.0 51.6 %collective-permute-start.29 = (bf16[48,1536]{1,0:T(8,128)(2,1)S(1)}, bf16[48,1536]{1,0:T(8,128)(2,1)S(1)}, u32[]{:S(2)}, u32[]{:S(2)}) collective-permute-start(bf16[48,1536]{1,0:T(8,128)(2,1)S(1)} %get-tuple-element.52), channel_id=1, source_target_pairs={{0,12},{4,8},{8,4},{12,0},{1,13},{5,9},{9,5},{13,1},{2,14},{6,10},... | collective-permute-start | bytes 442376 | tf_op jit(solution)/shard_map/ppermute | solution.py:32
  236.6 41.1 %collective-permute-start.28 = (bf16[48,1536]{1,0:T(8,128)(2,1)S(1)}, bf16[48,1536]{1,0:T(8,128)(2,1)S(1)}, u32[]{:S(2)}, u32[]{:S(2)}) collective-permute-start(bf16[48,1536]{1,0:T(8,128)(2,1)S(1)} %get-tuple-element.52), channel_id=1, source_target_pairs={{0,8},{4,12},{8,0},{12,4},{1,9},{5,13},{9,1},{13,5},{2,10},{6,14},... | collective-permute-start | bytes 442376 | tf_op jit(solution)/shard_map/ppermute | solution.py:32
  269.9 33.1 %collective-permute-start.22 = (bf16[3,96,2304]{2,1,0:T(8,128)(2,1)S(1)}, bf16[3,96,2304]{2,1,0:T(8,128)(2,1)S(1)}, u32[]{:S(2)}, u32[]{:S(2)}) collective-permute-start(bf16[3,96,2304]{2,1,0:T(8,128)(2,1)S(1)} %pad_maximum_fusion.27.refs_3_), channel_id=1, source_target_pairs={{0,2},{1,3},{2,0},{3,1},{4,6},{5,7},{6,4},{7,5},{8,10},{9,11},{10,... | collective-permute-start | bytes 3981320 | tf_op jit(solution)/shard_map/ppermute | solution.py:32
  277.7 66.1 %collective-permute-start.18 = (bf16[512,1536]{1,0:T(8,128)(2,1)}, bf16[512,1536]{1,0:T(8,128)(2,1)}, u32[]{:S(2)}, u32[]{:S(2)}) collective-permute-start(bf16[512,1536]{1,0:T(8,128)(2,1)} %add_convert_fusion.1), channel_id=1, source_target_pairs={{0,1},{1,0},{2,3},{3,2},{4,5},{5,4},{6,7},{7,6},{8,9},{9,8},{10,11... | collective-permute-start | bytes 4718600 | tf_op jit(solution)/shard_map/ppermute | solution.py:32
  277.8 33.1 %collective-permute-start.31 = (bf16[3,48,1536]{2,1,0:T(8,128)(2,1)S(1)}, bf16[3,48,1536]{2,1,0:T(8,128)(2,1)S(1)}, u32[]{:S(2)}, u32[]{:S(2)}) collective-permute-start(bf16[3,48,1536]{2,1,0:T(8,128)(2,1)S(1)} %pad_maximum_fusion.29.refs_1_), channel_id=1, source_target_pairs={{0,16},{16,0},{1,17},{17,1},{2,18},{18,2},{3,19},{19,3},{4,20},{20... | collective-permute-start | bytes 1327112 | tf_op jit(solution)/shard_map/ppermute | solution.py:32
  279.3 33.2 %collective-permute-start.30 = (bf16[3,48,1536]{2,1,0:T(8,128)(2,1)S(1)}, bf16[3,48,1536]{2,1,0:T(8,128)(2,1)S(1)}, u32[]{:S(2)}, u32[]{:S(2)}) collective-permute-start(bf16[3,48,1536]{2,1,0:T(8,128)(2,1)S(1)} %pad_maximum_fusion.29.refs_1_), channel_id=1, source_target_pairs={{0,2},{1,3},{2,0},{3,1},{4,6},{5,7},{6,4},{7,5},{8,10},{9,11},{10,... | collective-permute-start | bytes 1327112 | tf_op jit(solution)/shard_map/ppermute | solution.py:32
  359.4 110.7 %collective-permute-start.34 = (bf16[512,1536]{1,0:T(8,128)(2,1)S(1)}, bf16[512,1536]{1,0:T(8,128)(2,1)S(1)}, u32[]{:S(2)}, u32[]{:S(2)}) collective-permute-start(bf16[512,1536]{1,0:T(8,128)(2,1)S(1)} %convolution_convert_fusion.12), channel_id=1, source_target_pairs={{0,1},{1,0},{2,3},{3,2},{4,5},{5,4},{6,7},{7,6},{8,9},{9,8},{10,11... | collective-permute-start | bytes 4718600 | tf_op jit(solution)/shard_map/ppermute | solution.py:32
  362.2 78.1 %collective-permute-start.44 = (bf16[192,1536]{1,0:T(8,128)(2,1)S(1)}, bf16[192,1536]{1,0:T(8,128)(2,1)S(1)}, u32[]{:S(2)}, u32[]{:S(2)}) collective-permute-start(bf16[192,1536]{1,0:T(8,128)(2,1)S(1)} %copy-done.36), channel_id=1, source_target_pairs={{0,8},{4,12},{8,0},{12,4},{1,9},{5,13},{9,1},{13,5},{2,10},{6,14},... | collective-permute-start | bytes 1769480 | tf_op jit(solution)/shard_map/ppermute | solution.py:32
  363.0 77.2 %collective-permute-start.43 = (bf16[192,1536]{1,0:T(8,128)(2,1)S(1)}, bf16[192,1536]{1,0:T(8,128)(2,1)S(1)}, u32[]{:S(2)}, u32[]{:S(2)}) collective-permute-start(bf16[192,1536]{1,0:T(8,128)(2,1)S(1)} %copy-done.36), channel_id=1, source_target_pairs={{0,4},{4,0},{8,12},{12,8},{1,5},{5,1},{9,13},{13,9},{2,6},{6,2},{1... | collective-permute-start | bytes 1769480 | tf_op jit(solution)/shard_map/ppermute | solution.py:32
  364.3 77.8 %collective-permute-start.38 = (bf16[96,3072]{1,0:T(8,128)(2,1)S(1)}, bf16[96,3072]{1,0:T(8,128)(2,1)S(1)}, u32[]{:S(2)}, u32[]{:S(2)}) collective-permute-start(bf16[96,3072]{1,0:T(8,128)(2,1)S(1)} %copy-done.34), channel_id=1, source_target_pairs={{0,12},{4,8},{8,4},{12,0},{1,13},{5,9},{9,5},{13,1},{2,14},{6,10},... | collective-permute-start | bytes 1769480 | tf_op jit(solution)/shard_map/ppermute | solution.py:32
  378.0 86.9 %collective-permute-start.37 = (bf16[96,3072]{1,0:T(8,128)(2,1)S(1)}, bf16[96,3072]{1,0:T(8,128)(2,1)S(1)}, u32[]{:S(2)}, u32[]{:S(2)}) collective-permute-start(bf16[96,3072]{1,0:T(8,128)(2,1)S(1)} %copy-done.34), channel_id=1, source_target_pairs={{0,8},{4,12},{8,0},{12,4},{1,9},{5,13},{9,1},{13,5},{2,10},{6,14},... | collective-permute-start | bytes 1769480 | tf_op jit(solution)/shard_map/ppermute | solution.py:32
  440.5 78.9 %collective-permute-start.47 = (bf16[3,192,1536]{2,1,0:T(8,128)(2,1)S(1)}, bf16[3,192,1536]{2,1,0:T(8,128)(2,1)S(1)}, u32[]{:S(2)}, u32[]{:S(2)}) collective-permute-start(bf16[3,192,1536]{2,1,0:T(8,128)(2,1)S(1)} %pad_maximum_fusion.19.refs_1_), channel_id=1, source_target_pairs={{0,16},{16,0},{1,17},{17,1},{2,18},{18,2},{3,19},{19,3},{4,20},{20... | collective-permute-start | bytes 5308424 | tf_op jit(solution)/shard_map/ppermute | solution.py:32
  442.0 79.6 %collective-permute-start.46 = (bf16[3,192,1536]{2,1,0:T(8,128)(2,1)S(1)}, bf16[3,192,1536]{2,1,0:T(8,128)(2,1)S(1)}, u32[]{:S(2)}, u32[]{:S(2)}) collective-permute-start(bf16[3,192,1536]{2,1,0:T(8,128)(2,1)S(1)} %pad_maximum_fusion.19.refs_1_), channel_id=1, source_target_pairs={{0,2},{1,3},{2,0},{3,1},{4,6},{5,7},{6,4},{7,5},{8,10},{9,11},{10,... | collective-permute-start | bytes 5308424 | tf_op jit(solution)/shard_map/ppermute | solution.py:32
  467.0 50.6 %collective-permute-start.40 = (bf16[3,96,3072]{2,1,0:T(8,128)(2,1)S(1)}, bf16[3,96,3072]{2,1,0:T(8,128)(2,1)S(1)}, u32[]{:S(2)}, u32[]{:S(2)}) collective-permute-start(bf16[3,96,3072]{2,1,0:T(8,128)(2,1)S(1)} %pad_maximum_fusion.18.refs_1_), channel_id=1, source_target_pairs={{0,16},{16,0},{1,17},{17,1},{2,18},{18,2},{3,19},{19,3},{4,20},{20... | collective-permute-start | bytes 5308424 | tf_op jit(solution)/shard_map/ppermute | solution.py:32
  468.6 51.4 %collective-permute-start.39 = (bf16[3,96,3072]{2,1,0:T(8,128)(2,1)S(1)}, bf16[3,96,3072]{2,1,0:T(8,128)(2,1)S(1)}, u32[]{:S(2)}, u32[]{:S(2)}) collective-permute-start(bf16[3,96,3072]{2,1,0:T(8,128)(2,1)S(1)} %pad_maximum_fusion.18.refs_1_), channel_id=1, source_target_pairs={{0,2},{1,3},{2,0},{3,1},{4,6},{5,7},{6,4},{7,5},{8,10},{9,11},{10,... | collective-permute-start | bytes 5308424 | tf_op jit(solution)/shard_map/ppermute | solution.py:32
  474.2 95.1 %collective-permute-start.35 = (bf16[512,1536]{1,0:T(8,128)(2,1)}, bf16[512,1536]{1,0:T(8,128)(2,1)}, u32[]{:S(2)}, u32[]{:S(2)}) collective-permute-start(bf16[512,1536]{1,0:T(8,128)(2,1)} %add_convert_fusion), channel_id=1, source_target_pairs={{0,1},{1,0},{2,3},{3,2},{4,5},{5,4},{6,7},{7,6},{8,9},{9,8},{10,11... | collective-permute-start | bytes 4718600 | tf_op jit(solution)/shard_map/ppermute | solution.py:32
  519.4 37.3 %collective-permute-start.48 = (bf16[3,192,768]{2,1,0:T(8,128)(2,1)S(1)}, bf16[3,192,768]{2,1,0:T(8,128)(2,1)S(1)}, u32[]{:S(2)}, u32[]{:S(2)}) collective-permute-start(bf16[3,192,768]{2,1,0:T(8,128)(2,1)S(1)} %slice.300), channel_id=1, source_target_pairs={{0,2},{1,3},{2,0},{3,1},{4,6},{5,7},{6,4},{7,5},{8,10},{9,11},{10,... | collective-permute-start | bytes 2654216 | tf_op jit(solution)/shard_map/ppermute | solution.py:32
  521.7 36.1 %collective-permute-start.49 = (bf16[3,192,768]{2,1,0:T(8,128)(2,1)S(1)}, bf16[3,192,768]{2,1,0:T(8,128)(2,1)S(1)}, u32[]{:S(2)}, u32[]{:S(2)}) collective-permute-start(bf16[3,192,768]{2,1,0:T(8,128)(2,1)S(1)} %slice.301), channel_id=1, source_target_pairs={{0,16},{16,0},{1,17},{17,1},{2,18},{18,2},{3,19},{19,3},{4,20},{20... | collective-permute-start | bytes 2654216 | tf_op jit(solution)/shard_map/ppermute | solution.py:32
  540.3 71.0 %collective-permute-start.51 = (bf16[512,1536]{1,0:T(8,128)(2,1)S(1)}, bf16[512,1536]{1,0:T(8,128)(2,1)S(1)}, u32[]{:S(2)}, u32[]{:S(2)}) collective-permute-start(bf16[512,1536]{1,0:T(8,128)(2,1)S(1)} %bitcast.480), channel_id=1, source_target_pairs={{0,1},{1,0},{2,3},{3,2},{4,5},{5,4},{6,7},{7,6},{8,9},{9,8},{10,11... | collective-permute-start | bytes 4718600 | tf_op jit(solution)/shard_map/ppermute | solution.py:32
  717.6 32.9 %collective-permute-start.83 = (bf16[4,2,96,384]{3,2,0,1:T(8,128)(2,1)S(1)}, bf16[4,2,96,384]{3,2,0,1:T(8,128)(2,1)S(1)}, u32[]{:S(2)}, u32[]{:S(2)}) collective-permute-start(bf16[4,2,96,384]{3,2,0,1:T(8,128)(2,1)S(1)} %bitcast.497), channel_id=1, source_target_pairs={{0,16},{16,0},{1,17},{17,1},{2,18},{18,2},{3,19},{19,3},{4,20},{20... | collective-permute-start | bytes 1769480 | tf_op jit(solution)/shard_map/ppermute | solution.py:32
  725.2 76.6 %collective-permute-start.54 = (bf16[512,1536]{1,0:T(8,128)(2,1)}, bf16[512,1536]{1,0:T(8,128)(2,1)}, u32[]{:S(2)}, u32[]{:S(2)}) collective-permute-start(bf16[512,1536]{1,0:T(8,128)(2,1)} %convolution_convert_fusion.11), channel_id=1, source_target_pairs={{0,1},{1,0},{2,3},{3,2},{4,5},{5,4},{6,7},{7,6},{8,9},{9,8},{10,11... | collective-permute-start | bytes 4718600 | tf_op jit(solution)/shard_map/ppermute | solution.py:32
  737.8 92.7 %collective-permute-start.92 = (bf16[4,2,96,768]{3,2,0,1:T(8,128)(2,1)}, bf16[4,2,96,768]{3,2,0,1:T(8,128)(2,1)}, u32[]{:S(2)}, u32[]{:S(2)}) collective-permute-start(bf16[4,2,96,768]{3,2,0,1:T(8,128)(2,1)} %bitcast.430), channel_id=1, source_target_pairs={{0,2},{1,3},{2,0},{3,1},{4,6},{5,7},{6,4},{7,5},{8,10},{9,11},{10,... | collective-permute-start | bytes 3538952 | tf_op jit(solution)/shard_map/ppermute | solution.py:32
  801.8 603.4 %all-gather.23.cloned.1.call-start = ((), (), s32[]{:S(2)}) async-start(), calls=%async_computation.3 | async-start | bytes 1327104 | tf_op jit(solution)/shard_map/all_gather | solution.py:418
  822.7 159.1 %collective-permute-start.106 = (bf16[4,2,96,1536]{3,2,0,1:T(8,128)(2,1)}, bf16[4,2,96,1536]{3,2,0,1:T(8,128)(2,1)}, u32[]{:S(2)}, u32[]{:S(2)}) collective-permute-start(bf16[4,2,96,1536]{3,2,0,1:T(8,128)(2,1)} %bitcast.428), channel_id=1, source_target_pairs={{0,2},{1,3},{2,0},{3,1},{4,6},{5,7},{6,4},{7,5},{8,10},{9,11},{10,... | collective-permute-start | bytes 7077896 | tf_op jit(solution)/shard_map/ppermute | solution.py:32
  830.5 586.1 %all-gather.21.cloned.1.call-start = ((), (), s32[]{:S(2)}) async-start(), calls=%async_computation.2 | async-start | bytes 1327104 | tf_op jit(solution)/shard_map/all_gather | solution.py:418
  839.2 55.4 %collective-permute-start.78 = (bf16[4,2,48,768]{3,2,0,1:T(8,128)(2,1)}, bf16[4,2,48,768]{3,2,0,1:T(8,128)(2,1)}, u32[]{:S(2)}, u32[]{:S(2)}) collective-permute-start(bf16[4,2,48,768]{3,2,0,1:T(8,128)(2,1)} %bitcast.438), channel_id=1, source_target_pairs={{0,2},{1,3},{2,0},{3,1},{4,6},{5,7},{6,4},{7,5},{8,10},{9,11},{10,... | collective-permute-start | bytes 1769480 | tf_op jit(solution)/shard_map/ppermute | solution.py:32
  841.8 55.1 %collective-permute-start.76 = (bf16[4,2,48,768]{3,2,0,1:T(8,128)(2,1)}, bf16[4,2,48,768]{3,2,0,1:T(8,128)(2,1)S(1)}, u32[]{:S(2)}, u32[]{:S(2)}) collective-permute-start(bf16[4,2,48,768]{3,2,0,1:T(8,128)(2,1)} %bitcast.439), channel_id=1, source_target_pairs={{0,16},{16,0},{1,17},{17,1},{2,18},{18,2},{3,19},{19,3},{4,20},{20... | collective-permute-start | bytes 1769480 | tf_op jit(solution)/shard_map/ppermute | solution.py:32
  916.1 43.6 %collective-permute-start.90 = (bf16[4,2,96,768]{3,2,0,1:T(8,128)(2,1)}, bf16[4,2,96,768]{3,2,0,1:T(8,128)(2,1)}, u32[]{:S(2)}, u32[]{:S(2)}) collective-permute-start(bf16[4,2,96,768]{3,2,0,1:T(8,128)(2,1)} %bitcast.431), channel_id=1, source_target_pairs={{0,16},{16,0},{1,17},{17,1},{2,18},{18,2},{3,19},{19,3},{4,20},{20... | collective-permute-start | bytes 3538952 | tf_op jit(solution)/shard_map/ppermute | solution.py:32
  924.0 32.3 %collective-permute-start.65 = (bf16[4,96,384]{2,1,0:T(8,128)(2,1)S(1)}, bf16[4,96,384]{2,1,0:T(8,128)(2,1)S(1)}, u32[]{:S(2)}, u32[]{:S(2)}) collective-permute-start(bf16[4,96,384]{2,1,0:T(8,128)(2,1)S(1)} %dynamic-slice_bitcast_fusion.14), channel_id=1, source_target_pairs={{0,16},{16,0},{1,17},{17,1},{2,18},{18,2},{3,19},{19,3},{4,20},{20... | collective-permute-start | bytes 884744 | tf_op jit(solution)/shard_map/ppermute | solution.py:32
  926.6 494.2 %all-gather.17.cloned.1.call-start = ((), (), s32[]{:S(2)}) async-start(), calls=%async_computation | async-start | bytes 1327104 | tf_op jit(solution)/shard_map/all_gather | solution.py:418
  931.1 43.5 %collective-permute-start.93 = (bf16[4,96,768]{2,1,0:T(8,128)(2,1)}, bf16[4,96,768]{2,1,0:T(8,128)(2,1)}, u32[]{:S(2)}, u32[]{:S(2)}) collective-permute-start(bf16[4,96,768]{2,1,0:T(8,128)(2,1)} %dynamic-slice_bitcast_fusion.4), channel_id=1, source_target_pairs={{0,16},{16,0},{1,17},{17,1},{2,18},{18,2},{3,19},{19,3},{4,20},{20... | collective-permute-start | bytes 1769480 | tf_op jit(solution)/shard_map/ppermute | solution.py:32
  971.4 67.6 %collective-permute-start.104 = (bf16[4,2,96,1536]{3,2,0,1:T(8,128)(2,1)}, bf16[4,2,96,1536]{3,2,0,1:T(8,128)(2,1)}, u32[]{:S(2)}, u32[]{:S(2)}) collective-permute-start(bf16[4,2,96,1536]{3,2,0,1:T(8,128)(2,1)} %bitcast.429), channel_id=1, source_target_pairs={{0,16},{16,0},{1,17},{17,1},{2,18},{18,2},{3,19},{19,3},{4,20},{20... | collective-permute-start | bytes 7077896 | tf_op jit(solution)/shard_map/ppermute | solution.py:32
  974.1 510.3 %all-gather.25.cloned.1.call-start = ((), (), s32[]{:S(2)}) async-start(), calls=%async_computation.4 | async-start | bytes 2654208 | tf_op jit(solution)/shard_map/all_gather | solution.py:418
  985.7 69.8 %collective-permute-start.107 = (bf16[4,96,1536]{2,1,0:T(8,128)(2,1)S(1)}, bf16[4,96,1536]{2,1,0:T(8,128)(2,1)}, u32[]{:S(2)}, u32[]{:S(2)}) collective-permute-start(bf16[4,96,1536]{2,1,0:T(8,128)(2,1)S(1)} %dynamic-slice_bitcast_fusion.2), channel_id=1, source_target_pairs={{0,16},{16,0},{1,17},{17,1},{2,18},{18,2},{3,19},{19,3},{4,20},{20... | collective-permute-start | bytes 3538952 | tf_op jit(solution)/shard_map/ppermute | solution.py:32
  996.5 492.2 %all-gather.29.cloned.1.call-start = ((), (), s32[]{:S(2)}) async-start(), calls=%async_computation.6 | async-start | bytes 5308416 | tf_op jit(solution)/shard_map/all_gather | solution.py:418
  1059.2 38.6 %collective-permute-start.109 = (bf16[96,3072]{1,0:T(8,128)(2,1)S(1)}, bf16[96,3072]{1,0:T(8,128)(2,1)S(1)}, u32[]{:S(2)}, u32[]{:S(2)}) collective-permute-start(bf16[96,3072]{1,0:T(8,128)(2,1)S(1)} %get-tuple-element.117), channel_id=1, source_target_pairs={{0,8},{4,12},{8,0},{12,4},{1,9},{5,13},{9,1},{13,5},{2,10},{6,14},... | collective-permute-start | bytes 1769480 | tf_op jit(solution)/shard_map/ppermute | solution.py:32
  1061.4 36.4 %collective-permute-start.110 = (bf16[96,3072]{1,0:T(8,128)(2,1)S(1)}, bf16[96,3072]{1,0:T(8,128)(2,1)S(1)}, u32[]{:S(2)}, u32[]{:S(2)}) collective-permute-start(bf16[96,3072]{1,0:T(8,128)(2,1)S(1)} %get-tuple-element.118), channel_id=1, source_target_pairs={{0,12},{4,8},{8,4},{12,0},{1,13},{5,9},{9,5},{13,1},{2,14},{6,10},... | collective-permute-start | bytes 1769480 | tf_op jit(solution)/shard_map/ppermute | solution.py:32
  1099.0 396.0 %all-gather.31.cloned.1.call-start = ((), (), s32[]{:S(2)}) async-start(), calls=%async_computation.7 | async-start | bytes 5308416 | tf_op jit(solution)/shard_map/all_gather | solution.py:418
  1123.7 57.7 %collective-permute-start.113 = (bf16[4,2,192,768]{3,2,0,1:T(8,128)(2,1)S(1)}, bf16[4,2,192,768]{3,2,0,1:T(8,128)(2,1)S(1)}, u32[]{:S(2)}, u32[]{:S(2)}) collective-permute-start(bf16[4,2,192,768]{3,2,0,1:T(8,128)(2,1)S(1)} %bitcast.475), channel_id=1, source_target_pairs={{0,2},{1,3},{2,0},{3,1},{4,6},{5,7},{6,4},{7,5},{8,10},{9,11},{10,... | collective-permute-start | bytes 7077896 | tf_op jit(solution)/shard_map/ppermute | solution.py:32
  1127.1 64.3 %collective-permute-start.111 = (bf16[4,2,192,768]{3,2,0,1:T(8,128)(2,1)S(1)}, bf16[4,2,192,768]{3,2,0,1:T(8,128)(2,1)S(1)}, u32[]{:S(2)}, u32[]{:S(2)}) collective-permute-start(bf16[4,2,192,768]{3,2,0,1:T(8,128)(2,1)S(1)} %bitcast.474), channel_id=1, source_target_pairs={{0,16},{16,0},{1,17},{17,1},{2,18},{18,2},{3,19},{19,3},{4,20},{20... | collective-permute-start | bytes 7077896 | tf_op jit(solution)/shard_map/ppermute | solution.py:32
  1214.3 33.1 %collective-permute-start.115 = (bf16[192,1536]{1,0:T(8,128)(2,1)S(1)}, bf16[192,1536]{1,0:T(8,128)(2,1)S(1)}, u32[]{:S(2)}, u32[]{:S(2)}) collective-permute-start(bf16[192,1536]{1,0:T(8,128)(2,1)S(1)} %get-tuple-element.113), channel_id=1, source_target_pairs={{0,4},{4,0},{8,12},{12,8},{1,5},{5,1},{9,13},{13,9},{2,6},{6,2},{1... | collective-permute-start | bytes 1769480 | tf_op jit(solution)/shard_map/ppermute | solution.py:32
  1226.6 42.5 %collective-permute-start.116 = (bf16[192,1536]{1,0:T(8,128)(2,1)S(1)}, bf16[192,1536]{1,0:T(8,128)(2,1)S(1)}, u32[]{:S(2)}, u32[]{:S(2)}) collective-permute-start(bf16[192,1536]{1,0:T(8,128)(2,1)S(1)} %get-tuple-element.114), channel_id=1, source_target_pairs={{0,8},{4,12},{8,0},{12,4},{1,9},{5,13},{9,1},{13,5},{2,10},{6,14},... | collective-permute-start | bytes 1769480 | tf_op jit(solution)/shard_map/ppermute | solution.py:32
  1229.5 39.5 %collective-permute-start.117 = (bf16[192,1536]{1,0:T(8,128)(2,1)S(1)}, bf16[192,1536]{1,0:T(8,128)(2,1)S(1)}, u32[]{:S(2)}, u32[]{:S(2)}) collective-permute-start(bf16[192,1536]{1,0:T(8,128)(2,1)S(1)} %get-tuple-element.115), channel_id=1, source_target_pairs={{0,12},{4,8},{8,4},{12,0},{1,13},{5,9},{9,5},{13,1},{2,14},{6,10},... | collective-permute-start | bytes 1769480 | tf_op jit(solution)/shard_map/ppermute | solution.py:32
  1270.2 231.9 %all-gather.19.cloned.1.call-start = ((), (), s32[]{:S(2)}) async-start(), calls=%async_computation.1 | async-start | bytes 2654208 | tf_op jit(solution)/shard_map/all_gather | solution.py:418
  1280.8 105.6 %collective-permute-start.50 = (bf16[512,1536]{1,0:T(8,128)(2,1)}, bf16[512,1536]{1,0:T(8,128)(2,1)}, u32[]{:S(2)}, u32[]{:S(2)}) collective-permute-start(bf16[512,1536]{1,0:T(8,128)(2,1)} %fusion.50), channel_id=1, source_target_pairs={{0,1},{1,0},{2,3},{3,2},{4,5},{5,4},{6,7},{7,6},{8,9},{9,8},{10,11... | collective-permute-start | bytes 4718600 | tf_op jit(solution)/shard_map/ppermute | solution.py:32
  1284.9 113.6 %collective-permute-start.61 = (bf16[64,1536]{1,0:T(8,128)(2,1)S(1)}, bf16[64,1536]{1,0:T(8,128)(2,1)S(1)}, u32[]{:S(2)}, u32[]{:S(2)}) collective-permute-start(bf16[64,1536]{1,0:T(8,128)(2,1)S(1)} %convolution_convert_fusion.15), channel_id=1, source_target_pairs={{0,1},{1,0},{2,3},{3,2},{4,5},{5,4},{6,7},{7,6},{8,9},{9,8},{10,11... | collective-permute-start | bytes 589832 | tf_op jit(solution)/shard_map/ppermute | solution.py:32
  1298.8 40.7 %collective-permute-start.71 = (bf16[4,2,96,768]{3,2,0,1:T(8,128)(2,1)S(1)}, bf16[4,2,96,768]{3,2,0,1:T(8,128)(2,1)S(1)}, u32[]{:S(2)}, u32[]{:S(2)}) collective-permute-start(bf16[4,2,96,768]{3,2,0,1:T(8,128)(2,1)S(1)} %bitcast.485), channel_id=1, source_target_pairs={{0,2},{1,3},{2,0},{3,1},{4,6},{5,7},{6,4},{7,5},{8,10},{9,11},{10,... | collective-permute-start | bytes 3538952 | tf_op jit(solution)/shard_map/ppermute | solution.py:32
  1300.6 40.9 %collective-permute-start.69 = (bf16[4,2,96,768]{3,2,0,1:T(8,128)(2,1)S(1)}, bf16[4,2,96,768]{3,2,0,1:T(8,128)(2,1)S(1)}, u32[]{:S(2)}, u32[]{:S(2)}) collective-permute-start(bf16[4,2,96,768]{3,2,0,1:T(8,128)(2,1)S(1)} %bitcast.484), channel_id=1, source_target_pairs={{0,16},{16,0},{1,17},{17,1},{2,18},{18,2},{3,19},{19,3},{4,20},{20... | collective-permute-start | bytes 3538952 | tf_op jit(solution)/shard_map/ppermute | solution.py:32
  1303.5 58.0 %collective-permute-start.58 = (bf16[512,1536]{1,0:T(8,128)(2,1)S(1)}, bf16[512,1536]{1,0:T(8,128)(2,1)S(1)}, u32[]{:S(2)}, u32[]{:S(2)}) collective-permute-start(bf16[512,1536]{1,0:T(8,128)(2,1)S(1)} %convolution_convert_fusion.8), channel_id=1, source_target_pairs={{0,1},{1,0},{2,3},{3,2},{4,5},{5,4},{6,7},{7,6},{8,9},{9,8},{10,11... | collective-permute-start | bytes 4718600 | tf_op jit(solution)/shard_map/ppermute | solution.py:32
  1371.2 53.0 %collective-permute-start.56 = (bf16[512,1536]{1,0:T(8,128)(2,1)}, bf16[512,1536]{1,0:T(8,128)(2,1)}, u32[]{:S(2)}, u32[]{:S(2)}) collective-permute-start(bf16[512,1536]{1,0:T(8,128)(2,1)} %convolution_convert_fusion.10), channel_id=1, source_target_pairs={{0,1},{1,0},{2,3},{3,2},{4,5},{5,4},{6,7},{7,6},{8,9},{9,8},{10,11... | collective-permute-start | bytes 4718600 | tf_op jit(solution)/shard_map/ppermute | solution.py:32
  1383.9 48.5 %collective-permute-start.59 = (bf16[512,1536]{1,0:T(8,128)(2,1)}, bf16[512,1536]{1,0:T(8,128)(2,1)}, u32[]{:S(2)}, u32[]{:S(2)}) collective-permute-start(bf16[512,1536]{1,0:T(8,128)(2,1)} %fusion.49), channel_id=1, source_target_pairs={{16,0},{17,1},{18,2},{19,3},{20,4},{21,5},{22,6},{23,7},{24,8},{25... | collective-permute-start | bytes 4718600 | tf_op jit(solution)/shard_map/ppermute | solution.py:50
  (186 other events, 3555.7 us)
Sparse Core Ops, SparseCore 0:
  801.9 22.5 all-gather.26
  830.6 29.0 all-gather.22
  926.8 27.5 all-gather.20
  974.2 29.0 all-gather.16
  1005.1 38.5 all-gather.24
  1099.1 63.0 all-gather.28
  1270.3 60.2 all-gather.30
  1386.5 42.8 all-gather.18

commit v2 on v1

v2 whole, which is shorter than its diff:
```python
import math

import jax
import jax.numpy as jnp
from jax import lax
from jax.experimental import pallas as pl
from jax.experimental.pallas import tpu as pltpu
from jax.sharding import PartitionSpec as P

HD = 64
EPS = 1e-05
NEG = -1e30
BF16 = jnp.bfloat16
F32 = jnp.float32
VMEM_LIMIT = 48 * 1024 * 1024
PLANE = ("ctx", "y")
FEED = ("shard", "y")
EVERY = ("shard", "ctx", "y", "core")


def product(left, right):
    return jnp.dot(left, right, preferred_element_type=F32)


def over_rows(left, right):
    return lax.dot_general(left, right, (((0,), (0,)), ((), ())), preferred_element_type=F32)


def against(left, right):
    return lax.dot_general(left, right, (((1,), (1,)), ((), ())), preferred_element_type=F32)


def xor_permute(array, axis, bit):
    return lax.ppermute(array, axis, [(i, i ^ bit) for i in range(lax.axis_size(axis))])


def swap_ctx(array):
    return xor_permute(array, "ctx", 1)


def swap_row(array):
    return xor_permute(array, "y", 1)


def swap_core(array):
    return xor_permute(array, "core", 1)


def tied(*groups):
    return lax.optimization_barrier(groups)


def shifted(block, axis, distance):
    devices = range(lax.axis_size(axis))
    route = [(i - distance, i) for i in devices if i - distance in devices]
    return lax.ppermute(block, axis, route)


def pick(array, index, axis):
    return lax.dynamic_index_in_dim(array, index, axis, keepdims=False)


def both(own):
    return jnp.concatenate([own, swap_core(own)], axis=0)


def pair_sum(left, right, multiply):
    half = left.shape[0] // 2
    other = swap_core(multiply(left[half:], right).astype(BF16))
    return multiply(left[:half], right) + other.astype(F32)


class QuadSum:
    def __init__(self, near, far, right, multiply):
        half = near.shape[0] // 2
        sent = jnp.concatenate(
            [multiply(far[half:], right).astype(BF16), multiply(near[half:], right).astype(BF16)], axis=0
        )
        self.parts = sent, multiply(far[:half], right), multiply(near[:half], right)

    def cores(self):
        sent, far, near = self.parts
        half = near.shape[0]
        got = swap_core(sent).astype(F32)
        return (far + got[:half]).astype(BF16), near + got[half:]

    def total(self):
        far, near = self.cores()
        return near + swap_ctx(far).astype(F32)


def nt(left, right):
    return lax.dot_general(left, right, (((1,), (1,)), ((), ())), preferred_element_type=F32)


def tn(left, right):
    return lax.dot_general(left, right, (((0,), (0,)), ((), ())), preferred_element_type=F32)


def nn(left, right):
    return lax.dot_general(left, right, (((1,), (0,)), ((), ())), preferred_element_type=F32)


def query_block(span):
    return math.gcd(span, 256)


def key_chunks(causal, block, index):
    if not causal:
        return [(0, None, "none")]
    return [(0, None, "earlier"), (1, (index + 1) * block, "own")]


def masked(scores, mode, position, block, index):
    if mode == "earlier":
        return jnp.where(position > 0, scores, NEG)
    if mode == "own":
        row = lax.broadcasted_iota(jnp.int32, scores.shape, 0)
        column = lax.broadcasted_iota(jnp.int32, scores.shape, 1) + index * block
        return jnp.where(row <= column, scores, NEG)
    return scores


def attend_kernel(causal, position_ref, q_ref, k_ref, v_ref, o_ref, log_ref):
    position = position_ref[0]
    span = q_ref.shape[1]
    block = query_block(span)
    low = lax.broadcasted_iota(jnp.int32, (block, 2 * HD), 1) < HD
    for index in range(span // block):
        rows = pl.ds(index * block, block)
        queries = q_ref[0, rows, :] * BF16(HD ** -0.5)
        parts = []
        for head in range(2):
            side = jnp.where(low == (head == 0), queries, jnp.zeros_like(queries))
            scores = []
            for part, extent, mode in key_chunks(causal, block, index):
                keys = k_ref[part, 0, :extent, :]
                scores.append(masked(nt(keys, side), mode, position, block, index))
            top = scores[0].max(axis=0, keepdims=True)
            for other in scores[1:]:
                top = jnp.maximum(top, other.max(axis=0, keepdims=True))
            weights = [jnp.exp(each - top) for each in scores]
            total = sum(each.sum(axis=0, keepdims=True) for each in weights)
            inverse = 1.0 / total
            out = None
            for weight, (part, extent, mode) in zip(weights, key_chunks(causal, block, index)):
                term = tn(v_ref[part, 0, :extent, :], (weight * inverse).astype(BF16))
                out = term if out is None else out + term
            parts.append(out)
            log_ref[0, 0, head : head + 1, rows] = top + jnp.log(total)
        upper = lax.broadcasted_iota(jnp.int32, parts[0].shape, 0) < HD
        o_ref[0, rows, :] = jnp.where(upper, parts[0], parts[1]).T.astype(BF16)


def attend_back_kernel(
    causal, position_ref, q_ref, k_ref, v_ref, o_ref, g_ref, log_ref, dq_ref, dk_ref, dv_ref, dk_acc, dv_acc
):
    position = position_ref[0]
    span = q_ref.shape[1]
    block = query_block(span)
    low = lax.broadcasted_iota(jnp.int32, (block, 2 * HD), 1) < HD
    dk_acc[...] = jnp.zeros_like(dk_acc)
    dv_acc[...] = jnp.zeros_like(dv_acc)
    for index in range(span // block):
        rows = pl.ds(index * block, block)
        queries = q_ref[0, rows, :] * BF16(HD ** -0.5)
        grads = g_ref[0, rows, :]
        flat = (grads.astype(F32) * o_ref[0, rows, :].astype(F32)).T
        parts = []
        for head in range(2):
            mine = low == (head == 0)
            side = jnp.where(mine, queries, jnp.zeros_like(queries))
            grad = jnp.where(mine, grads, jnp.zeros_like(grads))
            delta = flat[head * HD : (head + 1) * HD].sum(axis=0, keepdims=True)
            log_total = log_ref[0, 0, head : head + 1, rows]
            dq = None
            for part, extent, mode in key_chunks(causal, block, index):
                keys = k_ref[part, 0, :extent, :]
                scores = masked(nt(keys, side), mode, position, block, index)
                probs = jnp.exp(scores - log_total)
                grad_probs = nt(v_ref[part, 0, :extent, :], grad)
                grad_scores = (probs * (grad_probs - delta)).astype(BF16)
                dk_acc[part, :extent, :] += nn(grad_scores, side)
                dv_acc[part, :extent, :] += nn(probs.astype(BF16), grad)
                term = tn(keys, grad_scores)
                dq = term if dq is None else dq + term
            parts.append(dq)
        upper = lax.broadcasted_iota(jnp.int32, parts[0].shape, 0) < HD
        dq_ref[0, rows, :] = (jnp.where(upper, parts[0], parts[1]).T * HD ** -0.5).astype(BF16)
    dk_ref[:, 0] = dk_acc[...].astype(BF16)
    dv_ref[:, 0] = dv_acc[...].astype(BF16)


def attend(position, queries, keys, values, key_base, value_base, causal):
    clips, span, width = queries.shape
    parts, unused, length, unused = keys.shape
    pair = 2 * HD
    pairs = width // pair
    work = 2 * clips * span * length * parts * width
    return pl.pallas_call(
        lambda *refs: attend_kernel(causal, *refs),
        grid=(clips, pairs),
        in_specs=[
            pl.BlockSpec(memory_space=pltpu.SMEM),
            pl.BlockSpec((1, span, pair), lambda b, j: (b, 0, j)),
            pl.BlockSpec((parts, 1, length, pair), lambda b, j: (0, b, 0, key_base + j)),
            pl.BlockSpec((parts, 1, length, pair), lambda b, j: (0, b, 0, value_base + j)),
        ],
        out_specs=[
            pl.BlockSpec((1, span, pair), lambda b, j: (b, 0, j)),
            pl.BlockSpec((1, 1, 2, span), lambda b, j: (b, j, 0, 0)),
        ],
        out_shape=[
            jax.ShapeDtypeStruct((clips, span, width), BF16),
            jax.ShapeDtypeStruct((clips, pairs, 2, span), F32),
        ],
        compiler_params=pltpu.CompilerParams(vmem_limit_bytes=VMEM_LIMIT),
        cost_estimate=pl.CostEstimate(flops=0, bytes_accessed=0, transcendentals=0),
    )(position, queries, keys, values)


def attend_back(position, queries, keys, values, out, grad, logs, key_base, value_base, causal):
    clips, span, width = queries.shape
    parts, unused, length, unused = keys.shape
    pair = 2 * HD
    pairs = width // pair
    work = 2 * clips * span * length * parts * width
    row_spec = pl.BlockSpec((1, span, pair), lambda b, j: (b, 0, j))
    return pl.pallas_call(
        lambda *refs: attend_back_kernel(causal, *refs),
        grid=(clips, pairs),
        in_specs=[
            pl.BlockSpec(memory_space=pltpu.SMEM),
            row_spec,
            pl.BlockSpec((parts, 1, length, pair), lambda b, j: (0, b, 0, key_base + j)),
            pl.BlockSpec((parts, 1, length, pair), lambda b, j: (0, b, 0, value_base + j)),
            row_spec,
            row_spec,
            pl.BlockSpec((1, 1, 2, span), lambda b, j: (b, j, 0, 0)),
        ],
        out_specs=[
            row_spec,
            pl.BlockSpec((parts, 1, length, pair), lambda b, j: (0, b, 0, j)),
            pl.BlockSpec((parts, 1, length, pair), lambda b, j: (0, b, 0, j)),
        ],
        out_shape=[
            jax.ShapeDtypeStruct((clips, span, width), BF16),
            jax.ShapeDtypeStruct((parts, clips, length, width), BF16),
            jax.ShapeDtypeStruct((parts, clips, length, width), BF16),
        ],
        scratch_shapes=[
            pltpu.VMEM((parts, length, pair), F32),
            pltpu.VMEM((parts, length, pair), F32),
        ],
        compiler_params=pltpu.CompilerParams(vmem_limit_bytes=VMEM_LIMIT),
        cost_estimate=pl.CostEstimate(flops=0, bytes_accessed=0, transcendentals=0),
    )(position, queries, keys, values, out, grad, logs)


def strip_parts(block, strips, share, index):
    size = block.shape[-1] // (share * strips)
    return [block[..., (share * j + index) * size : (share * j + index + 1) * size] for j in range(strips)]


KINDS = {"columns": (True, 2, 4), "rows": (False, 2, 4), "feed_columns": (True, 4, 2), "feed_rows": (False, 4, 2)}


class Place:
    def __init__(self, width):
        self.shards = lax.axis_size("shard")
        self.ctx = lax.axis_index("ctx")
        self.z = lax.axis_index("shard")
        self.core = lax.axis_index("core")
        self.y = lax.axis_index("y")
        self.staged = (
            self.shards == 4
            and lax.axis_size("ctx") == 2
            and lax.axis_size("y") == 2
            and (width // self.shards) % (2 * HD) == 0
            and (width // self.shards) % 128 == 0
        )
        self.strips = self.shards if self.staged else 1
        self.quarter = width // 16
        self.spot = jnp.stack(
            [self.z, self.ctx * 2 + self.y, self.y, self.core, self.core * 2 + self.ctx]
        ).astype(jnp.int32)

    def own_columns(self, array):
        rows, width = array.shape
        return lax.dynamic_slice_in_dim(array, self.core * (width // 2), width // 2, 1)

    def own_rows(self, array):
        rows, width = array.shape
        return lax.dynamic_slice_in_dim(array, self.core * (rows // 2), rows // 2, 0)


    def own_spec(self, kind, shard, turn):
        columns, share, pieces = KINDS[kind]
        rows, width = shard.shape
        if columns:
            return pl.BlockSpec((rows // pieces, width), lambda *at: (turn(*at), 0))
        which = 3 if share == 2 else 4
        return pl.BlockSpec(
            (rows // (share * pieces), width), lambda *at: (at[-1][which] * pieces + turn(*at), 0)
        )

    def own_parts(self, batch, blocks, at, store, when=True):
        for (kind, shard, row, column), block in zip(batch, blocks):
            columns, share, pieces = KINDS[kind]
            if not columns:

                @pl.when(when)
                def unused(row=row, column=column, block=block):
                    store(row, column, block[...])

                continue
            for index in range(share):

                @pl.when(when & (at[3 if share == 2 else 4] == index))
                def unused(row=row, column=column, block=block, share=share, index=index):
                    edge = column
                    for part in strip_parts(block, self.strips, share, index):
                        store(row, edge, part)
                        edge += part.shape[-1]

    def first_pieces(self, batches, shapes):
        entries = [entry for batch in batches for entry in batch]

        def here(kind):
            return lambda i, at: at[1 if KINDS[kind][2] == 4 else 2]

        def kernel(at, *refs):
            ins, outs = list(refs[: len(entries)]), refs[len(entries) :]
            for batch, out in zip(batches, outs):

                def store(row, column, part, out=out):
                    out[row : row + part.shape[0], column : column + part.shape[1]] = part

                self.own_parts(batch, [ins.pop(0) for entry in batch], at, store)

        return pl.pallas_call(
            kernel,
            grid_spec=pltpu.PrefetchScalarGridSpec(
                num_scalar_prefetch=1,
                grid=(1,),
                in_specs=[self.own_spec(kind, shard, here(kind)) for kind, shard, row, column in entries],
                out_specs=[pl.BlockSpec(shape, lambda i, at: (0, 0)) for shape in shapes],
            ),
            out_shape=[jax.ShapeDtypeStruct(shape, BF16) for shape in shapes],
            compiler_params=pltpu.CompilerParams(vmem_limit_bytes=VMEM_LIMIT),
        )(self.spot, *[shard for kind, shard, row, column in entries])

    def exchange_z(self, mine):
        return lax.all_gather(mine, "shard", axis=0, tiled=False)

    def foreign(self, gathered):
        return jnp.stack([pick(gathered, self.z ^ k, 0) for k in range(1, 4)])

    def exchange_sides(self, from_z):
        return from_z, swap_row(from_z), swap_ctx(from_z)

    def corners(self, sides):
        from_z, from_y, from_x = sides
        half = from_z.shape[-1] // 2
        return from_z, from_y, from_x, from_x[..., :half], from_y[..., half:]

    def exchange_corners(self, state):
        from_z, from_y, from_x, to_y, to_x = state
        return [from_z], [from_y], [from_x], [swap_row(to_y), swap_ctx(to_x)]

    def assemble(self, batch, turns, outputs):
        pieces = len(turns)
        here = 1 if pieces == 4 else 2
        count = len(batch)
        received = [(turn, array) for turn, arrays in enumerate(turns) for array in arrays]

        def step(turn, array):
            def index(s, k, at):
                now = jnp.maximum(k, 1) - 1
                return (jnp.where(s == turn, now, jnp.where(s < turn, 0, 2)), 0, 0)

            return pl.BlockSpec((1, *array.shape[1:]), index)

        def target(s, k, at):
            return (lax.bitwise_xor(at[0], k) * pieces + lax.bitwise_xor(at[here], s), 0)

        def kernel(at, *refs):
            ins, others, outs = refs[:count], refs[count : count + len(received)], refs[count + len(received) :]
            s, k = pl.program_id(0), pl.program_id(1)

            def store(row, column, part):
                for (first, rows, left, columns), out in zip(outputs, outs):
                    top, bottom = max(first, row), min(first + rows, row + part.shape[0])
                    low, high = max(left, column), min(left + columns, column + part.shape[1])
                    if top < bottom and low < high:
                        out[top - first : bottom - first, low - left : high - left] = part[
                            top - row : bottom - row, low - column : high - column
                        ]

            self.own_parts(batch, ins, at, store, k == 0)
            for turn in range(pieces):

                @pl.when((k > 0) & (s == turn))
                def unused(turn=turn):
                    edge = 0
                    for (which, array), ref in zip(received, others):
                        if which == turn:
                            store(0, edge, ref[0])
                            edge += array.shape[2]

        return pl.pallas_call(
            kernel,
            grid_spec=pltpu.PrefetchScalarGridSpec(
                num_scalar_prefetch=1,
                grid=(pieces, 4),
                in_specs=[
                    self.own_spec(kind, shard, lambda s, k, at: lax.bitwise_xor(at[here], s))
                    for kind, shard, row, column in batch
                ]
                + [step(turn, array) for turn, array in received],
                out_specs=[pl.BlockSpec((rows, columns), target) for first, rows, left, columns in outputs],
            ),
            out_shape=[
                jax.ShapeDtypeStruct((4 * pieces * rows, columns), BF16) for first, rows, left, columns in outputs
            ],
            compiler_params=pltpu.CompilerParams(vmem_limit_bytes=VMEM_LIMIT),
            cost_estimate=pl.CostEstimate(flops=0, bytes_accessed=0, transcendentals=0),
        )(self.spot, *[shard for kind, shard, row, column in batch], *[array for turn, array in received])

    def gather_plain(self, kind, *shards):
        whole = [lax.all_gather(s, "shard", axis=0, tiled=True) for s in shards]
        parts = [self.own_columns(w) if KINDS[kind][0] else self.own_rows(w) for w in whole]
        return jnp.concatenate(parts, axis=1)


    def first_sends(self, grad):
        rows, width = grad.shape[0] // 4, grad.shape[1]
        quarter, half = rows // 4, width // 2
        pieces = grad.reshape(4, 2, 2, quarter, width)
        first, second = pieces[..., :half], pieces[..., half:]
        x, y = self.ctx, self.y
        return pick(first, x, 1), pick(second, y, 2), pick(first, 1 - x, 1), pick(second, 1 - y, 2)

    def first_swap(self, sends):
        keep_a, keep_b, send_a, send_b = sends
        return keep_a, keep_b, swap_ctx(send_a), swap_row(send_b)

    def second_swap(self, state):
        keep_a, keep_b, got_a, got_b = state
        kept_a, kept_b = plus(keep_a, got_a), plus(keep_b, got_b)
        x, y = self.ctx, self.y
        return pick(kept_a, y, 1), pick(kept_b, x, 1), swap_row(pick(kept_a, 1 - y, 1)), swap_ctx(pick(kept_b, 1 - x, 1))

    def second_sum(self, state):
        keep_a, keep_b, got_a, got_b = state
        return jnp.concatenate([plus(keep_a, got_a), plus(keep_b, got_b)], axis=-1)

    def shard_sum(self, kept):
        return lax.psum_scatter(kept, "shard", scatter_dimension=0, tiled=False)

    def packed(self, piece):
        a, b = jnp.split(piece, 2, axis=1)
        block = a.shape[1] // 2
        part, short = block // 2, piece.shape[0] // 2
        rows = [each[:, part + block :] for each in (a, b)]
        return jnp.concatenate(
            [
                jnp.concatenate([a[:, :part], b[:, :part]], axis=1),
                a[:, part : part + block],
                b[:, part : part + block],
                *[jnp.concatenate([each[:short], each[short:]], axis=1) for each in rows],
            ],
            axis=0,
        )

    def spread(self, piece):
        half = piece.shape[-1] // 2
        from_y, from_x = swap_row(piece), swap_ctx(piece)
        corner = jnp.concatenate([swap_row(from_x[..., :half]), swap_ctx(from_y[..., half:])], axis=-1)
        own = jnp.stack([piece, from_y, from_x, corner])
        return own, swap_core(own)

    def feed_gradient(self, lefts, rights, which, joined=None):
        width, columns = lefts[0].shape[1], rights[0].shape[1]
        rows, block = width // 4, columns // 2
        piece = rows // 2
        count = len(lefts)

        def kernel(*refs):
            total = tn(refs[0][...], refs[count][...])
            for i in range(1, count):
                total = total + tn(refs[i][...], refs[count + i][...])
            refs[-1][...] = total.astype(BF16).reshape(refs[-1].shape)

        into = [] if joined is None else [joined]
        return pl.pallas_call(
            kernel,
            grid=(4, 2),
            in_specs=[pl.BlockSpec((each.shape[0], rows), lambda z, j: (0, z)) for each in lefts]
            + [pl.BlockSpec((each.shape[0], block), lambda z, j: (0, j)) for each in rights]
            + [pl.BlockSpec(memory_space=pl.ANY) for each in into],
            out_specs=pl.BlockSpec((1, 2, piece, block), lambda z, j: (z, 0, which, j)),
            out_shape=jax.ShapeDtypeStruct((4, 2, 2 * piece, columns), BF16),
            input_output_aliases={2 * count: 0} if into else {},
            compiler_params=pltpu.CompilerParams(vmem_limit_bytes=VMEM_LIMIT),
        )(*lefts, *rights, *into)

    def finish_up(self, own, other):
        piece, columns = own.shape[1] // 2, own.shape[2]
        size = columns // self.strips

        def spec(x):
            return pl.BlockSpec((1, piece, columns), lambda y, at: (lax.bitwise_xor(2 * x + y, at[1]), 0, 0))

        def kernel(at, *refs):
            out_ref = refs[4]
            for mine in range(2):

                @pl.when(at[3] == mine)
                def unused(mine=mine):
                    for core in range(2):
                        for x in range(2):
                            source = refs[x] if core == mine else refs[2 + x]
                            for j in range(self.strips):
                                edge = (4 * j + 2 * core + x) * size
                                out_ref[:, edge : edge + size] = source[0, :, j * size : (j + 1) * size].astype(F32)

        return pl.pallas_call(
            kernel,
            grid_spec=pltpu.PrefetchScalarGridSpec(
                num_scalar_prefetch=1,
                grid=(2,),
                in_specs=[spec(0), spec(1)] * 2,
                out_specs=pl.BlockSpec((piece, 4 * columns), lambda y, at: (y, 0)),
            ),
            out_shape=jax.ShapeDtypeStruct((2 * piece, 4 * columns), F32),
            compiler_params=pltpu.CompilerParams(vmem_limit_bytes=VMEM_LIMIT),
        )(self.spot, own, own, other, other)

    def finish_down(self, own, other):
        piece, columns = own.shape[1] // 2, own.shape[2]

        def kernel(at, own_ref, other_ref, out_ref):
            mine = pl.program_id(0) == at[3]

            @pl.when(mine)
            def unused():
                out_ref[...] = own_ref[0].astype(F32)

            @pl.when(jnp.logical_not(mine))
            def unused():
                out_ref[...] = other_ref[0].astype(F32)

        return pl.pallas_call(
            kernel,
            grid_spec=pltpu.PrefetchScalarGridSpec(
                num_scalar_prefetch=1,
                grid=(2, 4),
                in_specs=[
                    pl.BlockSpec((1, piece, columns), lambda c, p, at: (lax.bitwise_xor(p, at[1]), 1, 0))
                ] * 2,
                out_specs=pl.BlockSpec((piece, columns), lambda c, p, at: (c * 4 + p, 0)),
            ),
            out_shape=jax.ShapeDtypeStruct((8 * piece, columns), F32),
            compiler_params=pltpu.CompilerParams(vmem_limit_bytes=VMEM_LIMIT),
        )(self.spot, own, other)

    def all_sum(self, array):
        array = lax.psum_scatter(array, "shard", scatter_dimension=0, tiled=True)
        return lax.psum(array, ("ctx", "y", "core"))

    def plain_columns(self, grad, count):
        rows, width = grad.shape
        each = width // count
        outs = []
        for i in range(count):
            whole = jnp.zeros((rows, 2 * each), BF16)
            part = grad[:, i * each : (i + 1) * each]
            whole = lax.dynamic_update_slice_in_dim(whole, part, self.core * each, 1)
            outs.append(self.all_sum(whole).astype(F32))
        return outs

    def plain_rows(self, grad):
        rows, width = grad.shape
        whole = jnp.zeros((2 * rows, width), BF16)
        whole = lax.dynamic_update_slice_in_dim(whole, grad, self.core * rows, 0)
        return self.all_sum(whole).astype(F32)

    def finish_columns(self, own, other, count):
        width = own.shape[2]
        quarter = self.quarter
        size = width // self.strips

        def spec(j):
            return pl.BlockSpec((1, quarter, width), lambda p, at: (lax.bitwise_xor(p, at[1]), j, 0))

        def kernel(at, *refs):
            outs = refs[2 * count :]
            for mine in range(2):

                @pl.when(at[3] == mine)
                def unused(mine=mine):
                    for core in range(2):
                        ins = refs[:count] if core == mine else refs[count : 2 * count]
                        for source, out in zip(ins, outs):
                            for j in range(self.strips):
                                out[:, (2 * j + core) * size : (2 * j + core + 1) * size] = source[
                                    0, :, j * size : (j + 1) * size
                                ].astype(F32)

        return pl.pallas_call(
            kernel,
            grid_spec=pltpu.PrefetchScalarGridSpec(
                num_scalar_prefetch=1,
                grid=(4,),
                in_specs=[spec(j) for j in range(count)] * 2,
                out_specs=[pl.BlockSpec((quarter, 2 * width), lambda p, at: (p, 0))] * count,
            ),
            out_shape=[jax.ShapeDtypeStruct((4 * quarter, 2 * width), F32)] * count,
            compiler_params=pltpu.CompilerParams(vmem_limit_bytes=VMEM_LIMIT),
        )(self.spot, *([own] * count), *([other] * count))

    def finish_rows(self, own, other):
        width = own.shape[2]
        short = self.quarter // 2
        first = 3 * self.quarter // short
        spec = [
            pl.BlockSpec((1, short, width), lambda c, p, at, j=j: (lax.bitwise_xor(p, at[1]), first + j, 0))
            for j in range(2)
        ]

        def kernel(at, *refs):
            out_ref = refs[4]
            mine = pl.program_id(0) == at[3]

            def put(blocks):
                for j, block in enumerate(blocks):
                    out_ref[:, j * width : (j + 1) * width] = block[0].astype(F32)

            @pl.when(mine)
            def unused():
                put(refs[:2])

            @pl.when(jnp.logical_not(mine))
            def unused():
                put(refs[2:4])

        return pl.pallas_call(
            kernel,
            grid_spec=pltpu.PrefetchScalarGridSpec(
                num_scalar_prefetch=1,
                grid=(2, 4),
                in_specs=spec + spec,
                out_specs=pl.BlockSpec((short, 2 * width), lambda c, p, at: (c * 4 + p, 0)),
            ),
            out_shape=jax.ShapeDtypeStruct((8 * short, 2 * width), F32),
            compiler_params=pltpu.CompilerParams(vmem_limit_bytes=VMEM_LIMIT),
        )(self.spot, own, own, other, other)

    def gather_norms(self, shards):
        norms = jnp.stack(shards)
        if not self.staged:
            return lax.all_gather(norms, "shard", axis=1, tiled=True).astype(F32)
        whole = jnp.zeros((4, *norms.shape), norms.dtype)
        whole = lax.dynamic_update_slice_in_dim(whole, norms[None], self.z, 0)
        for k in range(1, 4):
            whole = lax.dynamic_update_slice_in_dim(whole, xor_permute(norms, "shard", k)[None], self.z ^ k, 0)
        return jnp.moveaxis(whole, 0, 1).reshape(norms.shape[0], -1).astype(F32)

    def sum_norms(self, grads):
        share = grads.shape[1] // self.shards
        if not self.staged:
            return lax.dynamic_slice_in_dim(lax.psum(grads, EVERY), self.z * share, share, 1)
        grads = grads + swap_core(grads)
        grads = grads + swap_ctx(grads)
        grads = grads + swap_row(grads)

        def part(z):
            return lax.dynamic_slice_in_dim(grads, z * share, share, 1)

        summed = part(self.z)
        for k in range(1, 4):
            summed = summed + xor_permute(part(self.z ^ k), "shard", k)
        return summed


def beside(*batches):
    return tuple(jnp.concatenate(each, axis=-1) for each in zip(*batches))


def restack(blocks):
    def one(block):
        half = block.shape[-1] // 2
        return jnp.concatenate([block[..., :half], block[..., half:]], axis=-2)

    return tuple(map(one, blocks))


def plus(left, right):
    return (left.astype(F32) + right.astype(F32)).astype(BF16)


def layer_norm(hidden, gain, shift):
    mean = jnp.mean(hidden, axis=-1, keepdims=True)
    centred = hidden - mean
    spread = jnp.mean(centred * centred, axis=-1, keepdims=True)
    return centred * lax.rsqrt(spread + EPS) * gain + shift


def norm_backward(hidden, gain, grad):
    mean = jnp.mean(hidden, axis=-1, keepdims=True)
    centred = hidden - mean
    inverse = lax.rsqrt(jnp.mean(centred * centred, axis=-1, keepdims=True) + EPS)
    unit = centred * inverse
    scaled = grad * gain
    grad_hidden = inverse * (
        scaled - jnp.mean(scaled, axis=-1, keepdims=True) - unit * jnp.mean(scaled * unit, axis=-1, keepdims=True)
    )
    return grad_hidden, jnp.sum(grad * unit, axis=0), jnp.sum(grad, axis=0)


def gelu_parts(pre):
    phi = 0.5 + 0.5 * lax.erf(pre * (0.5 ** 0.5))
    slope = phi + pre * jnp.exp(-0.5 * pre * pre) * ((2.0 * math.pi) ** -0.5)
    return pre * phi, slope


def local(
    frames,
    text_states,
    first_gain,
    first_shift,
    self_query,
    self_key,
    self_value,
    self_output,
    second_gain,
    second_shift,
    cross_query,
    cross_key,
    cross_value,
    cross_output,
    third_gain,
    third_shift,
    up_weight,
    down_weight,
    cotangent,
):
    clips, span, width = frames.shape
    texts = text_states.shape[1]
    rows = clips * span
    place = Place(width)
    position = place.ctx.astype(jnp.int32).reshape(1)
    half = width // 2
    pairs = half // (2 * HD)
    staged = place.staged

    norms = place.gather_norms([first_gain, first_shift, second_gain, second_shift, third_gain, third_shift])
    gain_one, shift_one, gain_two, shift_two, gain_three, shift_three = (norms[i] for i in range(6))
    cotangent_own = cotangent.reshape(rows, width)
    frames_own = frames.reshape(rows, width)
    if staged:
        quarter, short, wide = width // 16, half // 16, width // 8
        inputs = [("columns", self_query, 0, 0), ("columns", self_key, 0, half), ("columns", self_value, 0, width)]
        others = [
            ("rows", self_output, 0, 0),
            ("rows", cross_output, short, 0),
            ("columns", cross_query, 0, width),
            ("columns", cross_key, 0, width + half),
            ("columns", cross_value, 0, 2 * width),
        ]
        hidden = up_weight.shape[1] // 4
        feed = [("feed_columns", up_weight, 0, 0), ("feed_rows", down_weight, 0, hidden)]
        in_piece, other_piece, feed_piece = place.first_pieces(
            [inputs, others, feed],
            [(quarter, width + half), (quarter, 2 * width + half), (wide, hidden + width)],
        )
        in_piece = place.exchange_z(in_piece)
        frames_before = shifted(frames_own, "ctx", 1)
        frames_near = both(frames_own)
        cotangent_far = swap_ctx(cotangent_own)
        in_piece, other_piece, frames_before, frames_near = tied(
            place.foreign(in_piece), other_piece, frames_before, frames_near
        )
        in_piece, other_piece, frames_before = (
            place.exchange_sides(in_piece),
            place.exchange_z(other_piece),
            both(frames_before),
        )
        in_piece, frames_before = tied(place.corners(in_piece), frames_before)
        in_piece = place.exchange_corners(in_piece)
        frames_all = jnp.concatenate([frames_before, frames_near], axis=0)
        normed_one = layer_norm(frames_all.astype(F32), gain_one, shift_one).astype(BF16)
        in_piece, other_piece, feed_piece, normed_one, cotangent_far = tied(
            in_piece, place.foreign(other_piece), feed_piece, normed_one, cotangent_far
        )
        other_piece = place.exchange_sides(other_piece)
        w_feed = lax.all_gather(feed_piece, FEED, axis=0, tiled=True)
        w_query, w_key_value = place.assemble(
            inputs, in_piece, [(0, quarter, 0, half), (0, quarter, half, width)]
        )
    else:
        w_query = place.gather_plain("columns", self_query)
        w_key_value = place.gather_plain("columns", self_key, self_value)
        w_out = place.gather_plain("rows", self_output)
        w_cross_query = place.gather_plain("columns", cross_query)
        w_cross_kv = place.gather_plain("columns", cross_key, cross_value)
        w_cross_out = place.gather_plain("rows", cross_output)
        w_up = place.gather_plain("columns", up_weight)
        w_down = place.gather_plain("rows", down_weight)
        frames_all = jnp.concatenate([both(shifted(frames_own, "ctx", 1)), both(frames_own)], axis=0)
        normed_one = layer_norm(frames_all.astype(F32), gain_one, shift_one).astype(BF16)

    normed_here = normed_one[2 * rows :]
    queries = product(normed_here, w_query).astype(BF16).reshape(2 * clips, span, half)
    key_values = product(normed_one, w_key_value).astype(BF16).reshape(2, 2 * clips, span, width)
    attended, logs = attend(position, queries, key_values, key_values, 0, pairs, True)
    attended = attended.reshape(2 * rows, half)
    if staged:
        other_piece, attended = tied(place.corners(other_piece), attended)
        other_piece = place.exchange_corners(other_piece)
        w_out, w_cross_out, w_cross_query, w_cross_kv = place.assemble(
            others,
            other_piece,
            [(0, short, 0, width), (short, short, 0, width), (0, quarter, width, half), (0, quarter, width + half, width)],
        )
    hidden_zero = frames_own.astype(F32)
    hidden_one = hidden_zero + pair_sum(attended, w_out, product)

    normed_two = both(layer_norm(hidden_one, gain_two, shift_two).astype(BF16))
    text = both(text_states.reshape(clips * texts, width))
    cross_q = product(normed_two, w_cross_query).astype(BF16).reshape(2 * clips, span, half)
    cross_kv = product(text, w_cross_kv).astype(BF16).reshape(1, 2 * clips, texts, width)
    cross_att, cross_logs = attend(position, cross_q, cross_kv, cross_kv, 0, pairs, False)
    cross_att = cross_att.reshape(2 * rows, half)
    hidden_two = hidden_one + pair_sum(cross_att, w_cross_out, product)

    if staged:
        w_feed, hidden_two = tied(w_feed, hidden_two)
        w_up, w_down = w_feed[:, :hidden], w_feed[:, hidden:]
    normed_own = layer_norm(hidden_two, gain_three, shift_three).astype(BF16)
    normed_three = [both(normed_own)]
    grad_branch = [both(cotangent_own)]
    if staged:
        normed_three.append(both(swap_ctx(normed_own)))
        grad_branch.append(both(cotangent_far))
    activated, grad_pre = [], []
    for normed, grad in zip(normed_three, grad_branch):
        act, slope = gelu_parts(product(normed, w_up))
        activated.append(act.astype(BF16))
        grad_pre.append((against(grad, w_down) * slope).astype(BF16))
    if staged:
        far, near = QuadSum(*grad_pre, w_up, against).cores()
        far, activated, normed_three, grad_branch, grad_pre = tied(far, activated, normed_three, grad_branch, grad_pre)
        across = swap_ctx(far)
        feed = place.feed_gradient(activated, grad_branch, 1)
        feed = place.feed_gradient(normed_three, grad_pre, 0, feed)
        feed, near = tied(feed, near)
        feed = lax.psum_scatter(feed.reshape(-1, width), FEED, scatter_dimension=0, tiled=True)
        grad_normed = near + across.astype(F32)
        mixed = QuadSum(*activated, w_down, product)
    else:
        grad_down = over_rows(activated[0], grad_branch[0]).astype(BF16)
        grad_up = over_rows(normed_three[0], grad_pre[0]).astype(BF16)
        grad_normed = pair_sum(grad_pre[0], w_up, against)
    grad_hid, grad_gain_three, grad_shift_three = norm_backward(hidden_two, gain_three, grad_normed)
    grad_res = cotangent_own.astype(F32) + grad_hid

    grad_branch = both(grad_res.astype(BF16))
    grad_cross_out = over_rows(cross_att, grad_branch).astype(BF16)
    grad_catt = against(grad_branch, w_cross_out).astype(BF16).reshape(2 * clips, span, half)
    grad_cq, part_ck, part_cv = attend_back(
        position, cross_q, cross_kv, cross_kv, cross_att.reshape(2 * clips, span, half), grad_catt, cross_logs, 0, pairs, False
    )
    grad_cq = grad_cq.reshape(2 * rows, half)
    part = jnp.concatenate([part_ck, part_cv], axis=-1).reshape(2 * clips, texts, width)
    grad_ckv = (part.astype(F32) + swap_ctx(part).astype(F32)).astype(BF16)
    share = texts // lax.axis_size("ctx")
    start = place.ctx * share

    def part_rows(array):
        array = array.reshape(2 * clips, texts, width)
        return lax.dynamic_slice_in_dim(array, start, share, 1).reshape(2 * clips * share, width)

    grad_cross_kv = over_rows(part_rows(text), part_rows(grad_ckv)).astype(BF16)
    grad_cross_query = over_rows(normed_two, grad_cq).astype(BF16)
    if staged:
        early = beside(
            place.first_sends(grad_cross_query),
            place.first_sends(grad_cross_kv),
            restack(place.first_sends(grad_cross_out)),
        )
        early, grad_cq = tied(early, grad_cq)
        early = place.first_swap(early)
    grad_hid, grad_gain_two, grad_shift_two = norm_backward(
        hidden_one, gain_two, pair_sum(grad_cq, w_cross_query, against)
    )
    grad_res = grad_res + grad_hid

    grad_branch = both(grad_res.astype(BF16))
    grad_out = over_rows(attended, grad_branch).astype(BF16)
    grad_att = against(grad_branch, w_out).astype(BF16).reshape(2 * clips, span, half)
    if staged:
        early, grad_att, mixed.parts = tied(early, grad_att, mixed.parts)
        early = place.second_swap(early)
        mixed_far, mixed_near = mixed.cores()
        mixed = mixed_near + swap_ctx(mixed_far).astype(F32)
    grad_q, grad_k, grad_v = attend_back(
        position,
        queries,
        key_values,
        key_values,
        attended.reshape(2 * clips, span, half),
        grad_att,
        logs,
        0,
        pairs,
        True,
    )
    grad_q = grad_q.reshape(2 * rows, half)
    grad_k = grad_k.reshape(4 * rows, half)
    grad_v = grad_v.reshape(4 * rows, half)
    grad_kv = jnp.concatenate([grad_k, grad_v], axis=1)
    grad_key_value = over_rows(normed_one, grad_kv).astype(BF16)
    grad_query = over_rows(normed_here, grad_q).astype(BF16)
    if staged:
        late = beside(
            place.first_sends(grad_query), place.first_sends(grad_key_value), restack(place.first_sends(grad_out))
        )
        late, grad_q, grad_kv = tied(late, grad_q, grad_kv)
        late = place.first_swap(late)
    grad_normed_before = pair_sum(grad_kv[: 2 * rows], w_key_value, against)
    returned = shifted(grad_normed_before.astype(BF16), "ctx", -1)
    grad_normed = pair_sum(grad_q, w_query, against) + pair_sum(grad_kv[2 * rows :], w_key_value, against)
    if staged:
        early, late, feed, grad_normed = tied(place.second_sum(early), late, feed, grad_normed)
        early, late = place.shard_sum(early), place.second_swap(late)
    grad_text = pair_sum(grad_ckv.reshape(2 * clips * texts, width), w_cross_kv, against).reshape(clips, texts, width)
    mixed = hidden_two + (mixed if staged else pair_sum(activated[0], w_down, product))
    mixed = mixed.astype(BF16).reshape(clips, span, width)
    if staged:
        early, late, mixed, grad_text, feed = tied(early, place.second_sum(late), mixed, grad_text, feed)
        late, early, feed = place.shard_sum(late), place.spread(place.packed(early)), place.spread(feed)
    grad_hid, grad_gain_one, grad_shift_one = norm_backward(
        hidden_zero, gain_one, grad_normed + returned.astype(F32)
    )
    grad_frames = (grad_res + grad_hid).reshape(clips, span, width)

    small = jnp.stack(
        [grad_gain_one, grad_shift_one, grad_gain_two, grad_shift_two, grad_gain_three, grad_shift_three]
    )
    small = place.sum_norms(small)
    if staged:
        own, other = early
        total_cross_query, total_cross_key, total_cross_value = place.finish_columns(own, other, 3)
        total_cross_out = place.finish_rows(own, other)
        late, total_cross_query, total_cross_out = tied(late, total_cross_query, total_cross_out)
        late = place.spread(place.packed(late))
        total_up, total_down = place.finish_up(*feed), place.finish_down(*feed)
        late, total_up, total_down = tied(late, total_up, total_down)
        own, other = late
        total_query, total_key, total_value = place.finish_columns(own, other, 3)
        total_out = place.finish_rows(own, other)
    else:
        total_cross_out, total_out, total_down = map(place.plain_rows, (grad_cross_out, grad_out, grad_down))
        total_cross_key, total_cross_value = place.plain_columns(grad_cross_kv, 2)
        total_key, total_value = place.plain_columns(grad_key_value, 2)
        (total_cross_query,) = place.plain_columns(grad_cross_query, 1)
        (total_query,) = place.plain_columns(grad_query, 1)
        (total_up,) = place.plain_columns(grad_up, 1)
    return (
        mixed,
        grad_frames,
        grad_text,
        small[0],
        small[1],
        total_query,
        total_key,
        total_value,
        total_out,
        small[2],
        small[3],
        total_cross_query,
        total_cross_key,
        total_cross_value,
        total_cross_out,
        small[4],
        small[5],
        total_up,
        total_down,
    )


def solution(mesh):
    ctx, shard, rep = mesh.devices.shape
    mesh = jax.sharding.Mesh(mesh.devices.reshape(ctx, shard, rep // 2, 2), ("ctx", "shard", "y", "core"))
    clips = ("shard", "y", "core")
    rows = P(clips, "ctx", None)
    texts = P(clips, None, None)
    vector = P("shard")
    weight = P("shard", None)
    block = (vector, vector, weight, weight, weight, weight)
    in_specs = (rows, texts, *block, *block, vector, vector, weight, weight, rows)
    out_specs = (rows, rows, texts, *block, *block, vector, vector, weight, weight)
    return jax.shard_map(local, mesh=mesh, in_specs=in_specs, out_specs=out_specs, check_vma=False)
```

time: 1520 us -> 1050 us (0.69)
  waiting for transfers between devices: 670 us -> 432 us
  starting transfers between devices: 205 us -> 56.1 us
  blocking collectives: 53.2 us -> 0 us
  matrix products: 247 us -> 204 us
  local copies, waits for them, and re-layouts: 83.7 us -> 47.7 us
  Pallas kernels: 169 us -> 194 us
  other arithmetic: 69.6 us -> 91.9 us
    ppermute x116 -> x64, waiting for transfers between devices: 661 us -> 388 us  [xor_permute(): lax.ppermute(array, axis, [(i, i ^ bit) for i in range(lax.axis_size(axis...]
    ppermute x116 -> x64, starting transfers between devices: 196 us -> 47.8 us  [xor_permute(): lax.ppermute(array, axis, [(i, i ^ bit) for i in range(lax.axis_size(axis...]
    pallas_call x8, Pallas kernels: 24.2 us -> 70.3 us  [the longest x2 34.4 us: feed_gradient(): pl.pallas_call(kernel, grid=(4, 2), in_specs=[pl.BlockSpec((each.shape[0]...]
    all_gather x8 -> x3, waiting for transfers between devices: 0.03 us -> 43.6 us  [the longest x2 43.6 us: exchange_z(): return lax.all_gather(mine, 'shard', axis=0, tiled=False)]
    psum x1 -> x0, blocking collectives: 39.5 us -> none  [local(): small = lax.psum(small, EVERY)]
    dot_general x8 -> x6, matrix products: 59.7 us -> 27.2 us  [over_rows(): lax.dot_general(left, right, (((0,), (0,)), ((), ())), preferred_element_...]
    concatenate x0 -> x15, other arithmetic: none -> 23.3 us  [the longest x8 11.8 us: beside(): return tuple((jnp.concatenate(each, axis=-1) for each in zip(*batches)))]
    pallas_call x6 -> x2, Pallas kernels: 50.9 us -> 28.3 us  [assemble(): pl.pallas_call(kernel, grid_spec=pltpu.PrefetchScalarGridSpec(num_scalar_...]
  transfers between devices with their start and end apart: 126 -> 72, of which waited for: 56 -> 35; matrix products, arithmetic and copies ran while one was open for 18% -> 25% of each run, Pallas kernels for 7% -> 16%
where the time goes in v2:
time: 1050 us; the launch traced here: 1040 us
  waiting for transfers between devices  432 us (41%)
  matrix products  204 us (19%)
  Pallas kernels  194 us (18%)
  other arithmetic  91.9 us (9%)
  starting transfers between devices  56.1 us (5%)
  local copies, waits for them, and re-layouts  47.7 us (5%)
  between operations  16.7 us (2%)
    ppermute x64, waiting for transfers between devices, xor_permute(): lax.ppermute(array, axis, [(i, i ^ bit) for i in range(lax.axis_size(axis...  388 us
    dot_general x18, matrix products, against(): lax.dot_general(left, right, (((1,), (1,)), ((), ())), preferred_element_...  100 us
    dot_general x14, matrix products, product(): return jnp.dot(left, right, preferred_element_type=F32)  76.4 us
    pallas_call x2, Pallas kernels, attend_back(): pl.pallas_call(lambda *refs: attend_back_kernel(causal, *refs), grid=(cli...  50.2 us
    ppermute x64, starting transfers between devices, xor_permute(): lax.ppermute(array, axis, [(i, i ^ bit) for i in range(lax.axis_size(axis...  47.8 us
    all_gather x2, waiting for transfers between devices, exchange_z(): return lax.all_gather(mine, 'shard', axis=0, tiled=False)  43.6 us
    pallas_call x2, Pallas kernels, attend(): pl.pallas_call(lambda *refs: attend_kernel(causal, *refs), grid=(clips, p...  41.1 us
    pallas_call x2, Pallas kernels, feed_gradient(): pl.pallas_call(kernel, grid=(4, 2), in_specs=[pl.BlockSpec((each.shape[0]...  34.4 us
  transfers between devices with their start and end apart: 72, of which 35 were waited for; matrix products, arithmetic and copies ran while one was open for 25% of the time, Pallas kernels for 16%

profile of v2, /device:TPU:0, one launch (start us, length us, event | category | flops | bytes accessed | tf_op | source)
XLA Modules:
  0.0 1042.1 jit_solution(13270243457543620743)
XLA Ops:
  11.1 4.4 shard_map.330
  17.2 5.6 collective-permute-start
  26.1 33.7 %all-gather.8.cloned.1.call-done = bf16[384,2304]{1,0:T(8,128)(2,1)} async-done(((bf16[96,2304]{1,0:T(8,128)(2,1)}), bf16[384,2304]{1,0:T(8,128)(2,1)}) %all-gather.8.cloned.1.call-update) | async-done | bytes 1769488 | tf_op jit(solution)/shard_map/all_gather | solution.py:354
  70.7 4.7 collective-permute-done.8
  76.1 17.3 %collective-permute-done.3.refs_5_ = bf16[3,96,2304]{2,1,0:T(8,128)(2,1)S(1)} collective-permute-done((bf16[3,96,2304]{2,1,0:T(8,128)(2,1)S(1)}, bf16[3,96,2304]{2,1,0:T(8,128)(2,1)S(1)}, u32[]{:S(2)}, u32[]{:S(2)}) %collective-permute-start.3) | collective-permute-done | bytes 1327136 | tf_op jit(solution)/shard_map/ppermute | solution.py:34
  105.4 5.8 fusion.5
  111.2 10.0 all-gather.10.cloned.1.call-done
  127.3 13.8 %collective-permute-done.6.refs_7_ = bf16[3,96,1152]{2,1,0:T(8,128)(2,1)} collective-permute-done((bf16[3,96,1152]{2,1,0:T(8,128)(2,1)}, bf16[3,96,1152]{2,1,0:T(8,128)(2,1)}, u32[]{:S(2)}, u32[]{:S(2)}) %collective-permute-start.6) | collective-permute-done | bytes 663584 | tf_op jit(solution)/shard_map/ppermute | solution.py:34
  146.9 12.3 %shard_map.331 = (bf16[1536,768]{1,0:T(8,128)(2,1)}, bf16[1536,1536]{1,0:T(8,128)(2,1)}) custom-call(s32[5]{0:T(128)S(1)} %stack.122.at, bf16[384,1536]{1,0:T(8,128)(2,1)S(1)} %copy-done.3, bf16[384,1536]{1,0:T(8,128)(2,1)S(1)} %copy-done.5, bf16[384,1536]{1,0:T(8,128)(2,1)S(1)} %copy-done.7, bf16[3,96,2304]{2,1,0:T(8,128)(2,1)S(1)} %pad_maximum_fusion.29.refs_3_, ...), custom_call_target="tpu_custom_call" | custom-call | tf_op jit(solution)/shard_map/pallas_call | solution.py:411
  159.2 4.4 fusion.75
  163.6 11.8 %convolution_convert_fusion = bf16[2048,1536]{1,0:T(8,128)(2,1)} fusion(bf16[2048,1536]{1,0:T(8,128)(2,1)S(1)} %copy-done.40, bf16[1536,1536]{1,0:T(8,128)(2,1)S(1)} %copy-done.86), kind=kOutput, calls=%fused_computation.11 | convolution fusion | flops 9666822144 | bytes 17301504 | tf_op jit(solution)/shard_map/dot_general | solution.py:22
  175.4 31.6 %shard_map.332 = (bf16[2,512,768]{2,1,0:T(8,128)(2,1)S(1)}, f32[2,6,2,512]{3,2,1,0:T(2,128)S(1)}) custom-call(s32[1]{0:T(128)} %bitcast.14.refs_0_, bf16[2,512,768]{2,1,0:T(8,128)(2,1)S(1)} %bitcast.217, bf16[2,2,512,1536]{3,2,1,0:T(8,128)(2,1)} %bitcast.229, bf16[2,2,512,1536]{3,2,1,0:T(8,128)(2,1)} %bitcast.230), custom_call_target="tpu_custom_call" | custom-call | tf_op jit(solution)/shard_map/pallas_call | solution.py:200
  213.5 47.9 %collective-permute-done.13.refs_8_ = bf16[3,96,1920]{2,1,0:T(8,128)(2,1)S(1)} collective-permute-done((bf16[3,96,1920]{2,1,0:T(8,128)(2,1)S(1)}, bf16[3,96,1920]{2,1,0:T(8,128)(2,1)S(1)}, u32[]{:S(2)}, u32[]{:S(2)}) %collective-permute-start.13) | collective-permute-done | bytes 1105952 | tf_op jit(solution)/shard_map/ppermute | solution.py:34
  261.5 16.0 %shard_map.333 = (bf16[768,1536]{1,0:T(8,128)(2,1)}, bf16[768,1536]{1,0:T(8,128)(2,1)}, bf16[1536,768]{1,0:T(8,128)(2,1)}, bf16[1536,1536]{1,0:T(8,128)(2,1)}) custom-call(s32[5]{0:T(128)S(1)} %stack.122.at, bf16[384,1536]{1,0:T(8,128)(2,1)S(1)} %copy-done.8, bf16[384,1536]{1,0:T(8,128)(2,1)S(1)} %copy-done.9, bf16[384,1536]{1,0:T(8,128)(2,1)S(1)} %copy-done.10, ...), custom_call_target="tpu_custom_call" | custom-call | tf_op jit(solution)/shard_map/pallas_call | solution.py:411
  277.5 4.3 convolution_convert_fusion.15
  285.6 3.8 fusion.139
  298.2 9.5 shard_map.334
  314.0 6.1 fusion.23
  330.7 32.5 %collective-permute-done.20 = bf16[512,1536]{1,0:T(8,128)(2,1)S(1)} collective-permute-done((bf16[512,1536]{1,0:T(8,128)(2,1)S(1)}, bf16[512,1536]{1,0:T(8,128)(2,1)S(1)}, u32[]{:S(2)}, u32[]{:S(2)}) %collective-permute-start.20) | collective-permute-done | bytes 1572896 | tf_op jit(solution)/shard_map/ppermute | solution.py:34
  363.3 9.3 multiply_convert_fusion.1
  373.8 9.9 fusion.17.refs_2_
  383.7 6.1 convolution_convert_fusion.12
  390.0 10.4 %multiply_convert_fusion = (bf16[1024,1536]{1,0:T(8,128)(2,1)}, f32[1024,1536]{1,0:T(8,128)}) fusion(bf16[1024,1536]{1,0:T(8,128)(2,1)S(1)} %constant_dynamic-update-slice_fusion.2.refs_1_, bf16[1536,3072]{1,0:T(8,128)(2,1)} %all-gather.6.cloned.1.call-done), kind=kOutput, calls=%fused_computation.27 | convolution fusion | flops 4839702528 | bytes 17301504 | tf_op jit(solution)/shard_map/dot_general | solution.py:22
  400.4 9.1 fusion.11.refs_3_
  409.5 6.1 convolution_convert_fusion.13
  422.6 7.2 fusion.35
  430.3 17.2 %shard_map.335.refs_4_ = bf16[4,2,384,1536]{3,2,1,0:T(8,128)(2,1)} custom-call(bf16[1024,1536]{1,0:T(8,128)(2,1)S(1)} %get-tuple-element.162.refs_0_, bf16[1024,1536]{1,0:T(8,128)(2,1)} %get-tuple-element.163.refs_1_, bf16[1024,1536]{1,0:T(8,128)(2,1)} %pad_maximum_fusion.6.refs_2_, bf16[1024,1536]{1,0:T(8,128)(2,1)} %copy-done.38), custom_call_target="tpu_custom_call" | custom-call | tf_op jit(solution)/shard_map/pallas_call | solution.py:496
  447.5 17.2 %shard_map.336 = bf16[4,2,384,1536]{3,2,1,0:T(8,128)(2,1)} custom-call(bf16[1024,1536]{1,0:T(8,128)(2,1)S(1)} %pad_maximum_fusion.7.refs_0_, bf16[1024,1536]{1,0:T(8,128)(2,1)} %copy-done.39, bf16[1024,1536]{1,0:T(8,128)(2,1)} %copy-done.49, bf16[1024,1536]{1,0:T(8,128)(2,1)} %copy-done.50, ...), custom_call_target="tpu_custom_call", output_to_operand_aliasing={{}: (4, {})} | custom-call | tf_op jit(solution)/shard_map/pallas_call | solution.py:496
  464.6 6.4 slice_add_fusion.2
  479.8 6.4 fusion.73
  486.2 13.9 %shard_map.337 = (bf16[2,512,768]{2,1,0:T(8,128)(2,1)S(1)}, bf16[1,2,64,768]{3,2,1,0:T(8,128)(2,1)S(1)}, bf16[1,2,64,768]{3,2,1,0:T(8,128)(2,1)S(1)}) custom-call(s32[1]{0:T(128)} %bitcast.14.refs_0_, bf16[2,512,768]{2,1,0:T(8,128)(2,1)S(1)} %bitcast.216, bf16[1,2,64,1536]{3,2,1,0:T(8,128)(2,1)S(1)} %bitcast.213, bf16[1,2,64,1536]{3,2,1,0:T(8,128)(2,1)S(1)} %bitcast.214, ...), custom_call_target="tpu_custom_call" | custom-call | tf_op jit(solution)/shard_map/pallas_call | solution.py:229
  503.7 4.8 convolution_convert_fusion.4
  511.6 8.6 collective-permute-done.27
  537.7 5.4 convolution_convert_fusion.10
  543.2 6.9 fusion.61
  557.5 4.4 fusion.63
  571.5 4.3 convolution_convert_fusion.2
  579.6 5.4 fusion.74
  585.0 32.2 %collective-permute-done.28 = bf16[4,2,96,1536]{3,2,0,1:T(8,128)(2,1)S(1)} collective-permute-done((bf16[4,2,96,1536]{3,2,0,1:T(8,128)(2,1)S(1)}, bf16[4,2,96,1536]{3,2,0,1:T(8,128)(2,1)S(1)}, u32[]{:S(2)}, u32[]{:S(2)}) %collective-permute-start.28) | collective-permute-done | bytes 2359328 | tf_op jit(solution)/shard_map/ppermute | solution.py:34
  617.2 26.7 %collective-permute-done.29 = bf16[4,2,96,1536]{3,2,0,1:T(8,128)(2,1)S(1)} collective-permute-done((bf16[4,2,96,1536]{3,2,0,1:T(8,128)(2,1)S(1)}, bf16[4,2,96,1536]{3,2,0,1:T(8,128)(2,1)S(1)}, u32[]{:S(2)}, u32[]{:S(2)}) %collective-permute-start.29) | collective-permute-done | bytes 2359328 | tf_op jit(solution)/shard_map/ppermute | solution.py:34
  650.1 36.3 %shard_map.338 = (bf16[2,512,768]{2,1,0:T(8,128)(2,1)S(1)}, bf16[2,2,512,768]{3,2,1,0:T(8,128)(2,1)}, bf16[2,2,512,768]{3,2,1,0:T(8,128)(2,1)}) custom-call(s32[1]{0:T(128)} %bitcast.14.refs_0_, bf16[2,512,768]{2,1,0:T(8,128)(2,1)S(1)} %bitcast.218, bf16[2,2,512,1536]{3,2,1,0:T(8,128)(2,1)} %bitcast.231, bf16[2,2,512,1536]{3,2,1,0:T(8,128)(2,1)} %bitcast.232, ...), custom_call_target="tpu_custom_call" | custom-call | tf_op jit(solution)/shard_map/pallas_call | solution.py:229
  691.6 10.9 %convolution_convert_fusion.1 = bf16[1536,1536]{1,0:T(8,128)(2,1)S(1)} fusion(bf16[2048,1536]{1,0:T(8,128)(2,1)S(1)} %bitcast.243, bf16[2048,768]{1,0:T(8,128)(2,1)} %bitcast.259, bf16[2048,768]{1,0:T(8,128)(2,1)S(1)} %bitcast.258), kind=kOutput, calls=%fused_computation.12 | convolution fusion | flops 9678618624 | bytes 17301504 | tf_op jit(solution)/shard_map/dot_general | solution.py:26
  711.7 5.9 pad_maximum_fusion.1
  717.6 6.8 convolution_convert_fusion.7
  736.8 9.0 add_add_fusion
  745.9 5.5 convert_element_type.327
  751.3 33.2 %collective-permute-done.34 = bf16[4,2,96,1536]{3,2,0,1:T(8,128)(2,1)} collective-permute-done((bf16[4,2,96,1536]{3,2,0,1:T(8,128)(2,1)}, bf16[4,2,96,1536]{3,2,0,1:T(8,128)(2,1)}, u32[]{:S(2)}, u32[]{:S(2)}) %collective-permute-start.34) | collective-permute-done | bytes 2359328 | tf_op jit(solution)/shard_map/ppermute | solution.py:34
  797.2 29.3 %collective-permute-done.41 = bf16[512,1536]{1,0:T(8,128)(2,1)S(1)} collective-permute-done((bf16[512,1536]{1,0:T(8,128)(2,1)S(1)}, bf16[512,1536]{1,0:T(8,128)(2,1)S(1)}, u32[]{:S(2)}, u32[]{:S(2)}) %collective-permute-start.41) | collective-permute-done | bytes 1572896 | tf_op jit(solution)/shard_map/ppermute | solution.py:34
  829.2 20.9 %collective-permute-done.39 = bf16[4,96,1536]{2,1,0:T(8,128)(2,1)S(1)} collective-permute-done((bf16[4,96,1536]{2,1,0:T(8,128)(2,1)S(1)}, bf16[4,96,1536]{2,1,0:T(8,128)(2,1)S(1)}, u32[]{:S(2)}, u32[]{:S(2)}) %collective-permute-start.39) | collective-permute-done | bytes 1179680 | tf_op jit(solution)/shard_map/ppermute | solution.py:34
  855.7 12.3 %collective-permute-done.52 = bf16[384,768]{1,0:T(8,128)(2,1)S(1)} collective-permute-done((bf16[384,768]{1,0:T(8,128)(2,1)S(1)}, bf16[384,768]{1,0:T(8,128)(2,1)S(1)}, u32[]{:S(2)}, u32[]{:S(2)}) %collective-permute-start.52) | collective-permute-done | bytes 589856 | tf_op jit(solution)/shard_map/ppermute | solution.py:34
  872.3 5.8 collective-permute-done.53
  879.5 20.9 %collective-permute-done.62 = bf16[384,1536]{1,0:T(8,128)(2,1)S(1)} collective-permute-done((bf16[384,1536]{1,0:T(8,128)(2,1)S(1)}, bf16[384,1536]{1,0:T(8,128)(2,1)S(1)}, u32[]{:S(2)}, u32[]{:S(2)}) %collective-permute-start.62) | collective-permute-done | bytes 1179680 | tf_op jit(solution)/shard_map/ppermute | solution.py:34
  903.6 6.6 convolution_convert_fusion.6
  919.8 4.0 shard_map.339
  929.5 5.5 add_convert_fusion.4
  936.9 6.9 collective-permute-done.57
  946.1 6.1 collective-permute-done.58
  952.1 31.3 %collective-permute-done.59 = bf16[384,384]{1,0:T(8,128)(2,1)S(1)} collective-permute-done((bf16[384,384]{1,0:T(8,128)(2,1)S(1)}, bf16[384,384]{1,0:T(8,128)(2,1)S(1)}, u32[]{:S(2)}, u32[]{:S(2)}) %collective-permute-start.59) | collective-permute-done | bytes 294944 | tf_op jit(solution)/shard_map/ppermute | solution.py:34
  988.5 4.1 collective-permute-done.46
  1000.3 5.5 fusion.28
  1006.5 10.0 shard_map.342
  1016.5 6.2 shard_map.341
  1022.7 6.1 shard_map.344
  1028.9 5.9 shard_map.343
  (544 shorter events, 237.1 us)
Async XLA Ops:
  7.2 52.6 %all-gather.8.cloned.1.call-start = ((), (), s32[]{:S(2)}) async-start(), calls=%async_computation.7 | async-start | bytes 2211840 | tf_op jit(solution)/shard_map/all_gather | solution.py:354
  16.6 104.6 %all-gather.10.cloned.1.call-start = ((), (), s32[]{:S(2)}) async-start(), calls=%async_computation.8 | async-start | bytes 3686400 | tf_op jit(solution)/shard_map/all_gather | solution.py:354
  16.7 6.1 collective-permute-start.1
  17.2 44.1 %collective-permute-start = (bf16[512,1536]{1,0:T(8,128)(2,1)S(1)}, bf16[512,1536]{1,0:T(8,128)(2,1)}, u32[]{:S(2)}, u32[]{:S(2)}) collective-permute-start(bf16[512,1536]{1,0:T(8,128)(2,1)S(1)} %bitcast.237), channel_id=1, source_target_pairs={{0,16},{1,17},{2,18},{3,19},{4,20},{5,21},{6,22},{7,23},{8,24},{9,... | collective-permute-start | bytes 4718600 | tf_op jit(solution)/shard_map/ppermute | solution.py:56
  61.3 258.7 %all-gather.6.cloned.1.call-start = ((), (), s32[]{:S(2)}) async-start(), calls=%async_computation.3 | async-start | bytes 10616832 | tf_op jit(solution)/shard_map/all_gather | solution.py:798
  61.4 35.0 %collective-permute-start.4 = (bf16[512,1536]{1,0:T(8,128)(2,1)}, bf16[512,1536]{1,0:T(8,128)(2,1)}, u32[]{:S(2)}, u32[]{:S(2)}) collective-permute-start(bf16[512,1536]{1,0:T(8,128)(2,1)} %collective-permute-done), channel_id=1, source_target_pairs={{0,1},{1,0},{2,3},{3,2},{4,5},{5,4},{6,7},{7,6},{8,9},{9,8},{10,11... | collective-permute-start | bytes 4718600 | tf_op jit(solution)/shard_map/ppermute | solution.py:34
  61.5 32.0 %collective-permute-start.3 = (bf16[3,96,2304]{2,1,0:T(8,128)(2,1)S(1)}, bf16[3,96,2304]{2,1,0:T(8,128)(2,1)S(1)}, u32[]{:S(2)}, u32[]{:S(2)}) collective-permute-start(bf16[3,96,2304]{2,1,0:T(8,128)(2,1)S(1)} %pad_maximum_fusion.29.refs_3_), channel_id=1, source_target_pairs={{0,16},{16,0},{1,17},{17,1},{2,18},{18,2},{3,19},{19,3},{4,20},{20... | collective-permute-start | bytes 3981320 | tf_op jit(solution)/shard_map/ppermute | solution.py:34
  63.0 31.4 %collective-permute-start.2 = (bf16[3,96,2304]{2,1,0:T(8,128)(2,1)S(1)}, bf16[3,96,2304]{2,1,0:T(8,128)(2,1)}, u32[]{:S(2)}, u32[]{:S(2)}) collective-permute-start(bf16[3,96,2304]{2,1,0:T(8,128)(2,1)S(1)} %pad_maximum_fusion.29.refs_3_), channel_id=1, source_target_pairs={{0,2},{2,0},{1,3},{3,1},{4,6},{6,4},{5,7},{7,5},{8,10},{10,8},{9,1... | collective-permute-start | bytes 3981320 | tf_op jit(solution)/shard_map/ppermute | solution.py:34
  64.6 10.8 %collective-permute-start.9 = (bf16[6,384]{1,0:T(8,128)(2,1)S(1)}, bf16[6,384]{1,0:T(8,128)(2,1)S(1)}, u32[]{:S(2)}, u32[]{:S(2)}) collective-permute-start(bf16[6,384]{1,0:T(8,128)(2,1)S(1)} %stack.131), channel_id=1, source_target_pairs={{0,12},{4,8},{8,4},{12,0},{1,13},{5,9},{9,5},{13,1},{2,14},{6,10},... | collective-permute-start | bytes 13832 | tf_op jit(solution)/shard_map/ppermute | solution.py:34
  69.5 5.9 collective-permute-start.8
  75.4 51.9 %collective-permute-start.10 = (bf16[512,1536]{1,0:T(8,128)(2,1)}, bf16[512,1536]{1,0:T(8,128)(2,1)}, u32[]{:S(2)}, u32[]{:S(2)}) collective-permute-start(bf16[512,1536]{1,0:T(8,128)(2,1)} %bitcast.244), channel_id=1, source_target_pairs={{0,16},{16,0},{1,17},{17,1},{2,18},{18,2},{3,19},{19,3},{4,20},{20... | collective-permute-start | bytes 4718600 | tf_op jit(solution)/shard_map/ppermute | solution.py:34
  98.7 28.6 %collective-permute-start.5 = (bf16[3,96,1152]{2,1,0:T(8,128)(2,1)}, bf16[3,96,1152]{2,1,0:T(8,128)(2,1)S(1)}, u32[]{:S(2)}, u32[]{:S(2)}) collective-permute-start(bf16[3,96,1152]{2,1,0:T(8,128)(2,1)} %slice.432), channel_id=1, source_target_pairs={{0,2},{2,0},{1,3},{3,1},{4,6},{6,4},{5,7},{7,5},{8,10},{10,8},{9,1... | collective-permute-start | bytes 1990664 | tf_op jit(solution)/shard_map/ppermute | solution.py:34
  100.2 40.8 %collective-permute-start.6 = (bf16[3,96,1152]{2,1,0:T(8,128)(2,1)}, bf16[3,96,1152]{2,1,0:T(8,128)(2,1)}, u32[]{:S(2)}, u32[]{:S(2)}) collective-permute-start(bf16[3,96,1152]{2,1,0:T(8,128)(2,1)} %slice.433), channel_id=1, source_target_pairs={{0,16},{16,0},{1,17},{17,1},{2,18},{18,2},{3,19},{19,3},{4,20},{20... | collective-permute-start | bytes 1990664 | tf_op jit(solution)/shard_map/ppermute | solution.py:34
  141.1 644.2 %reduce-scatter.4.cloned.1.call-start = ((), (), s32[]{:S(2)}) async-start(), calls=%async_computation.4 | async-start | bytes 10616832 | tf_op jit(solution)/shard_map/reduce_scatter | solution.py:859
  141.3 66.3 %collective-permute-start.12 = (bf16[3,96,3840]{2,1,0:T(8,128)(2,1)}, bf16[3,96,3840]{2,1,0:T(8,128)(2,1)S(1)}, u32[]{:S(2)}, u32[]{:S(2)}) collective-permute-start(bf16[3,96,3840]{2,1,0:T(8,128)(2,1)} %pad_maximum_fusion.16.refs_5_), channel_id=1, source_target_pairs={{0,16},{16,0},{1,17},{17,1},{2,18},{18,2},{3,19},{19,3},{4,20},{20... | collective-permute-start | bytes 6635528 | tf_op jit(solution)/shard_map/ppermute | solution.py:34
  142.9 66.8 %collective-permute-start.11 = (bf16[3,96,3840]{2,1,0:T(8,128)(2,1)}, bf16[3,96,3840]{2,1,0:T(8,128)(2,1)}, u32[]{:S(2)}, u32[]{:S(2)}) collective-permute-start(bf16[3,96,3840]{2,1,0:T(8,128)(2,1)} %pad_maximum_fusion.16.refs_5_), channel_id=1, source_target_pairs={{0,2},{2,0},{1,3},{3,1},{4,6},{6,4},{5,7},{7,5},{8,10},{10,8},{9,1... | collective-permute-start | bytes 6635528 | tf_op jit(solution)/shard_map/ppermute | solution.py:34
  211.4 50.0 %collective-permute-start.13 = (bf16[3,96,1920]{2,1,0:T(8,128)(2,1)S(1)}, bf16[3,96,1920]{2,1,0:T(8,128)(2,1)S(1)}, u32[]{:S(2)}, u32[]{:S(2)}) collective-permute-start(bf16[3,96,1920]{2,1,0:T(8,128)(2,1)S(1)} %slice.436), channel_id=1, source_target_pairs={{0,2},{2,0},{1,3},{3,1},{4,6},{6,4},{5,7},{7,5},{8,10},{10,8},{9,1... | collective-permute-start | bytes 3317768 | tf_op jit(solution)/shard_map/ppermute | solution.py:34
  213.5 47.9 %collective-permute-start.14 = (bf16[3,96,1920]{2,1,0:T(8,128)(2,1)S(1)}, bf16[3,96,1920]{2,1,0:T(8,128)(2,1)S(1)}, u32[]{:S(2)}, u32[]{:S(2)}) collective-permute-start(bf16[3,96,1920]{2,1,0:T(8,128)(2,1)S(1)} %slice.437), channel_id=1, source_target_pairs={{0,16},{16,0},{1,17},{17,1},{2,18},{18,2},{3,19},{19,3},{4,20},{20... | collective-permute-start | bytes 3317768 | tf_op jit(solution)/shard_map/ppermute | solution.py:34
  291.0 4.5 collective-permute-start.16
  311.1 18.1 %collective-permute-start.19 = (bf16[512,1536]{1,0:T(8,128)(2,1)}, bf16[512,1536]{1,0:T(8,128)(2,1)}, u32[]{:S(2)}, u32[]{:S(2)}) collective-permute-start(bf16[512,1536]{1,0:T(8,128)(2,1)} %collective-permute-done.10), channel_id=1, source_target_pairs={{0,1},{1,0},{2,3},{3,2},{4,5},{5,4},{6,7},{7,6},{8,9},{9,8},{10,11... | collective-permute-start | bytes 4718600 | tf_op jit(solution)/shard_map/ppermute | solution.py:34
  326.7 36.5 %collective-permute-start.20 = (bf16[512,1536]{1,0:T(8,128)(2,1)S(1)}, bf16[512,1536]{1,0:T(8,128)(2,1)S(1)}, u32[]{:S(2)}, u32[]{:S(2)}) collective-permute-start(bf16[512,1536]{1,0:T(8,128)(2,1)S(1)} %add_convert_fusion.5), channel_id=1, source_target_pairs={{0,16},{16,0},{1,17},{17,1},{2,18},{18,2},{3,19},{19,3},{4,20},{20... | collective-permute-start | bytes 4718600 | tf_op jit(solution)/shard_map/ppermute | solution.py:34
  327.0 36.3 %collective-permute-start.23 = (bf16[512,1536]{1,0:T(8,128)(2,1)S(1)}, bf16[512,1536]{1,0:T(8,128)(2,1)S(1)}, u32[]{:S(2)}, u32[]{:S(2)}) collective-permute-start(bf16[512,1536]{1,0:T(8,128)(2,1)S(1)} %add_convert_fusion.5), channel_id=1, source_target_pairs={{0,1},{1,0},{2,3},{3,2},{4,5},{5,4},{6,7},{7,6},{8,9},{9,8},{10,11... | collective-permute-start | bytes 4718600 | tf_op jit(solution)/shard_map/ppermute | solution.py:34
  327.5 45.2 %collective-permute-start.22 = (bf16[512,1536]{1,0:T(8,128)(2,1)S(1)}, bf16[512,1536]{1,0:T(8,128)(2,1)S(1)}, u32[]{:S(2)}, u32[]{:S(2)}) collective-permute-start(bf16[512,1536]{1,0:T(8,128)(2,1)S(1)} %bitcast.245), channel_id=1, source_target_pairs={{0,1},{1,0},{2,3},{3,2},{4,5},{5,4},{6,7},{7,6},{8,9},{9,8},{10,11... | collective-permute-start | bytes 4718600 | tf_op jit(solution)/shard_map/ppermute | solution.py:34
  363.2 26.6 %collective-permute-start.21 = (bf16[512,1536]{1,0:T(8,128)(2,1)S(1)}, bf16[512,1536]{1,0:T(8,128)(2,1)S(1)}, u32[]{:S(2)}, u32[]{:S(2)}) collective-permute-start(bf16[512,1536]{1,0:T(8,128)(2,1)S(1)} %collective-permute-done.20), channel_id=1, source_target_pairs={{0,1},{1,0},{2,3},{3,2},{4,5},{5,4},{6,7},{7,6},{8,9},{9,8},{10,11... | collective-permute-start | bytes 4718600 | tf_op jit(solution)/shard_map/ppermute | solution.py:34
  415.9 5.9 collective-permute-start.24
  429.9 41.2 %collective-permute-start.25 = (bf16[512,1536]{1,0:T(8,128)(2,1)S(1)}, bf16[512,1536]{1,0:T(8,128)(2,1)S(1)}, u32[]{:S(2)}, u32[]{:S(2)}) collective-permute-start(bf16[512,1536]{1,0:T(8,128)(2,1)S(1)} %fusion.35), channel_id=1, source_target_pairs={{0,16},{16,0},{1,17},{17,1},{2,18},{18,2},{3,19},{19,3},{4,20},{20... | collective-permute-start | bytes 4718600 | tf_op jit(solution)/shard_map/ppermute | solution.py:34
  509.0 11.2 %collective-permute-start.27 = (bf16[2,64,1536]{2,1,0:T(8,128)(2,1)S(1)}, bf16[2,64,1536]{2,1,0:T(8,128)(2,1)S(1)}, u32[]{:S(2)}, u32[]{:S(2)}) collective-permute-start(bf16[2,64,1536]{2,1,0:T(8,128)(2,1)S(1)} %maximum_bitcast_fusion.3), channel_id=1, source_target_pairs={{0,16},{16,0},{1,17},{17,1},{2,18},{18,2},{3,19},{19,3},{4,20},{20... | collective-permute-start | bytes 1179656 | tf_op jit(solution)/shard_map/ppermute | solution.py:34
  533.5 16.6 %collective-permute-start.30 = (bf16[512,1536]{1,0:T(8,128)(2,1)}, bf16[512,1536]{1,0:T(8,128)(2,1)}, u32[]{:S(2)}, u32[]{:S(2)}) collective-permute-start(bf16[512,1536]{1,0:T(8,128)(2,1)} %convolution_convert_fusion.11), channel_id=1, source_target_pairs={{0,1},{1,0},{2,3},{3,2},{4,5},{5,4},{6,7},{7,6},{8,9},{9,8},{10,11... | collective-permute-start | bytes 4718600 | tf_op jit(solution)/shard_map/ppermute | solution.py:34
  537.3 314.9 %reduce-scatter.6.cloned.1.call-start = ((), (), s32[]{:S(2)}) async-start(), calls=%async_computation.5 | async-start | bytes 2949120 | tf_op jit(solution)/shard_map/reduce_scatter | solution.py:459
  556.3 15.2 %collective-permute-start.31 = (bf16[512,1536]{1,0:T(8,128)(2,1)S(1)}, bf16[512,1536]{1,0:T(8,128)(2,1)}, u32[]{:S(2)}, u32[]{:S(2)}) collective-permute-start(bf16[512,1536]{1,0:T(8,128)(2,1)S(1)} %get-tuple-element.245), channel_id=1, source_target_pairs={{0,1},{1,0},{2,3},{3,2},{4,5},{5,4},{6,7},{7,6},{8,9},{9,8},{10,11... | collective-permute-start | bytes 4718600 | tf_op jit(solution)/shard_map/ppermute | solution.py:34
  563.4 5.7 collective-permute-start.42
  563.9 53.3 %collective-permute-start.28 = (bf16[4,2,96,1536]{3,2,0,1:T(8,128)(2,1)S(1)}, bf16[4,2,96,1536]{3,2,0,1:T(8,128)(2,1)S(1)}, u32[]{:S(2)}, u32[]{:S(2)}) collective-permute-start(bf16[4,2,96,1536]{3,2,0,1:T(8,128)(2,1)S(1)} %copy-done.53), channel_id=1, source_target_pairs={{0,16},{16,0},{1,17},{17,1},{2,18},{18,2},{3,19},{19,3},{4,20},{20... | collective-permute-start | bytes 7077896 | tf_op jit(solution)/shard_map/ppermute | solution.py:34
  565.7 78.3 %collective-permute-start.29 = (bf16[4,2,96,1536]{3,2,0,1:T(8,128)(2,1)S(1)}, bf16[4,2,96,1536]{3,2,0,1:T(8,128)(2,1)S(1)}, u32[]{:S(2)}, u32[]{:S(2)}) collective-permute-start(bf16[4,2,96,1536]{3,2,0,1:T(8,128)(2,1)S(1)} %copy-done.52), channel_id=1, source_target_pairs={{0,2},{2,0},{1,3},{3,1},{4,6},{6,4},{5,7},{7,5},{8,10},{10,8},{9,1... | collective-permute-start | bytes 7077896 | tf_op jit(solution)/shard_map/ppermute | solution.py:34
  645.8 84.8 %collective-permute-start.32 = (bf16[4,96,1536]{2,1,0:T(8,128)(2,1)}, bf16[4,96,1536]{2,1,0:T(8,128)(2,1)}, u32[]{:S(2)}, u32[]{:S(2)}) collective-permute-start(bf16[4,96,1536]{2,1,0:T(8,128)(2,1)} %dynamic-slice_bitcast_fusion.3), channel_id=1, source_target_pairs={{0,2},{2,0},{1,3},{3,1},{4,6},{6,4},{5,7},{7,5},{8,10},{10,8},{9,1... | collective-permute-start | bytes 3538952 | tf_op jit(solution)/shard_map/ppermute | solution.py:34
  649.1 82.5 %collective-permute-start.33 = (bf16[4,96,1536]{2,1,0:T(8,128)(2,1)}, bf16[4,96,1536]{2,1,0:T(8,128)(2,1)}, u32[]{:S(2)}, u32[]{:S(2)}) collective-permute-start(bf16[4,96,1536]{2,1,0:T(8,128)(2,1)} %dynamic-slice_bitcast_fusion.2), channel_id=1, source_target_pairs={{0,16},{16,0},{1,17},{17,1},{2,18},{18,2},{3,19},{19,3},{4,20},{20... | collective-permute-start | bytes 3538952 | tf_op jit(solution)/shard_map/ppermute | solution.py:34
  724.4 12.4 %collective-permute-start.37 = (bf16[512,1536]{1,0:T(8,128)(2,1)}, bf16[512,1536]{1,0:T(8,128)(2,1)}, u32[]{:S(2)}, u32[]{:S(2)}) collective-permute-start(bf16[512,1536]{1,0:T(8,128)(2,1)} %convolution_convert_fusion.7), channel_id=1, source_target_pairs={{0,1},{1,0},{2,3},{3,2},{4,5},{5,4},{6,7},{7,6},{8,9},{9,8},{10,11... | collective-permute-start | bytes 4718600 | tf_op jit(solution)/shard_map/ppermute | solution.py:34
  724.4 21.5 %collective-permute-start.40 = (bf16[1024,1536]{1,0:T(8,128)(2,1)}, bf16[1024,1536]{1,0:T(8,128)(2,1)}, u32[]{:S(2)}, u32[]{:S(2)}) collective-permute-start(bf16[1024,1536]{1,0:T(8,128)(2,1)} %pad_maximum_fusion.11), channel_id=1, source_target_pairs={{0,1},{1,0},{2,3},{3,2},{4,5},{5,4},{6,7},{7,6},{8,9},{9,8},{10,11... | collective-permute-start | bytes 9437192 | tf_op jit(solution)/shard_map/ppermute | solution.py:34
  727.5 9.4 collective-permute-start.36
  730.6 54.0 %collective-permute-start.34 = (bf16[4,2,96,1536]{3,2,0,1:T(8,128)(2,1)}, bf16[4,2,96,1536]{3,2,0,1:T(8,128)(2,1)}, u32[]{:S(2)}, u32[]{:S(2)}) collective-permute-start(bf16[4,2,96,1536]{3,2,0,1:T(8,128)(2,1)} %maximum_maximum_fusion.6), channel_id=1, source_target_pairs={{0,16},{16,0},{1,17},{17,1},{2,18},{18,2},{3,19},{19,3},{4,20},{20... | collective-permute-start | bytes 7077896 | tf_op jit(solution)/shard_map/ppermute | solution.py:34
  731.6 53.7 %collective-permute-start.35 = (bf16[4,2,96,1536]{3,2,0,1:T(8,128)(2,1)}, bf16[4,2,96,1536]{3,2,0,1:T(8,128)(2,1)}, u32[]{:S(2)}, u32[]{:S(2)}) collective-permute-start(bf16[4,2,96,1536]{3,2,0,1:T(8,128)(2,1)} %maximum_maximum_fusion.7), channel_id=1, source_target_pairs={{0,2},{2,0},{1,3},{3,1},{4,6},{6,4},{5,7},{7,5},{8,10},{10,8},{9,1... | collective-permute-start | bytes 7077896 | tf_op jit(solution)/shard_map/ppermute | solution.py:34
  785.3 138.6 %reduce-scatter.8.cloned.1.call-start = ((), (), s32[]{:S(2)}) async-start(), calls=%async_computation.6 | async-start | bytes 2949120 | tf_op jit(solution)/shard_map/reduce_scatter | solution.py:459
  789.1 37.4 %collective-permute-start.41 = (bf16[512,1536]{1,0:T(8,128)(2,1)S(1)}, bf16[512,1536]{1,0:T(8,128)(2,1)S(1)}, u32[]{:S(2)}, u32[]{:S(2)}) collective-permute-start(bf16[512,1536]{1,0:T(8,128)(2,1)S(1)} %fusion.31), channel_id=1, source_target_pairs={{0,16},{16,0},{1,17},{17,1},{2,18},{18,2},{3,19},{19,3},{4,20},{20... | collective-permute-start | bytes 4718600 | tf_op jit(solution)/shard_map/ppermute | solution.py:34
  792.8 36.1 %collective-permute-start.38 = (bf16[4,96,1536]{2,1,0:T(8,128)(2,1)S(1)}, bf16[4,96,1536]{2,1,0:T(8,128)(2,1)S(1)}, u32[]{:S(2)}, u32[]{:S(2)}) collective-permute-start(bf16[4,96,1536]{2,1,0:T(8,128)(2,1)S(1)} %dynamic-slice_bitcast_fusion.1), channel_id=1, source_target_pairs={{0,2},{2,0},{1,3},{3,1},{4,6},{6,4},{5,7},{7,5},{8,10},{10,8},{9,1... | collective-permute-start | bytes 3538952 | tf_op jit(solution)/shard_map/ppermute | solution.py:34
  795.9 54.2 %collective-permute-start.39 = (bf16[4,96,1536]{2,1,0:T(8,128)(2,1)S(1)}, bf16[4,96,1536]{2,1,0:T(8,128)(2,1)S(1)}, u32[]{:S(2)}, u32[]{:S(2)}) collective-permute-start(bf16[4,96,1536]{2,1,0:T(8,128)(2,1)S(1)} %dynamic-slice_bitcast_fusion), channel_id=1, source_target_pairs={{0,16},{16,0},{1,17},{17,1},{2,18},{18,2},{3,19},{19,3},{4,20},{20... | collective-permute-start | bytes 3538952 | tf_op jit(solution)/shard_map/ppermute | solution.py:34
  854.3 13.8 %collective-permute-start.52 = (bf16[384,768]{1,0:T(8,128)(2,1)S(1)}, bf16[384,768]{1,0:T(8,128)(2,1)S(1)}, u32[]{:S(2)}, u32[]{:S(2)}) collective-permute-start(bf16[384,768]{1,0:T(8,128)(2,1)S(1)} %maximum_dynamic-update-slice_fusion.2), channel_id=1, source_target_pairs={{0,16},{16,0},{1,17},{17,1},{2,18},{18,2},{3,19},{19,3},{4,20},{20... | collective-permute-start | bytes 1769480 | tf_op jit(solution)/shard_map/ppermute | solution.py:34
  855.3 13.7 %collective-permute-start.51 = (bf16[384,768]{1,0:T(8,128)(2,1)S(1)}, bf16[384,768]{1,0:T(8,128)(2,1)S(1)}, u32[]{:S(2)}, u32[]{:S(2)}) collective-permute-start(bf16[384,768]{1,0:T(8,128)(2,1)S(1)} %maximum_dynamic-update-slice_fusion.2), channel_id=1, source_target_pairs={{0,2},{2,0},{1,3},{3,1},{4,6},{6,4},{5,7},{7,5},{8,10},{10,8},{9,1... | collective-permute-start | bytes 1769480 | tf_op jit(solution)/shard_map/ppermute | solution.py:34
  868.1 10.0 collective-permute-start.53
  869.1 10.0 collective-permute-start.54
  870.2 30.2 %collective-permute-start.62 = (bf16[384,1536]{1,0:T(8,128)(2,1)S(1)}, bf16[384,1536]{1,0:T(8,128)(2,1)S(1)}, u32[]{:S(2)}, u32[]{:S(2)}) collective-permute-start(bf16[384,1536]{1,0:T(8,128)(2,1)S(1)} %copy-done.66), channel_id=1, source_target_pairs={{0,16},{16,0},{1,17},{17,1},{2,18},{18,2},{3,19},{19,3},{4,20},{20... | collective-permute-start | bytes 3538952 | tf_op jit(solution)/shard_map/ppermute | solution.py:34
  871.2 31.3 %collective-permute-start.61 = (bf16[384,1536]{1,0:T(8,128)(2,1)S(1)}, bf16[384,1536]{1,0:T(8,128)(2,1)S(1)}, u32[]{:S(2)}, u32[]{:S(2)}) collective-permute-start(bf16[384,1536]{1,0:T(8,128)(2,1)S(1)} %copy-done.66), channel_id=1, source_target_pairs={{0,2},{2,0},{1,3},{3,1},{4,6},{6,4},{5,7},{7,5},{8,10},{10,8},{9,1... | collective-permute-start | bytes 3538952 | tf_op jit(solution)/shard_map/ppermute | solution.py:34
  879.5 36.7 %collective-permute-start.55 = (bf16[4,384,768]{2,1,0:T(8,128)(2,1)S(1)}, bf16[4,384,768]{2,1,0:T(8,128)(2,1)S(1)}, u32[]{:S(2)}, u32[]{:S(2)}) collective-permute-start(bf16[4,384,768]{2,1,0:T(8,128)(2,1)S(1)} %pad_maximum_fusion.14.refs_0_.refs_1_.refs_2_), channel_id=1, source_target_pairs={{0,1},{1,0},{2,3},{3,2},{4,5},{5,4},{6,7},{7,6},{8,9},{9,8},{10,11... | collective-permute-start | bytes 7077896 | tf_op jit(solution)/shard_map/ppermute | solution.py:34
  900.5 12.5 %collective-permute-start.63 = (bf16[384,768]{1,0:T(8,128)(2,1)S(1)}, bf16[384,768]{1,0:T(8,128)(2,1)S(1)}, u32[]{:S(2)}, u32[]{:S(2)}) collective-permute-start(bf16[384,768]{1,0:T(8,128)(2,1)S(1)} %slice.486), channel_id=1, source_target_pairs={{0,2},{2,0},{1,3},{3,1},{4,6},{6,4},{5,7},{7,5},{8,10},{10,8},{9,1... | collective-permute-start | bytes 1769480 | tf_op jit(solution)/shard_map/ppermute | solution.py:34
  902.5 11.1 %collective-permute-start.64 = (bf16[384,768]{1,0:T(8,128)(2,1)S(1)}, bf16[384,768]{1,0:T(8,128)(2,1)S(1)}, u32[]{:S(2)}, u32[]{:S(2)}) collective-permute-start(bf16[384,768]{1,0:T(8,128)(2,1)S(1)} %slice.487), channel_id=1, source_target_pairs={{0,16},{16,0},{1,17},{17,1},{2,18},{18,2},{3,19},{19,3},{4,20},{20... | collective-permute-start | bytes 1769480 | tf_op jit(solution)/shard_map/ppermute | solution.py:34
  910.2 19.4 %collective-permute-start.43 = (bf16[512,1536]{1,0:T(8,128)(2,1)}, bf16[512,1536]{1,0:T(8,128)(2,1)S(1)}, u32[]{:S(2)}, u32[]{:S(2)}) collective-permute-start(bf16[512,1536]{1,0:T(8,128)(2,1)} %convolution_convert_fusion.6), channel_id=1, source_target_pairs={{0,1},{1,0},{2,3},{3,2},{4,5},{5,4},{6,7},{7,6},{8,9},{9,8},{10,11... | collective-permute-start | bytes 4718600 | tf_op jit(solution)/shard_map/ppermute | solution.py:34
  916.2 90.3 %collective-permute-start.65 = (bf16[4,384,1536]{2,1,0:T(8,128)(2,1)}, bf16[4,384,1536]{2,1,0:T(8,128)(2,1)}, u32[]{:S(2)}, u32[]{:S(2)}) collective-permute-start(bf16[4,384,1536]{2,1,0:T(8,128)(2,1)} %pad_maximum_fusion.2.refs_0_.refs_1_.own_ref), channel_id=1, source_target_pairs={{0,1},{1,0},{2,3},{3,2},{4,5},{5,4},{6,7},{7,6},{8,9},{9,8},{10,11... | collective-permute-start | bytes 14155784 | tf_op jit(solution)/shard_map/ppermute | solution.py:34
  927.6 16.2 %collective-permute-start.57 = (bf16[384,768]{1,0:T(8,128)(2,1)S(1)}, bf16[384,768]{1,0:T(8,128)(2,1)S(1)}, u32[]{:S(2)}, u32[]{:S(2)}) collective-permute-start(bf16[384,768]{1,0:T(8,128)(2,1)S(1)} %maximum_dynamic-update-slice_fusion.4), channel_id=1, source_target_pairs={{0,16},{16,0},{1,17},{17,1},{2,18},{18,2},{3,19},{19,3},{4,20},{20... | collective-permute-start | bytes 1769480 | tf_op jit(solution)/shard_map/ppermute | solution.py:34
  928.6 16.1 %collective-permute-start.56 = (bf16[384,768]{1,0:T(8,128)(2,1)S(1)}, bf16[384,768]{1,0:T(8,128)(2,1)S(1)}, u32[]{:S(2)}, u32[]{:S(2)}) collective-permute-start(bf16[384,768]{1,0:T(8,128)(2,1)S(1)} %maximum_dynamic-update-slice_fusion.4), channel_id=1, source_target_pairs={{0,2},{2,0},{1,3},{3,1},{4,6},{6,4},{5,7},{7,5},{8,10},{10,8},{9,1... | collective-permute-start | bytes 1769480 | tf_op jit(solution)/shard_map/ppermute | solution.py:34
  935.0 48.9 %collective-permute-start.44 = (bf16[512,1536]{1,0:T(8,128)(2,1)S(1)}, bf16[512,1536]{1,0:T(8,128)(2,1)S(1)}, u32[]{:S(2)}, u32[]{:S(2)}) collective-permute-start(bf16[512,1536]{1,0:T(8,128)(2,1)S(1)} %add_convert_fusion.4), channel_id=1, source_target_pairs={{16,0},{17,1},{18,2},{19,3},{20,4},{21,5},{22,6},{23,7},{24,8},{25... | collective-permute-start | bytes 4718600 | tf_op jit(solution)/shard_map/ppermute | solution.py:56
  943.8 8.3 collective-permute-start.58
  944.8 38.6 %collective-permute-start.59 = (bf16[384,384]{1,0:T(8,128)(2,1)S(1)}, bf16[384,384]{1,0:T(8,128)(2,1)S(1)}, u32[]{:S(2)}, u32[]{:S(2)}) collective-permute-start(bf16[384,384]{1,0:T(8,128)(2,1)S(1)} %slice.485), channel_id=1, source_target_pairs={{0,16},{16,0},{1,17},{17,1},{2,18},{18,2},{3,19},{19,3},{4,20},{20... | collective-permute-start | bytes 884744 | tf_op jit(solution)/shard_map/ppermute | solution.py:34
  983.8 39.0 %collective-permute-start.60 = (bf16[4,384,768]{2,1,0:T(8,128)(2,1)S(1)}, bf16[4,384,768]{2,1,0:T(8,128)(2,1)}, u32[]{:S(2)}, u32[]{:S(2)}) collective-permute-start(bf16[4,384,768]{2,1,0:T(8,128)(2,1)S(1)} %pad_maximum_fusion.15.refs_0_.refs_1_.refs_2_), channel_id=1, source_target_pairs={{0,1},{1,0},{2,3},{3,2},{4,5},{5,4},{6,7},{7,6},{8,9},{9,8},{10,11... | collective-permute-start | bytes 7077896 | tf_op jit(solution)/shard_map/ppermute | solution.py:34
  996.8 9.0 collective-permute-start.48
  997.0 8.8 collective-permute-start.50
  999.3 6.5 collective-permute-start.49
  (115 other events, 1846.4 us)
Sparse Core Ops, SparseCore 0:
  16.7 42.9 all-gather.7
  61.9 59.2 all-gather.9
  141.2 166.6 all-gather.5
  537.4 187.3 reduce-scatter.3
  785.4 45.7 reduce-scatter.5
  852.4 45.7 reduce-scatter.7

commit v3 on v2

--- a/solution.py
+++ b/solution.py
@@ -473,11 +473,22 @@
             axis=0,
         )
 
-    def spread(self, piece):
+
+    def spread_sides(self, piece):
+        return piece, swap_row(piece), swap_ctx(piece)
+
+    def spread_parts(self, sides):
+        piece, from_y, from_x = sides
         half = piece.shape[-1] // 2
-        from_y, from_x = swap_row(piece), swap_ctx(piece)
-        corner = jnp.concatenate([swap_row(from_x[..., :half]), swap_ctx(from_y[..., half:])], axis=-1)
-        own = jnp.stack([piece, from_y, from_x, corner])
+        return piece, from_y, from_x, from_x[..., :half], from_y[..., half:]
+
+    def spread_corners(self, parts):
+        piece, from_y, from_x, to_y, to_x = parts
+        return piece, from_y, from_x, swap_row(to_y), swap_ctx(to_x)
+
+    def spread_cores(self, parts):
+        piece, from_y, from_x, left, right = parts
+        own = jnp.stack([piece, from_y, from_x, jnp.concatenate([left, right], axis=-1)])
         return own, swap_core(own)
 
     def feed_gradient(self, lefts, rights, which, joined=None):
@@ -839,16 +850,22 @@
         w_feed, hidden_two = tied(w_feed, hidden_two)
         w_up, w_down = w_feed[:, :hidden], w_feed[:, hidden:]
     normed_own = layer_norm(hidden_two, gain_three, shift_three).astype(BF16)
-    normed_three = [both(normed_own)]
-    grad_branch = [both(cotangent_own)]
-    if staged:
-        normed_three.append(both(swap_ctx(normed_own)))
-        grad_branch.append(both(cotangent_far))
-    activated, grad_pre = [], []
-    for normed, grad in zip(normed_three, grad_branch):
+    normed_three, grad_branch, activated, grad_pre = [both(normed_own)], [both(cotangent_own)], [], []
+
+    def feed_rows(normed, grad):
         act, slope = gelu_parts(product(normed, w_up))
         activated.append(act.astype(BF16))
         grad_pre.append((against(grad, w_down) * slope).astype(BF16))
+
+    if staged:
+        normed_far = swap_ctx(normed_own)
+        grad_branch.append(both(cotangent_far))
+        feed_rows(normed_three[0], grad_branch[0])
+        normed_far, activated[0], grad_pre[0] = tied(normed_far, activated[0], grad_pre[0])
+        normed_three.append(both(normed_far))
+        feed_rows(normed_three[1], grad_branch[1])
+    else:
+        feed_rows(normed_three[0], grad_branch[0])
     if staged:
         far, near = QuadSum(*grad_pre, w_up, against).cores()
         far, activated, normed_three, grad_branch, grad_pre = tied(far, activated, normed_three, grad_branch, grad_pre)
@@ -892,6 +909,8 @@
         )
         early, grad_cq = tied(early, grad_cq)
         early = place.first_swap(early)
+        mixed_far, mixed = mixed.cores()
+        mixed = mixed + swap_ctx(mixed_far).astype(F32)
     grad_hid, grad_gain_two, grad_shift_two = norm_backward(
         hidden_one, gain_two, pair_sum(grad_cq, w_cross_query, against)
     )
@@ -901,10 +920,8 @@
     grad_out = over_rows(attended, grad_branch).astype(BF16)
     grad_att = against(grad_branch, w_out).astype(BF16).reshape(2 * clips, span, half)
     if staged:
-        early, grad_att, mixed.parts = tied(early, grad_att, mixed.parts)
-        early = place.second_swap(early)
-        mixed_far, mixed_near = mixed.cores()
-        mixed = mixed_near + swap_ctx(mixed_far).astype(F32)
+        early, grad_att, mixed, feed = tied(early, grad_att, mixed, feed)
+        early, feed = place.second_swap(early), place.spread_sides(feed)
     grad_q, grad_k, grad_v = attend_back(
         position,
         queries,
@@ -927,20 +944,25 @@
         late = beside(
             place.first_sends(grad_query), place.first_sends(grad_key_value), restack(place.first_sends(grad_out))
         )
-        late, grad_q, grad_kv = tied(late, grad_q, grad_kv)
-        late = place.first_swap(late)
-    grad_normed_before = pair_sum(grad_kv[: 2 * rows], w_key_value, against)
-    returned = shifted(grad_normed_before.astype(BF16), "ctx", -1)
+        early, late, feed, grad_q, grad_kv = tied(
+            place.second_sum(early), late, place.spread_parts(feed), grad_q, grad_kv
+        )
+        early, late, feed = place.shard_sum(early), place.first_swap(late), place.spread_corners(feed)
+    grad_normed_before = pair_sum(grad_kv[: 2 * rows], w_key_value, against).astype(BF16)
     grad_normed = pair_sum(grad_q, w_query, against) + pair_sum(grad_kv[2 * rows :], w_key_value, against)
-    if staged:
-        early, late, feed, grad_normed = tied(place.second_sum(early), late, feed, grad_normed)
-        early, late = place.shard_sum(early), place.second_swap(late)
     grad_text = pair_sum(grad_ckv.reshape(2 * clips * texts, width), w_cross_kv, against).reshape(clips, texts, width)
     mixed = hidden_two + (mixed if staged else pair_sum(activated[0], w_down, product))
     mixed = mixed.astype(BF16).reshape(clips, span, width)
     if staged:
-        early, late, mixed, grad_text, feed = tied(early, place.second_sum(late), mixed, grad_text, feed)
-        late, early, feed = place.shard_sum(late), place.spread(place.packed(early)), place.spread(feed)
+        late, feed, grad_normed, grad_normed_before, grad_text, mixed = tied(
+            late, feed, grad_normed, grad_normed_before, grad_text, mixed
+        )
+        late, feed = place.second_swap(late), place.spread_cores(feed)
+    returned = shifted(grad_normed_before, "ctx", -1)
+    if staged:
+        early, late = tied(place.packed(early), place.second_sum(late))
+        early, late = place.spread_sides(early), place.shard_sum(late)
+        total_up, total_down = place.finish_up(*feed), place.finish_down(*feed)
     grad_hid, grad_gain_one, grad_shift_one = norm_backward(
         hidden_zero, gain_one, grad_normed + returned.astype(F32)
     )
@@ -951,16 +973,18 @@
     )
     small = place.sum_norms(small)
     if staged:
-        own, other = early
-        total_cross_query, total_cross_key, total_cross_value = place.finish_columns(own, other, 3)
-        total_cross_out = place.finish_rows(own, other)
+        early, late, total_up, total_down, grad_frames = tied(
+            place.spread_parts(early), place.packed(late), total_up, total_down, grad_frames
+        )
+        late, early = place.spread_sides(late), place.spread_corners(early)
+        late, early = tied(place.spread_parts(late), early)
+        late, early = place.spread_corners(late), place.spread_cores(early)
+        total_cross_query, total_cross_key, total_cross_value = place.finish_columns(*early, 3)
+        total_cross_out = place.finish_rows(*early)
         late, total_cross_query, total_cross_out = tied(late, total_cross_query, total_cross_out)
-        late = place.spread(place.packed(late))
-        total_up, total_down = place.finish_up(*feed), place.finish_down(*feed)
-        late, total_up, total_down = tied(late, total_up, total_down)
-        own, other = late
-        total_query, total_key, total_value = place.finish_columns(own, other, 3)
-        total_out = place.finish_rows(own, other)
+        late = place.spread_cores(late)
+        total_query, total_key, total_value = place.finish_columns(*late, 3)
+        total_out = place.finish_rows(*late)
     else:
         total_cross_out, total_out, total_down = map(place.plain_rows, (grad_cross_out, grad_out, grad_down))
         total_cross_key, total_cross_value = place.plain_columns(grad_cross_kv, 2)

time: 1050 us -> 1000 us (0.952)
  waiting for transfers between devices: 432 us -> 405 us
  matrix products: 204 us -> 187 us
    ppermute x64, waiting for transfers between devices: 388 us -> 302 us  [xor_permute(): lax.ppermute(array, axis, [(i, i ^ bit) for i in range(lax.axis_size(axis...]
    ppermute x2, waiting for transfers between devices: 0.01 us -> 34.1 us  [shifted(): return lax.ppermute(block, axis, route)]
    reduce_scatter x1, waiting for transfers between devices: 0.01 us -> 24.2 us  [local(): lax.psum_scatter(feed.reshape(-1, width), FEED, scatter_dimension=0, tile...]
    dot_general x18, matrix products: 100 us -> 85 us  [against(): lax.dot_general(left, right, (((1,), (1,)), ((), ())), preferred_element_...]
    unnamed x244 -> x264, local copies, waits for them, and re-layouts: 24.1 us -> 26.4 us
  transfers between devices with their start and end apart: 72 -> 72, of which waited for: 35 -> 34; matrix products, arithmetic and copies ran while one was open for 25% -> 26% of each run, Pallas kernels for 16% -> 18%
where the time goes in v3:
time: 1000 us; the launch traced here: 996 us
  waiting for transfers between devices  405 us (40%)
  Pallas kernels  195 us (20%)
  matrix products  187 us (19%)
  other arithmetic  81.7 us (8%)
  starting transfers between devices  58.5 us (6%)
  local copies, waits for them, and re-layouts  52.7 us (5%)
  between operations  16.6 us (2%)
    ppermute x64, waiting for transfers between devices, xor_permute(): lax.ppermute(array, axis, [(i, i ^ bit) for i in range(lax.axis_size(axis...  302 us
    dot_general x18, matrix products, against(): lax.dot_general(left, right, (((1,), (1,)), ((), ())), preferred_element_...  85 us
    dot_general x14, matrix products, product(): return jnp.dot(left, right, preferred_element_type=F32)  74 us
    ppermute x64, starting transfers between devices, xor_permute(): lax.ppermute(array, axis, [(i, i ^ bit) for i in range(lax.axis_size(axis...  50.2 us
    pallas_call x2, Pallas kernels, attend_back(): pl.pallas_call(lambda *refs: attend_back_kernel(causal, *refs), grid=(cli...  49.9 us
    all_gather x2, waiting for transfers between devices, exchange_z(): return lax.all_gather(mine, 'shard', axis=0, tiled=False)  43.6 us
    pallas_call x2, Pallas kernels, attend(): pl.pallas_call(lambda *refs: attend_kernel(causal, *refs), grid=(clips, p...  41.1 us
    pallas_call x2, Pallas kernels, feed_gradient(): pl.pallas_call(kernel, grid=(4, 2), in_specs=[pl.BlockSpec((each.shape[0]...  35.3 us
  transfers between devices with their start and end apart: 72, of which 34 were waited for; matrix products, arithmetic and copies ran while one was open for 26% of the time, Pallas kernels for 18%

profile of v3, /device:TPU:0, one launch (start us, length us, event | category | flops | bytes accessed | tf_op | source)
XLA Modules:
  0.0 996.1 jit_solution(11939127165187367624)
XLA Ops:
  11.1 4.4 shard_map.330
  17.2 5.6 collective-permute-start
  22.8 3.3 pad_maximum_fusion.3
  26.1 33.7 %all-gather.8.cloned.1.call-done = bf16[384,2304]{1,0:T(8,128)(2,1)} async-done(((bf16[96,2304]{1,0:T(8,128)(2,1)}), bf16[384,2304]{1,0:T(8,128)(2,1)}) %all-gather.8.cloned.1.call-update) | async-done | bytes 1769488 | tf_op jit(solution)/shard_map/all_gather | solution.py:354
  70.1 3.8 collective-permute-done.9
  74.1 19.4 %collective-permute-done.3.refs_5_ = bf16[3,96,2304]{2,1,0:T(8,128)(2,1)S(1)} collective-permute-done((bf16[3,96,2304]{2,1,0:T(8,128)(2,1)S(1)}, bf16[3,96,2304]{2,1,0:T(8,128)(2,1)S(1)}, u32[]{:S(2)}, u32[]{:S(2)}) %collective-permute-start.3) | collective-permute-done | bytes 1327136 | tf_op jit(solution)/shard_map/ppermute | solution.py:34
  105.4 5.8 fusion.5
  111.2 9.9 all-gather.10.cloned.1.call-done
  127.3 13.8 %collective-permute-done.6.refs_7_ = bf16[3,96,1152]{2,1,0:T(8,128)(2,1)} collective-permute-done((bf16[3,96,1152]{2,1,0:T(8,128)(2,1)}, bf16[3,96,1152]{2,1,0:T(8,128)(2,1)}, u32[]{:S(2)}, u32[]{:S(2)}) %collective-permute-start.6) | collective-permute-done | bytes 663584 | tf_op jit(solution)/shard_map/ppermute | solution.py:34
  147.3 12.3 %shard_map.331 = (bf16[1536,768]{1,0:T(8,128)(2,1)}, bf16[1536,1536]{1,0:T(8,128)(2,1)}) custom-call(s32[5]{0:T(128)S(1)} %stack.122.at, bf16[384,1536]{1,0:T(8,128)(2,1)S(1)} %copy-done.5, bf16[384,1536]{1,0:T(8,128)(2,1)S(1)} %copy-done.7, bf16[384,1536]{1,0:T(8,128)(2,1)S(1)} %copy-done.9, bf16[3,96,2304]{2,1,0:T(8,128)(2,1)S(1)} %pad_maximum_fusion.29.refs_3_, ...), custom_call_target="tpu_custom_call" | custom-call | tf_op jit(solution)/shard_map/pallas_call | solution.py:411
  159.6 4.4 fusion.71
  164.0 11.8 %convolution_convert_fusion = bf16[2048,1536]{1,0:T(8,128)(2,1)} fusion(bf16[2048,1536]{1,0:T(8,128)(2,1)S(1)} %copy-done.47, bf16[1536,1536]{1,0:T(8,128)(2,1)S(1)} %copy-done.96), kind=kOutput, calls=%fused_computation.11 | convolution fusion | flops 9666822144 | bytes 17301504 | tf_op jit(solution)/shard_map/dot_general | solution.py:22
  175.8 31.6 %shard_map.332 = (bf16[2,512,768]{2,1,0:T(8,128)(2,1)S(1)}, f32[2,6,2,512]{3,2,1,0:T(2,128)S(1)}) custom-call(s32[1]{0:T(128)} %bitcast.14.refs_0_, bf16[2,512,768]{2,1,0:T(8,128)(2,1)S(1)} %bitcast.217, bf16[2,2,512,1536]{3,2,1,0:T(8,128)(2,1)} %bitcast.229, bf16[2,2,512,1536]{3,2,1,0:T(8,128)(2,1)} %bitcast.230), custom_call_target="tpu_custom_call" | custom-call | tf_op jit(solution)/shard_map/pallas_call | solution.py:200
  214.1 47.9 %collective-permute-done.13.refs_8_ = bf16[3,96,1920]{2,1,0:T(8,128)(2,1)S(1)} collective-permute-done((bf16[3,96,1920]{2,1,0:T(8,128)(2,1)S(1)}, bf16[3,96,1920]{2,1,0:T(8,128)(2,1)S(1)}, u32[]{:S(2)}, u32[]{:S(2)}) %collective-permute-start.13) | collective-permute-done | bytes 1105952 | tf_op jit(solution)/shard_map/ppermute | solution.py:34
  262.0 15.9 %shard_map.333 = (bf16[768,1536]{1,0:T(8,128)(2,1)}, bf16[768,1536]{1,0:T(8,128)(2,1)}, bf16[1536,768]{1,0:T(8,128)(2,1)}, bf16[1536,1536]{1,0:T(8,128)(2,1)}) custom-call(s32[5]{0:T(128)S(1)} %stack.122.at, bf16[384,1536]{1,0:T(8,128)(2,1)S(1)} %copy-done.10, bf16[384,1536]{1,0:T(8,128)(2,1)S(1)} %copy-done.11, bf16[384,1536]{1,0:T(8,128)(2,1)S(1)} %copy-done.12, ...), custom_call_target="tpu_custom_call" | custom-call | tf_op jit(solution)/shard_map/pallas_call | solution.py:411
  277.9 4.3 convolution_convert_fusion.15
  282.3 3.7 collective-permute-done.15
  286.0 3.8 fusion.132
  298.7 9.5 shard_map.334
  314.5 6.1 fusion.23
  328.8 9.3 multiply_convert_fusion.1
  338.2 9.8 fusion.11.refs_2_
  348.0 14.7 %collective-permute-done.20 = bf16[512,1536]{1,0:T(8,128)(2,1)S(1)} collective-permute-done((bf16[512,1536]{1,0:T(8,128)(2,1)S(1)}, bf16[512,1536]{1,0:T(8,128)(2,1)S(1)}, u32[]{:S(2)}, u32[]{:S(2)}) %collective-permute-start.20) | collective-permute-done | bytes 1572896 | tf_op jit(solution)/shard_map/ppermute | solution.py:34
  367.3 7.5 multiply_convert_fusion
  374.8 9.9 fusion.17.refs_3_
  394.3 3.9 fusion.34
  400.4 17.3 %shard_map.335.refs_4_ = bf16[4,2,384,1536]{3,2,1,0:T(8,128)(2,1)} custom-call(bf16[1024,1536]{1,0:T(8,128)(2,1)S(1)} %copy-done.13, bf16[1024,1536]{1,0:T(8,128)(2,1)} %get-tuple-element.196.refs_1_, bf16[1024,1536]{1,0:T(8,128)(2,1)} %pad_maximum_fusion.7.refs_2_, bf16[1024,1536]{1,0:T(8,128)(2,1)} %copy-done.45), custom_call_target="tpu_custom_call" | custom-call | tf_op jit(solution)/shard_map/pallas_call | solution.py:507
  417.8 18.0 %shard_map.336 = bf16[4,2,384,1536]{3,2,1,0:T(8,128)(2,1)} custom-call(bf16[1024,1536]{1,0:T(8,128)(2,1)S(1)} %pad_maximum_fusion.6.refs_0_, bf16[1024,1536]{1,0:T(8,128)(2,1)} %copy-done.46, bf16[1024,1536]{1,0:T(8,128)(2,1)} %copy-done.57, bf16[1024,1536]{1,0:T(8,128)(2,1)} %copy-done.59, ...), custom_call_target="tpu_custom_call", output_to_operand_aliasing={{}: (4, {})} | custom-call | tf_op jit(solution)/shard_map/pallas_call | solution.py:507
  435.8 6.6 convolution_add_fusion.6
  444.5 4.5 multiply_reduce_fusion
  452.1 6.1 convolution_convert_fusion.10
  462.6 4.7 fusion.69
  467.3 13.5 %shard_map.337 = (bf16[2,512,768]{2,1,0:T(8,128)(2,1)S(1)}, bf16[1,2,64,768]{3,2,1,0:T(8,128)(2,1)S(1)}, bf16[1,2,64,768]{3,2,1,0:T(8,128)(2,1)S(1)}) custom-call(s32[1]{0:T(128)} %bitcast.14.refs_0_, bf16[2,512,768]{2,1,0:T(8,128)(2,1)S(1)} %bitcast.216, bf16[1,2,64,1536]{3,2,1,0:T(8,128)(2,1)S(1)} %bitcast.213, bf16[1,2,64,1536]{3,2,1,0:T(8,128)(2,1)S(1)} %bitcast.214, ...), custom_call_target="tpu_custom_call" | custom-call | tf_op jit(solution)/shard_map/pallas_call | solution.py:229
  482.6 4.6 convolution_convert_fusion.5
  489.3 3.3 convolution_convert_fusion.4
  506.5 5.2 fusion.32
  526.0 23.0 %collective-permute-done.33 = bf16[512,1536]{1,0:T(8,128)(2,1)S(1)} collective-permute-done((bf16[512,1536]{1,0:T(8,128)(2,1)S(1)}, bf16[512,1536]{1,0:T(8,128)(2,1)S(1)}, u32[]{:S(2)}, u32[]{:S(2)}) %collective-permute-start.33) | collective-permute-done | bytes 1572896 | tf_op jit(solution)/shard_map/ppermute | solution.py:34
  549.0 6.9 fusion.33
  562.9 4.7 fusion.70
  567.6 31.7 %collective-permute-done.28 = bf16[4,2,96,1536]{3,2,0,1:T(8,128)(2,1)} collective-permute-done((bf16[4,2,96,1536]{3,2,0,1:T(8,128)(2,1)S(1)}, bf16[4,2,96,1536]{3,2,0,1:T(8,128)(2,1)}, u32[]{:S(2)}, u32[]{:S(2)}) %collective-permute-start.28) | collective-permute-done | bytes 2359328 | tf_op jit(solution)/shard_map/ppermute | solution.py:34
  599.3 6.7 collective-permute-done.29
  606.0 24.2 %reduce-scatter.4.cloned.1.call-done = bf16[384,1536]{1,0:T(8,128)(2,1)} async-done(((bf16[3072,1536]{1,0:T(8,128)(2,1)}), bf16[384,1536]{1,0:T(8,128)(2,1)}) %reduce-scatter.4.cloned.1.call-update) | async-done | bytes 1179664 | tf_op jit(solution)/shard_map/reduce_scatter | solution.py:876
  632.8 36.4 %shard_map.338 = (bf16[2,512,768]{2,1,0:T(8,128)(2,1)S(1)}, bf16[2,2,512,768]{3,2,1,0:T(8,128)(2,1)}, bf16[2,2,512,768]{3,2,1,0:T(8,128)(2,1)}) custom-call(s32[1]{0:T(128)} %bitcast.14.refs_0_, bf16[2,512,768]{2,1,0:T(8,128)(2,1)S(1)} %bitcast.218, bf16[2,2,512,1536]{3,2,1,0:T(8,128)(2,1)} %bitcast.231, bf16[2,2,512,1536]{3,2,1,0:T(8,128)(2,1)} %bitcast.232, ...), custom_call_target="tpu_custom_call" | custom-call | tf_op jit(solution)/shard_map/pallas_call | solution.py:229
  669.2 5.2 convolution_convert_fusion.3
  677.2 10.8 %convolution_convert_fusion.1 = bf16[1536,1536]{1,0:T(8,128)(2,1)S(1)} fusion(bf16[2048,1536]{1,0:T(8,128)(2,1)S(1)} %bitcast.241, bf16[2048,768]{1,0:T(8,128)(2,1)S(1)} %bitcast.259, bf16[2048,768]{1,0:T(8,128)(2,1)S(1)} %bitcast.257), kind=kOutput, calls=%fused_computation.12 | convolution fusion | flops 9678618624 | bytes 17301504 | tf_op jit(solution)/shard_map/dot_general | solution.py:26
  708.7 13.5 %collective-permute-done.34 = bf16[4,96,1536]{2,1,0:T(8,128)(2,1)} collective-permute-done((bf16[4,96,1536]{2,1,0:T(8,128)(2,1)}, bf16[4,96,1536]{2,1,0:T(8,128)(2,1)}, u32[]{:S(2)}, u32[]{:S(2)}) %collective-permute-start.34) | collective-permute-done | bytes 1179680 | tf_op jit(solution)/shard_map/ppermute | solution.py:34
  730.9 6.6 convolution_convert_fusion.6
  737.5 6.7 convolution_convert_fusion.7
  751.8 7.1 fusion.35
  760.5 6.0 convolution_add_fusion.5
  769.6 44.4 %collective-permute-done.40 = bf16[384,768]{1,0:T(8,128)(2,1)S(1)} collective-permute-done((bf16[384,768]{1,0:T(8,128)(2,1)}, bf16[384,768]{1,0:T(8,128)(2,1)S(1)}, u32[]{:S(2)}, u32[]{:S(2)}) %collective-permute-start.40) | collective-permute-done | bytes 589856 | tf_op jit(solution)/shard_map/ppermute | solution.py:34
  821.6 3.7 pad_maximum_fusion.2.refs_0_.refs_1_.own_ref
  825.3 18.4 %collective-permute-done.46 = bf16[4,96,1536]{2,1,0:T(8,128)(2,1)S(1)} collective-permute-done((bf16[4,96,1536]{2,1,0:T(8,128)(2,1)S(1)}, bf16[4,96,1536]{2,1,0:T(8,128)(2,1)S(1)}, u32[]{:S(2)}, u32[]{:S(2)}) %collective-permute-start.46) | collective-permute-done | bytes 1179680 | tf_op jit(solution)/shard_map/ppermute | solution.py:34
  855.4 34.1 %collective-permute-done.51 = bf16[512,1536]{1,0:T(8,128)(2,1)S(1)} collective-permute-done((bf16[512,1536]{1,0:T(8,128)(2,1)}, bf16[512,1536]{1,0:T(8,128)(2,1)S(1)}, u32[]{:S(2)}, u32[]{:S(2)}) %collective-permute-start.51) | collective-permute-done | bytes 1572896 | tf_op jit(solution)/shard_map/ppermute | solution.py:56
  894.9 8.9 collective-permute-done.49
  903.9 10.0 %shard_map.340 = f32[1536,1536]{1,0:T(8,128)} custom-call(s32[5]{0:T(128)S(1)} %copy-done.23, bf16[4,384,1536]{2,1,0:T(8,128)(2,1)} %pad_maximum_fusion.2.refs_0_.refs_1_.own_ref, bf16[4,384,1536]{2,1,0:T(8,128)(2,1)} %collective-permute-done.50.refs_2_.refs_3_.other_ref), custom_call_target="tpu_custom_call" | custom-call | tf_op jit(solution)/shard_map/pallas_call | solution.py:565
  914.0 6.2 shard_map.339
  928.0 10.7 %collective-permute-done.59 = bf16[384,768]{1,0:T(8,128)(2,1)S(1)} collective-permute-done((bf16[384,768]{1,0:T(8,128)(2,1)S(1)}, bf16[384,768]{1,0:T(8,128)(2,1)S(1)}, u32[]{:S(2)}, u32[]{:S(2)}) %collective-permute-start.59) | collective-permute-done | bytes 589856 | tf_op jit(solution)/shard_map/ppermute | solution.py:34
  948.0 3.6 shard_map.342
  951.6 4.0 shard_map.341
  956.8 3.8 collective-permute-done.52
  961.4 3.5 collective-permute-done.53
  977.0 6.1 shard_map.344
  983.2 5.9 shard_map.343
  (563 shorter events, 236.6 us)
Async XLA Ops:
  7.2 52.6 %all-gather.8.cloned.1.call-start = ((), (), s32[]{:S(2)}) async-start(), calls=%async_computation.7 | async-start | bytes 2211840 | tf_op jit(solution)/shard_map/all_gather | solution.py:354
  16.6 104.5 %all-gather.10.cloned.1.call-start = ((), (), s32[]{:S(2)}) async-start(), calls=%async_computation.8 | async-start | bytes 3686400 | tf_op jit(solution)/shard_map/all_gather | solution.py:354
  16.7 6.1 collective-permute-start.1
  17.2 44.1 %collective-permute-start = (bf16[512,1536]{1,0:T(8,128)(2,1)S(1)}, bf16[512,1536]{1,0:T(8,128)(2,1)}, u32[]{:S(2)}, u32[]{:S(2)}) collective-permute-start(bf16[512,1536]{1,0:T(8,128)(2,1)S(1)} %bitcast.237), channel_id=1, source_target_pairs={{0,16},{1,17},{2,18},{3,19},{4,20},{5,21},{6,22},{7,23},{8,24},{9,... | collective-permute-start | bytes 4718600 | tf_op jit(solution)/shard_map/ppermute | solution.py:56
  61.3 259.2 %all-gather.6.cloned.1.call-start = ((), (), s32[]{:S(2)}) async-start(), calls=%async_computation.3 | async-start | bytes 10616832 | tf_op jit(solution)/shard_map/all_gather | solution.py:809
  61.4 35.0 %collective-permute-start.4 = (bf16[512,1536]{1,0:T(8,128)(2,1)}, bf16[512,1536]{1,0:T(8,128)(2,1)}, u32[]{:S(2)}, u32[]{:S(2)}) collective-permute-start(bf16[512,1536]{1,0:T(8,128)(2,1)} %collective-permute-done), channel_id=1, source_target_pairs={{0,1},{1,0},{2,3},{3,2},{4,5},{5,4},{6,7},{7,6},{8,9},{9,8},{10,11... | collective-permute-start | bytes 4718600 | tf_op jit(solution)/shard_map/ppermute | solution.py:34
  61.5 32.0 %collective-permute-start.3 = (bf16[3,96,2304]{2,1,0:T(8,128)(2,1)S(1)}, bf16[3,96,2304]{2,1,0:T(8,128)(2,1)S(1)}, u32[]{:S(2)}, u32[]{:S(2)}) collective-permute-start(bf16[3,96,2304]{2,1,0:T(8,128)(2,1)S(1)} %pad_maximum_fusion.29.refs_3_), channel_id=1, source_target_pairs={{0,16},{16,0},{1,17},{17,1},{2,18},{18,2},{3,19},{19,3},{4,20},{20... | collective-permute-start | bytes 3981320 | tf_op jit(solution)/shard_map/ppermute | solution.py:34
  63.0 31.4 %collective-permute-start.2 = (bf16[3,96,2304]{2,1,0:T(8,128)(2,1)S(1)}, bf16[3,96,2304]{2,1,0:T(8,128)(2,1)}, u32[]{:S(2)}, u32[]{:S(2)}) collective-permute-start(bf16[3,96,2304]{2,1,0:T(8,128)(2,1)S(1)} %pad_maximum_fusion.29.refs_3_), channel_id=1, source_target_pairs={{0,2},{2,0},{1,3},{3,1},{4,6},{6,4},{5,7},{7,5},{8,10},{10,8},{9,1... | collective-permute-start | bytes 3981320 | tf_op jit(solution)/shard_map/ppermute | solution.py:34
  65.0 4.5 collective-permute-start.8
  68.3 5.6 collective-permute-start.9
  69.6 57.7 %collective-permute-start.10 = (bf16[512,1536]{1,0:T(8,128)(2,1)}, bf16[512,1536]{1,0:T(8,128)(2,1)}, u32[]{:S(2)}, u32[]{:S(2)}) collective-permute-start(bf16[512,1536]{1,0:T(8,128)(2,1)} %bitcast.244), channel_id=1, source_target_pairs={{0,16},{16,0},{1,17},{17,1},{2,18},{18,2},{3,19},{19,3},{4,20},{20... | collective-permute-start | bytes 4718600 | tf_op jit(solution)/shard_map/ppermute | solution.py:34
  98.7 28.6 %collective-permute-start.5 = (bf16[3,96,1152]{2,1,0:T(8,128)(2,1)}, bf16[3,96,1152]{2,1,0:T(8,128)(2,1)S(1)}, u32[]{:S(2)}, u32[]{:S(2)}) collective-permute-start(bf16[3,96,1152]{2,1,0:T(8,128)(2,1)} %slice.432), channel_id=1, source_target_pairs={{0,2},{2,0},{1,3},{3,1},{4,6},{6,4},{5,7},{7,5},{8,10},{10,8},{9,1... | collective-permute-start | bytes 1990664 | tf_op jit(solution)/shard_map/ppermute | solution.py:34
  100.2 40.8 %collective-permute-start.6 = (bf16[3,96,1152]{2,1,0:T(8,128)(2,1)}, bf16[3,96,1152]{2,1,0:T(8,128)(2,1)}, u32[]{:S(2)}, u32[]{:S(2)}) collective-permute-start(bf16[3,96,1152]{2,1,0:T(8,128)(2,1)} %slice.433), channel_id=1, source_target_pairs={{0,16},{16,0},{1,17},{17,1},{2,18},{18,2},{3,19},{19,3},{4,20},{20... | collective-permute-start | bytes 1990664 | tf_op jit(solution)/shard_map/ppermute | solution.py:34
  141.1 489.2 %reduce-scatter.4.cloned.1.call-start = ((), (), s32[]{:S(2)}) async-start(), calls=%async_computation.4 | async-start | bytes 10616832 | tf_op jit(solution)/shard_map/reduce_scatter | solution.py:876
  141.6 66.5 %collective-permute-start.12 = (bf16[3,96,3840]{2,1,0:T(8,128)(2,1)}, bf16[3,96,3840]{2,1,0:T(8,128)(2,1)S(1)}, u32[]{:S(2)}, u32[]{:S(2)}) collective-permute-start(bf16[3,96,3840]{2,1,0:T(8,128)(2,1)} %pad_maximum_fusion.16.refs_5_), channel_id=1, source_target_pairs={{0,16},{16,0},{1,17},{17,1},{2,18},{18,2},{3,19},{19,3},{4,20},{20... | collective-permute-start | bytes 6635528 | tf_op jit(solution)/shard_map/ppermute | solution.py:34
  143.2 67.1 %collective-permute-start.11 = (bf16[3,96,3840]{2,1,0:T(8,128)(2,1)}, bf16[3,96,3840]{2,1,0:T(8,128)(2,1)}, u32[]{:S(2)}, u32[]{:S(2)}) collective-permute-start(bf16[3,96,3840]{2,1,0:T(8,128)(2,1)} %pad_maximum_fusion.16.refs_5_), channel_id=1, source_target_pairs={{0,2},{2,0},{1,3},{3,1},{4,6},{6,4},{5,7},{7,5},{8,10},{10,8},{9,1... | collective-permute-start | bytes 6635528 | tf_op jit(solution)/shard_map/ppermute | solution.py:34
  211.9 50.1 %collective-permute-start.13 = (bf16[3,96,1920]{2,1,0:T(8,128)(2,1)S(1)}, bf16[3,96,1920]{2,1,0:T(8,128)(2,1)S(1)}, u32[]{:S(2)}, u32[]{:S(2)}) collective-permute-start(bf16[3,96,1920]{2,1,0:T(8,128)(2,1)S(1)} %slice.436), channel_id=1, source_target_pairs={{0,2},{2,0},{1,3},{3,1},{4,6},{6,4},{5,7},{7,5},{8,10},{10,8},{9,1... | collective-permute-start | bytes 3317768 | tf_op jit(solution)/shard_map/ppermute | solution.py:34
  214.1 47.9 %collective-permute-start.14 = (bf16[3,96,1920]{2,1,0:T(8,128)(2,1)S(1)}, bf16[3,96,1920]{2,1,0:T(8,128)(2,1)S(1)}, u32[]{:S(2)}, u32[]{:S(2)}) collective-permute-start(bf16[3,96,1920]{2,1,0:T(8,128)(2,1)S(1)} %slice.437), channel_id=1, source_target_pairs={{0,16},{16,0},{1,17},{17,1},{2,18},{18,2},{3,19},{19,3},{4,20},{20... | collective-permute-start | bytes 3317768 | tf_op jit(solution)/shard_map/ppermute | solution.py:34
  291.5 4.5 collective-permute-start.16
  325.5 12.6 %collective-permute-start.22 = (bf16[512,1536]{1,0:T(8,128)(2,1)S(1)}, bf16[512,1536]{1,0:T(8,128)(2,1)S(1)}, u32[]{:S(2)}, u32[]{:S(2)}) collective-permute-start(bf16[512,1536]{1,0:T(8,128)(2,1)S(1)} %bitcast.245), channel_id=1, source_target_pairs={{0,1},{1,0},{2,3},{3,2},{4,5},{5,4},{6,7},{7,6},{8,9},{9,8},{10,11... | collective-permute-start | bytes 4718600 | tf_op jit(solution)/shard_map/ppermute | solution.py:34
  325.9 38.3 %collective-permute-start.19 = (bf16[512,1536]{1,0:T(8,128)(2,1)}, bf16[512,1536]{1,0:T(8,128)(2,1)S(1)}, u32[]{:S(2)}, u32[]{:S(2)}) collective-permute-start(bf16[512,1536]{1,0:T(8,128)(2,1)} %collective-permute-done.10), channel_id=1, source_target_pairs={{0,1},{1,0},{2,3},{3,2},{4,5},{5,4},{6,7},{7,6},{8,9},{9,8},{10,11... | collective-permute-start | bytes 4718600 | tf_op jit(solution)/shard_map/ppermute | solution.py:34
  326.0 36.7 %collective-permute-start.20 = (bf16[512,1536]{1,0:T(8,128)(2,1)S(1)}, bf16[512,1536]{1,0:T(8,128)(2,1)S(1)}, u32[]{:S(2)}, u32[]{:S(2)}) collective-permute-start(bf16[512,1536]{1,0:T(8,128)(2,1)S(1)} %add_convert_fusion.5), channel_id=1, source_target_pairs={{0,16},{16,0},{1,17},{17,1},{2,18},{18,2},{3,19},{19,3},{4,20},{20... | collective-permute-start | bytes 4718600 | tf_op jit(solution)/shard_map/ppermute | solution.py:34
  362.7 4.4 collective-permute-start.23
  387.5 5.9 collective-permute-start.24
  398.2 46.2 %collective-permute-start.25 = (bf16[512,1536]{1,0:T(8,128)(2,1)}, bf16[512,1536]{1,0:T(8,128)(2,1)}, u32[]{:S(2)}, u32[]{:S(2)}) collective-permute-start(bf16[512,1536]{1,0:T(8,128)(2,1)} %fusion.34), channel_id=1, source_target_pairs={{0,16},{16,0},{1,17},{17,1},{2,18},{18,2},{3,19},{19,3},{4,20},{20... | collective-permute-start | bytes 4718600 | tf_op jit(solution)/shard_map/ppermute | solution.py:34
  442.4 406.5 %reduce-scatter.6.cloned.1.call-start = ((), (), s32[]{:S(2)}) async-start(), calls=%async_computation.5 | async-start | bytes 2949120 | tf_op jit(solution)/shard_map/reduce_scatter | solution.py:459
  451.9 9.5 collective-permute-start.26
  461.2 42.3 %collective-permute-start.32 = (bf16[1024,1536]{1,0:T(8,128)(2,1)S(1)}, bf16[1024,1536]{1,0:T(8,128)(2,1)}, u32[]{:S(2)}, u32[]{:S(2)}) collective-permute-start(bf16[1024,1536]{1,0:T(8,128)(2,1)S(1)} %pad_maximum_fusion.11), channel_id=1, source_target_pairs={{0,1},{1,0},{2,3},{3,2},{4,5},{5,4},{6,7},{7,6},{8,9},{9,8},{10,11... | collective-permute-start | bytes 9437192 | tf_op jit(solution)/shard_map/ppermute | solution.py:34
  480.8 13.1 %collective-permute-start.27 = (bf16[2,64,1536]{2,1,0:T(8,128)(2,1)S(1)}, bf16[2,64,1536]{2,1,0:T(8,128)(2,1)S(1)}, u32[]{:S(2)}, u32[]{:S(2)}) collective-permute-start(bf16[2,64,1536]{2,1,0:T(8,128)(2,1)S(1)} %maximum_bitcast_fusion.3), channel_id=1, source_target_pairs={{0,16},{16,0},{1,17},{17,1},{2,18},{18,2},{3,19},{19,3},{4,20},{20... | collective-permute-start | bytes 1179656 | tf_op jit(solution)/shard_map/ppermute | solution.py:34
  503.4 8.5 collective-permute-start.30
  511.7 37.3 %collective-permute-start.33 = (bf16[512,1536]{1,0:T(8,128)(2,1)S(1)}, bf16[512,1536]{1,0:T(8,128)(2,1)S(1)}, u32[]{:S(2)}, u32[]{:S(2)}) collective-permute-start(bf16[512,1536]{1,0:T(8,128)(2,1)S(1)} %fusion.32), channel_id=1, source_target_pairs={{0,16},{16,0},{1,17},{17,1},{2,18},{18,2},{3,19},{19,3},{4,20},{20... | collective-permute-start | bytes 4718600 | tf_op jit(solution)/shard_map/ppermute | solution.py:34
  517.4 38.4 %collective-permute-start.31 = (bf16[512,1536]{1,0:T(8,128)(2,1)S(1)}, bf16[512,1536]{1,0:T(8,128)(2,1)S(1)}, u32[]{:S(2)}, u32[]{:S(2)}) collective-permute-start(bf16[512,1536]{1,0:T(8,128)(2,1)S(1)} %get-tuple-element.305), channel_id=1, source_target_pairs={{0,1},{1,0},{2,3},{3,2},{4,5},{5,4},{6,7},{7,6},{8,9},{9,8},{10,11... | collective-permute-start | bytes 4718600 | tf_op jit(solution)/shard_map/ppermute | solution.py:34
  520.3 79.0 %collective-permute-start.28 = (bf16[4,2,96,1536]{3,2,0,1:T(8,128)(2,1)S(1)}, bf16[4,2,96,1536]{3,2,0,1:T(8,128)(2,1)}, u32[]{:S(2)}, u32[]{:S(2)}) collective-permute-start(bf16[4,2,96,1536]{3,2,0,1:T(8,128)(2,1)S(1)} %maximum_maximum_fusion.2), channel_id=1, source_target_pairs={{0,16},{16,0},{1,17},{17,1},{2,18},{18,2},{3,19},{19,3},{4,20},{20... | collective-permute-start | bytes 7077896 | tf_op jit(solution)/shard_map/ppermute | solution.py:34
  522.0 84.1 %collective-permute-start.29 = (bf16[4,2,96,1536]{3,2,0,1:T(8,128)(2,1)S(1)}, bf16[4,2,96,1536]{3,2,0,1:T(8,128)(2,1)}, u32[]{:S(2)}, u32[]{:S(2)}) collective-permute-start(bf16[4,2,96,1536]{3,2,0,1:T(8,128)(2,1)S(1)} %maximum_maximum_fusion.3), channel_id=1, source_target_pairs={{0,2},{2,0},{1,3},{3,1},{4,6},{6,4},{5,7},{7,5},{8,10},{10,8},{9,1... | collective-permute-start | bytes 7077896 | tf_op jit(solution)/shard_map/ppermute | solution.py:34
  630.3 93.4 %collective-permute-start.37 = (bf16[384,1536]{1,0:T(8,128)(2,1)}, bf16[384,1536]{1,0:T(8,128)(2,1)}, u32[]{:S(2)}, u32[]{:S(2)}) collective-permute-start(bf16[384,1536]{1,0:T(8,128)(2,1)} %reduce-scatter.4.cloned.1.call-done), channel_id=1, source_target_pairs={{0,16},{16,0},{1,17},{17,1},{2,18},{18,2},{3,19},{19,3},{4,20},{20... | collective-permute-start | bytes 3538952 | tf_op jit(solution)/shard_map/ppermute | solution.py:34
  631.8 97.2 %collective-permute-start.36 = (bf16[384,1536]{1,0:T(8,128)(2,1)}, bf16[384,1536]{1,0:T(8,128)(2,1)}, u32[]{:S(2)}, u32[]{:S(2)}) collective-permute-start(bf16[384,1536]{1,0:T(8,128)(2,1)} %reduce-scatter.4.cloned.1.call-done), channel_id=1, source_target_pairs={{0,2},{2,0},{1,3},{3,1},{4,6},{6,4},{5,7},{7,5},{8,10},{10,8},{9,1... | collective-permute-start | bytes 3538952 | tf_op jit(solution)/shard_map/ppermute | solution.py:34
  694.8 27.4 %collective-permute-start.34 = (bf16[4,96,1536]{2,1,0:T(8,128)(2,1)}, bf16[4,96,1536]{2,1,0:T(8,128)(2,1)}, u32[]{:S(2)}, u32[]{:S(2)}) collective-permute-start(bf16[4,96,1536]{2,1,0:T(8,128)(2,1)} %dynamic-slice_bitcast_fusion.3), channel_id=1, source_target_pairs={{0,2},{2,0},{1,3},{3,1},{4,6},{6,4},{5,7},{7,5},{8,10},{10,8},{9,1... | collective-permute-start | bytes 3538952 | tf_op jit(solution)/shard_map/ppermute | solution.py:34
  698.3 27.4 %collective-permute-start.35 = (bf16[4,96,1536]{2,1,0:T(8,128)(2,1)S(1)}, bf16[4,96,1536]{2,1,0:T(8,128)(2,1)}, u32[]{:S(2)}, u32[]{:S(2)}) collective-permute-start(bf16[4,96,1536]{2,1,0:T(8,128)(2,1)S(1)} %dynamic-slice_bitcast_fusion.2), channel_id=1, source_target_pairs={{0,16},{16,0},{1,17},{17,1},{2,18},{18,2},{3,19},{19,3},{4,20},{20... | collective-permute-start | bytes 3538952 | tf_op jit(solution)/shard_map/ppermute | solution.py:34
  737.5 13.1 %collective-permute-start.44 = (bf16[512,1536]{1,0:T(8,128)(2,1)}, bf16[512,1536]{1,0:T(8,128)(2,1)}, u32[]{:S(2)}, u32[]{:S(2)}) collective-permute-start(bf16[512,1536]{1,0:T(8,128)(2,1)} %convolution_convert_fusion.6), channel_id=1, source_target_pairs={{0,1},{1,0},{2,3},{3,2},{4,5},{5,4},{6,7},{7,6},{8,9},{9,8},{10,11... | collective-permute-start | bytes 4718600 | tf_op jit(solution)/shard_map/ppermute | solution.py:34
  744.3 14.6 %collective-permute-start.43 = (bf16[512,1536]{1,0:T(8,128)(2,1)}, bf16[512,1536]{1,0:T(8,128)(2,1)}, u32[]{:S(2)}, u32[]{:S(2)}) collective-permute-start(bf16[512,1536]{1,0:T(8,128)(2,1)} %convolution_convert_fusion.7), channel_id=1, source_target_pairs={{0,1},{1,0},{2,3},{3,2},{4,5},{5,4},{6,7},{7,6},{8,9},{9,8},{10,11... | collective-permute-start | bytes 4718600 | tf_op jit(solution)/shard_map/ppermute | solution.py:34
  747.2 19.3 %collective-permute-start.42 = (bf16[512,1536]{1,0:T(8,128)(2,1)}, bf16[512,1536]{1,0:T(8,128)(2,1)S(1)}, u32[]{:S(2)}, u32[]{:S(2)}) collective-permute-start(bf16[512,1536]{1,0:T(8,128)(2,1)} %convolution_convert_fusion.8), channel_id=1, source_target_pairs={{0,1},{1,0},{2,3},{3,2},{4,5},{5,4},{6,7},{7,6},{8,9},{9,8},{10,11... | collective-permute-start | bytes 4718600 | tf_op jit(solution)/shard_map/ppermute | solution.py:34
  747.4 66.6 %collective-permute-start.38 = (bf16[4,2,96,1536]{3,2,0,1:T(8,128)(2,1)}, bf16[4,2,96,1536]{3,2,0,1:T(8,128)(2,1)}, u32[]{:S(2)}, u32[]{:S(2)}) collective-permute-start(bf16[4,2,96,1536]{3,2,0,1:T(8,128)(2,1)} %maximum_maximum_fusion.6), channel_id=1, source_target_pairs={{0,16},{16,0},{1,17},{17,1},{2,18},{18,2},{3,19},{19,3},{4,20},{20... | collective-permute-start | bytes 7077896 | tf_op jit(solution)/shard_map/ppermute | solution.py:34
  747.9 66.1 %collective-permute-start.39 = (bf16[4,2,96,1536]{3,2,0,1:T(8,128)(2,1)}, bf16[4,2,96,1536]{3,2,0,1:T(8,128)(2,1)}, u32[]{:S(2)}, u32[]{:S(2)}) collective-permute-start(bf16[4,2,96,1536]{3,2,0,1:T(8,128)(2,1)} %maximum_maximum_fusion.7), channel_id=1, source_target_pairs={{0,2},{2,0},{1,3},{3,1},{4,6},{6,4},{5,7},{7,5},{8,10},{10,8},{9,1... | collective-permute-start | bytes 7077896 | tf_op jit(solution)/shard_map/ppermute | solution.py:34
  750.4 169.8 %reduce-scatter.8.cloned.1.call-start = ((), (), s32[]{:S(2)}) async-start(), calls=%async_computation.6 | async-start | bytes 2949120 | tf_op jit(solution)/shard_map/reduce_scatter | solution.py:459
  750.7 63.3 %collective-permute-start.40 = (bf16[384,768]{1,0:T(8,128)(2,1)}, bf16[384,768]{1,0:T(8,128)(2,1)S(1)}, u32[]{:S(2)}, u32[]{:S(2)}) collective-permute-start(bf16[384,768]{1,0:T(8,128)(2,1)} %slice.476), channel_id=1, source_target_pairs={{0,2},{2,0},{1,3},{3,1},{4,6},{6,4},{5,7},{7,5},{8,10},{10,8},{9,1... | collective-permute-start | bytes 1769480 | tf_op jit(solution)/shard_map/ppermute | solution.py:34
  758.9 55.1 %collective-permute-start.41 = (bf16[384,768]{1,0:T(8,128)(2,1)S(1)}, bf16[384,768]{1,0:T(8,128)(2,1)S(1)}, u32[]{:S(2)}, u32[]{:S(2)}) collective-permute-start(bf16[384,768]{1,0:T(8,128)(2,1)S(1)} %copy-done.77), channel_id=1, source_target_pairs={{0,16},{16,0},{1,17},{17,1},{2,18},{18,2},{3,19},{19,3},{4,20},{20... | collective-permute-start | bytes 1769480 | tf_op jit(solution)/shard_map/ppermute | solution.py:34
  816.4 27.2 %collective-permute-start.46 = (bf16[4,96,1536]{2,1,0:T(8,128)(2,1)S(1)}, bf16[4,96,1536]{2,1,0:T(8,128)(2,1)S(1)}, u32[]{:S(2)}, u32[]{:S(2)}) collective-permute-start(bf16[4,96,1536]{2,1,0:T(8,128)(2,1)S(1)} %dynamic-slice_bitcast_fusion.1), channel_id=1, source_target_pairs={{0,2},{2,0},{1,3},{3,1},{4,6},{6,4},{5,7},{7,5},{8,10},{10,8},{9,1... | collective-permute-start | bytes 3538952 | tf_op jit(solution)/shard_map/ppermute | solution.py:34
  819.9 27.0 %collective-permute-start.47 = (bf16[4,96,1536]{2,1,0:T(8,128)(2,1)S(1)}, bf16[4,96,1536]{2,1,0:T(8,128)(2,1)S(1)}, u32[]{:S(2)}, u32[]{:S(2)}) collective-permute-start(bf16[4,96,1536]{2,1,0:T(8,128)(2,1)S(1)} %dynamic-slice_bitcast_fusion), channel_id=1, source_target_pairs={{0,16},{16,0},{1,17},{17,1},{2,18},{18,2},{3,19},{19,3},{4,20},{20... | collective-permute-start | bytes 3538952 | tf_op jit(solution)/shard_map/ppermute | solution.py:34
  825.3 78.6 %collective-permute-start.50 = (bf16[4,384,1536]{2,1,0:T(8,128)(2,1)}, bf16[4,384,1536]{2,1,0:T(8,128)(2,1)}, u32[]{:S(2)}, u32[]{:S(2)}) collective-permute-start(bf16[4,384,1536]{2,1,0:T(8,128)(2,1)} %pad_maximum_fusion.2.refs_0_.refs_1_.own_ref), channel_id=1, source_target_pairs={{0,1},{1,0},{2,3},{3,2},{4,5},{5,4},{6,7},{7,6},{8,9},{9,8},{10,11... | collective-permute-start | bytes 14155784 | tf_op jit(solution)/shard_map/ppermute | solution.py:34
  852.8 36.8 %collective-permute-start.51 = (bf16[512,1536]{1,0:T(8,128)(2,1)}, bf16[512,1536]{1,0:T(8,128)(2,1)S(1)}, u32[]{:S(2)}, u32[]{:S(2)}) collective-permute-start(bf16[512,1536]{1,0:T(8,128)(2,1)} %fusion.35), channel_id=1, source_target_pairs={{16,0},{17,1},{18,2},{19,3},{20,4},{21,5},{22,6},{23,7},{24,8},{25... | collective-permute-start | bytes 4718600 | tf_op jit(solution)/shard_map/ppermute | solution.py:56
  891.2 12.6 %collective-permute-start.49 = (bf16[384,768]{1,0:T(8,128)(2,1)S(1)}, bf16[384,768]{1,0:T(8,128)(2,1)S(1)}, u32[]{:S(2)}, u32[]{:S(2)}) collective-permute-start(bf16[384,768]{1,0:T(8,128)(2,1)S(1)} %maximum_dynamic-update-slice_fusion.2), channel_id=1, source_target_pairs={{0,16},{16,0},{1,17},{17,1},{2,18},{18,2},{3,19},{19,3},{4,20},{20... | collective-permute-start | bytes 1769480 | tf_op jit(solution)/shard_map/ppermute | solution.py:34
  891.3 12.6 %collective-permute-start.48 = (bf16[384,768]{1,0:T(8,128)(2,1)S(1)}, bf16[384,768]{1,0:T(8,128)(2,1)S(1)}, u32[]{:S(2)}, u32[]{:S(2)}) collective-permute-start(bf16[384,768]{1,0:T(8,128)(2,1)S(1)} %maximum_dynamic-update-slice_fusion.2), channel_id=1, source_target_pairs={{0,2},{2,0},{1,3},{3,1},{4,6},{6,4},{5,7},{7,5},{8,10},{10,8},{9,1... | collective-permute-start | bytes 1769480 | tf_op jit(solution)/shard_map/ppermute | solution.py:34
  923.9 14.8 %collective-permute-start.59 = (bf16[384,768]{1,0:T(8,128)(2,1)S(1)}, bf16[384,768]{1,0:T(8,128)(2,1)S(1)}, u32[]{:S(2)}, u32[]{:S(2)}) collective-permute-start(bf16[384,768]{1,0:T(8,128)(2,1)S(1)} %maximum_dynamic-update-slice_fusion.4), channel_id=1, source_target_pairs={{0,16},{16,0},{1,17},{17,1},{2,18},{18,2},{3,19},{19,3},{4,20},{20... | collective-permute-start | bytes 1769480 | tf_op jit(solution)/shard_map/ppermute | solution.py:34
  925.6 14.2 %collective-permute-start.58 = (bf16[384,768]{1,0:T(8,128)(2,1)S(1)}, bf16[384,768]{1,0:T(8,128)(2,1)S(1)}, u32[]{:S(2)}, u32[]{:S(2)}) collective-permute-start(bf16[384,768]{1,0:T(8,128)(2,1)S(1)} %maximum_dynamic-update-slice_fusion.4), channel_id=1, source_target_pairs={{0,2},{2,0},{1,3},{3,1},{4,6},{6,4},{5,7},{7,5},{8,10},{10,8},{9,1... | collective-permute-start | bytes 1769480 | tf_op jit(solution)/shard_map/ppermute | solution.py:34
  926.6 16.4 %collective-permute-start.60 = (bf16[384,384]{1,0:T(8,128)(2,1)S(1)}, bf16[384,384]{1,0:T(8,128)(2,1)S(1)}, u32[]{:S(2)}, u32[]{:S(2)}) collective-permute-start(bf16[384,384]{1,0:T(8,128)(2,1)S(1)} %slice.488), channel_id=1, source_target_pairs={{0,2},{2,0},{1,3},{3,1},{4,6},{6,4},{5,7},{7,5},{8,10},{10,8},{9,1... | collective-permute-start | bytes 884744 | tf_op jit(solution)/shard_map/ppermute | solution.py:34
  927.7 15.3 %collective-permute-start.61 = (bf16[384,384]{1,0:T(8,128)(2,1)S(1)}, bf16[384,384]{1,0:T(8,128)(2,1)S(1)}, u32[]{:S(2)}, u32[]{:S(2)}) collective-permute-start(bf16[384,384]{1,0:T(8,128)(2,1)S(1)} %slice.489), channel_id=1, source_target_pairs={{0,16},{16,0},{1,17},{17,1},{2,18},{18,2},{3,19},{19,3},{4,20},{20... | collective-permute-start | bytes 884744 | tf_op jit(solution)/shard_map/ppermute | solution.py:34
  943.4 4.6 collective-permute-start.64
  943.4 12.2 %collective-permute-start.62 = (bf16[384,384]{1,0:T(8,128)(2,1)S(1)}, bf16[384,384]{1,0:T(8,128)(2,1)S(1)}, u32[]{:S(2)}, u32[]{:S(2)}) collective-permute-start(bf16[384,384]{1,0:T(8,128)(2,1)S(1)} %slice.500), channel_id=1, source_target_pairs={{0,2},{2,0},{1,3},{3,1},{4,6},{6,4},{5,7},{7,5},{8,10},{10,8},{9,1... | collective-permute-start | bytes 884744 | tf_op jit(solution)/shard_map/ppermute | solution.py:34
  944.5 11.2 %collective-permute-start.63 = (bf16[384,384]{1,0:T(8,128)(2,1)S(1)}, bf16[384,384]{1,0:T(8,128)(2,1)S(1)}, u32[]{:S(2)}, u32[]{:S(2)}) collective-permute-start(bf16[384,384]{1,0:T(8,128)(2,1)S(1)} %slice.501), channel_id=1, source_target_pairs={{0,16},{16,0},{1,17},{17,1},{2,18},{18,2},{3,19},{19,3},{4,20},{20... | collective-permute-start | bytes 884744 | tf_op jit(solution)/shard_map/ppermute | solution.py:34
  956.0 21.0 %collective-permute-start.65 = (bf16[4,384,768]{2,1,0:T(8,128)(2,1)S(1)}, bf16[4,384,768]{2,1,0:T(8,128)(2,1)}, u32[]{:S(2)}, u32[]{:S(2)}) collective-permute-start(bf16[4,384,768]{2,1,0:T(8,128)(2,1)S(1)} %pad_maximum_fusion.15.refs_0_.refs_1_.refs_2_), channel_id=1, source_target_pairs={{0,1},{1,0},{2,3},{3,2},{4,5},{5,4},{6,7},{7,6},{8,9},{9,8},{10,11... | collective-permute-start | bytes 7077896 | tf_op jit(solution)/shard_map/ppermute | solution.py:34
  956.5 4.2 collective-permute-start.52
  969.0 4.5 collective-permute-start.55
  969.2 4.6 collective-permute-start.56
  970.9 5.5 collective-permute-start.57
  (125 other events, 1800.6 us)
Sparse Core Ops, SparseCore 0:
  16.7 42.9 all-gather.7
  61.9 59.1 all-gather.9
  141.2 166.9 all-gather.5
  442.5 187.7 reduce-scatter.3
  750.5 46.8 reduce-scatter.5
  852.9 46.7 reduce-scatter.7

commit v4 on v3

--- a/solution.py
+++ b/solution.py
@@ -545,6 +545,7 @@
                 out_specs=pl.BlockSpec((piece, 4 * columns), lambda y, at: (y, 0)),
             ),
             out_shape=jax.ShapeDtypeStruct((2 * piece, 4 * columns), F32),
+            cost_estimate=pl.CostEstimate(flops=0, bytes_accessed=6 * own.size, transcendentals=0),
             compiler_params=pltpu.CompilerParams(vmem_limit_bytes=VMEM_LIMIT),
         )(self.spot, own, own, other, other)
 
@@ -573,6 +574,7 @@
                 out_specs=pl.BlockSpec((piece, columns), lambda c, p, at: (c * 4 + p, 0)),
             ),
             out_shape=jax.ShapeDtypeStruct((8 * piece, columns), F32),
+            cost_estimate=pl.CostEstimate(flops=0, bytes_accessed=6 * own.size, transcendentals=0),
             compiler_params=pltpu.CompilerParams(vmem_limit_bytes=VMEM_LIMIT),
         )(self.spot, own, other)
 
@@ -963,6 +965,7 @@
         early, late = tied(place.packed(early), place.second_sum(late))
         early, late = place.spread_sides(early), place.shard_sum(late)
         total_up, total_down = place.finish_up(*feed), place.finish_down(*feed)
+        returned, total_up, total_down = tied(returned, total_up, total_down)
     grad_hid, grad_gain_one, grad_shift_one = norm_backward(
         hidden_zero, gain_one, grad_normed + returned.astype(F32)
     )
@@ -973,11 +976,9 @@
     )
     small = place.sum_norms(small)
     if staged:
-        early, late, total_up, total_down, grad_frames = tied(
-            place.spread_parts(early), place.packed(late), total_up, total_down, grad_frames
-        )
+        early, late, grad_frames = tied(place.spread_parts(early), place.packed(late), grad_frames)
         late, early = place.spread_sides(late), place.spread_corners(early)
-        late, early = tied(place.spread_parts(late), early)
+        late, early, small = tied(place.spread_parts(late), early, small)
         late, early = place.spread_corners(late), place.spread_cores(early)
         total_cross_query, total_cross_key, total_cross_value = place.finish_columns(*early, 3)
         total_cross_out = place.finish_rows(*early)

time: 1000 us -> 1010 us (1.010)
    ppermute x2, waiting for transfers between devices: 34.1 us -> 0.01 us  [shifted(): return lax.ppermute(block, axis, route)]
    ppermute x64, waiting for transfers between devices: 302 us -> 335 us  [xor_permute(): lax.ppermute(array, axis, [(i, i ^ bit) for i in range(lax.axis_size(axis...]
    unnamed x264 -> x260, local copies, waits for them, and re-layouts: 26.4 us -> 27.8 us
  transfers between devices with their start and end apart: 72 -> 72, of which waited for: 34 -> 32; matrix products, arithmetic and copies ran while one was open for 26% -> 26% of each run, Pallas kernels for 18% -> 18%
where the time goes in v4:
time: 1010 us; the launch traced here: 999 us
  waiting for transfers between devices  403 us (40%)
  Pallas kernels  191 us (19%)
  matrix products  188 us (19%)
  other arithmetic  85.8 us (8%)
  starting transfers between devices  59.8 us (6%)
  local copies, waits for them, and re-layouts  55.5 us (5%)
  between operations  16.5 us (2%)
    ppermute x64, waiting for transfers between devices, xor_permute(): lax.ppermute(array, axis, [(i, i ^ bit) for i in range(lax.axis_size(axis...  335 us
    dot_general x18, matrix products, against(): lax.dot_general(left, right, (((1,), (1,)), ((), ())), preferred_element_...  84.6 us
    dot_general x14, matrix products, product(): return jnp.dot(left, right, preferred_element_type=F32)  75 us
    ppermute x64, starting transfers between devices, xor_permute(): lax.ppermute(array, axis, [(i, i ^ bit) for i in range(lax.axis_size(axis...  51.7 us
    pallas_call x2, Pallas kernels, attend_back(): pl.pallas_call(lambda *refs: attend_back_kernel(causal, *refs), grid=(cli...  49.8 us
    all_gather x2, waiting for transfers between devices, exchange_z(): return lax.all_gather(mine, 'shard', axis=0, tiled=False)  43.6 us
    pallas_call x2, Pallas kernels, attend(): pl.pallas_call(lambda *refs: attend_kernel(causal, *refs), grid=(clips, p...  41.1 us
    pallas_call x2, Pallas kernels, feed_gradient(): pl.pallas_call(kernel, grid=(4, 2), in_specs=[pl.BlockSpec((each.shape[0]...  35.3 us
  transfers between devices with their start and end apart: 72, of which 32 were waited for; matrix products, arithmetic and copies ran while one was open for 26% of the time, Pallas kernels for 18%

profile of v4, /device:TPU:0, one launch (start us, length us, event | category | flops | bytes accessed | tf_op | source)
XLA Modules:
  0.0 998.7 jit_solution(2294473271405001015)
XLA Ops:
  11.1 4.4 shard_map.330
  17.2 5.6 collective-permute-start
  26.1 33.7 %all-gather.8.cloned.1.call-done = bf16[384,2304]{1,0:T(8,128)(2,1)} async-done(((bf16[96,2304]{1,0:T(8,128)(2,1)}), bf16[384,2304]{1,0:T(8,128)(2,1)}) %all-gather.8.cloned.1.call-update) | async-done | bytes 1769488 | tf_op jit(solution)/shard_map/all_gather | solution.py:354
  70.1 3.8 collective-permute-done.9
  74.1 19.4 %collective-permute-done.3.refs_5_ = bf16[3,96,2304]{2,1,0:T(8,128)(2,1)S(1)} collective-permute-done((bf16[3,96,2304]{2,1,0:T(8,128)(2,1)S(1)}, bf16[3,96,2304]{2,1,0:T(8,128)(2,1)S(1)}, u32[]{:S(2)}, u32[]{:S(2)}) %collective-permute-start.3) | collective-permute-done | bytes 1327136 | tf_op jit(solution)/shard_map/ppermute | solution.py:34
  105.4 5.8 fusion.5
  111.2 9.9 all-gather.10.cloned.1.call-done
  127.3 13.8 %collective-permute-done.6.refs_7_ = bf16[3,96,1152]{2,1,0:T(8,128)(2,1)} collective-permute-done((bf16[3,96,1152]{2,1,0:T(8,128)(2,1)}, bf16[3,96,1152]{2,1,0:T(8,128)(2,1)}, u32[]{:S(2)}, u32[]{:S(2)}) %collective-permute-start.6) | collective-permute-done | bytes 663584 | tf_op jit(solution)/shard_map/ppermute | solution.py:34
  147.3 12.3 %shard_map.331 = (bf16[1536,768]{1,0:T(8,128)(2,1)}, bf16[1536,1536]{1,0:T(8,128)(2,1)}) custom-call(s32[5]{0:T(128)S(1)} %stack.122.at, bf16[384,1536]{1,0:T(8,128)(2,1)S(1)} %copy-done.5, bf16[384,1536]{1,0:T(8,128)(2,1)S(1)} %copy-done.7, bf16[384,1536]{1,0:T(8,128)(2,1)S(1)} %copy-done.9, bf16[3,96,2304]{2,1,0:T(8,128)(2,1)S(1)} %pad_maximum_fusion.29.refs_3_, ...), custom_call_target="tpu_custom_call" | custom-call | tf_op jit(solution)/shard_map/pallas_call | solution.py:411
  159.6 4.4 fusion.71
  164.0 11.8 %convolution_convert_fusion = bf16[2048,1536]{1,0:T(8,128)(2,1)} fusion(bf16[2048,1536]{1,0:T(8,128)(2,1)S(1)} %copy-done.47, bf16[1536,1536]{1,0:T(8,128)(2,1)S(1)} %copy-done.94), kind=kOutput, calls=%fused_computation.11 | convolution fusion | flops 9666822144 | bytes 17301504 | tf_op jit(solution)/shard_map/dot_general | solution.py:22
  175.8 31.6 %shard_map.332 = (bf16[2,512,768]{2,1,0:T(8,128)(2,1)S(1)}, f32[2,6,2,512]{3,2,1,0:T(2,128)S(1)}) custom-call(s32[1]{0:T(128)} %bitcast.14.refs_0_, bf16[2,512,768]{2,1,0:T(8,128)(2,1)S(1)} %bitcast.217, bf16[2,2,512,1536]{3,2,1,0:T(8,128)(2,1)} %bitcast.229, bf16[2,2,512,1536]{3,2,1,0:T(8,128)(2,1)} %bitcast.230), custom_call_target="tpu_custom_call" | custom-call | tf_op jit(solution)/shard_map/pallas_call | solution.py:200
  214.1 47.8 %collective-permute-done.13.refs_8_ = bf16[3,96,1920]{2,1,0:T(8,128)(2,1)S(1)} collective-permute-done((bf16[3,96,1920]{2,1,0:T(8,128)(2,1)S(1)}, bf16[3,96,1920]{2,1,0:T(8,128)(2,1)S(1)}, u32[]{:S(2)}, u32[]{:S(2)}) %collective-permute-start.13) | collective-permute-done | bytes 1105952 | tf_op jit(solution)/shard_map/ppermute | solution.py:34
  262.0 15.9 %shard_map.333 = (bf16[768,1536]{1,0:T(8,128)(2,1)}, bf16[768,1536]{1,0:T(8,128)(2,1)}, bf16[1536,768]{1,0:T(8,128)(2,1)}, bf16[1536,1536]{1,0:T(8,128)(2,1)}) custom-call(s32[5]{0:T(128)S(1)} %stack.122.at, bf16[384,1536]{1,0:T(8,128)(2,1)S(1)} %copy-done.10, bf16[384,1536]{1,0:T(8,128)(2,1)S(1)} %copy-done.11, bf16[384,1536]{1,0:T(8,128)(2,1)S(1)} %copy-done.12, ...), custom_call_target="tpu_custom_call" | custom-call | tf_op jit(solution)/shard_map/pallas_call | solution.py:411
  277.9 4.3 convolution_convert_fusion.15
  282.3 3.7 collective-permute-done.15
  286.0 3.8 fusion.132
  298.6 9.5 shard_map.334
  314.5 6.1 fusion.23
  328.8 9.4 multiply_convert_fusion.1
  338.2 9.8 fusion.11.refs_2_
  348.0 14.7 %collective-permute-done.20 = bf16[512,1536]{1,0:T(8,128)(2,1)S(1)} collective-permute-done((bf16[512,1536]{1,0:T(8,128)(2,1)S(1)}, bf16[512,1536]{1,0:T(8,128)(2,1)S(1)}, u32[]{:S(2)}, u32[]{:S(2)}) %collective-permute-start.20) | collective-permute-done | bytes 1572896 | tf_op jit(solution)/shard_map/ppermute | solution.py:34
  367.2 7.5 multiply_convert_fusion
  374.7 9.9 fusion.17.refs_3_
  394.2 3.9 fusion.34
  400.4 17.3 %shard_map.335.refs_4_ = bf16[4,2,384,1536]{3,2,1,0:T(8,128)(2,1)} custom-call(bf16[1024,1536]{1,0:T(8,128)(2,1)S(1)} %copy-done.13, bf16[1024,1536]{1,0:T(8,128)(2,1)} %get-tuple-element.198.refs_1_, bf16[1024,1536]{1,0:T(8,128)(2,1)} %pad_maximum_fusion.7.refs_2_, bf16[1024,1536]{1,0:T(8,128)(2,1)} %copy-done.45), custom_call_target="tpu_custom_call" | custom-call | tf_op jit(solution)/shard_map/pallas_call | solution.py:507
  417.7 18.0 %shard_map.336 = bf16[4,2,384,1536]{3,2,1,0:T(8,128)(2,1)} custom-call(bf16[1024,1536]{1,0:T(8,128)(2,1)S(1)} %pad_maximum_fusion.6.refs_0_, bf16[1024,1536]{1,0:T(8,128)(2,1)} %copy-done.46, bf16[1024,1536]{1,0:T(8,128)(2,1)} %copy-done.57, bf16[1024,1536]{1,0:T(8,128)(2,1)} %copy-done.59, ...), custom_call_target="tpu_custom_call", output_to_operand_aliasing={{}: (4, {})} | custom-call | tf_op jit(solution)/shard_map/pallas_call | solution.py:507
  435.7 6.6 convolution_add_fusion.6
  444.4 4.5 multiply_reduce_fusion
  452.0 6.2 convolution_convert_fusion.10
  462.5 4.7 fusion.69
  467.2 13.5 %shard_map.337 = (bf16[2,512,768]{2,1,0:T(8,128)(2,1)S(1)}, bf16[1,2,64,768]{3,2,1,0:T(8,128)(2,1)S(1)}, bf16[1,2,64,768]{3,2,1,0:T(8,128)(2,1)S(1)}) custom-call(s32[1]{0:T(128)} %bitcast.14.refs_0_, bf16[2,512,768]{2,1,0:T(8,128)(2,1)S(1)} %bitcast.216, bf16[1,2,64,1536]{3,2,1,0:T(8,128)(2,1)S(1)} %bitcast.213, bf16[1,2,64,1536]{3,2,1,0:T(8,128)(2,1)S(1)} %bitcast.214, ...), custom_call_target="tpu_custom_call" | custom-call | tf_op jit(solution)/shard_map/pallas_call | solution.py:229
  482.5 4.6 convolution_convert_fusion.5
  489.2 3.3 convolution_convert_fusion.4
  506.5 6.3 fusion.32
  526.4 23.8 %collective-permute-done.33 = bf16[512,1536]{1,0:T(8,128)(2,1)S(1)} collective-permute-done((bf16[512,1536]{1,0:T(8,128)(2,1)}, bf16[512,1536]{1,0:T(8,128)(2,1)S(1)}, u32[]{:S(2)}, u32[]{:S(2)}) %collective-permute-start.33) | collective-permute-done | bytes 1572896 | tf_op jit(solution)/shard_map/ppermute | solution.py:34
  550.2 6.7 fusion.33
  563.9 4.7 fusion.70
  568.6 31.9 %collective-permute-done.28 = bf16[4,2,96,1536]{3,2,0,1:T(8,128)(2,1)} collective-permute-done((bf16[4,2,96,1536]{3,2,0,1:T(8,128)(2,1)S(1)}, bf16[4,2,96,1536]{3,2,0,1:T(8,128)(2,1)}, u32[]{:S(2)}, u32[]{:S(2)}) %collective-permute-start.28) | collective-permute-done | bytes 2359328 | tf_op jit(solution)/shard_map/ppermute | solution.py:34
  600.5 6.2 collective-permute-done.29
  606.7 23.6 %reduce-scatter.4.cloned.1.call-done = bf16[384,1536]{1,0:T(8,128)(2,1)} async-done(((bf16[3072,1536]{1,0:T(8,128)(2,1)}), bf16[384,1536]{1,0:T(8,128)(2,1)}) %reduce-scatter.4.cloned.1.call-update) | async-done | bytes 1179664 | tf_op jit(solution)/shard_map/reduce_scatter | solution.py:878
  632.4 36.3 %shard_map.338 = (bf16[2,512,768]{2,1,0:T(8,128)(2,1)S(1)}, bf16[2,2,512,768]{3,2,1,0:T(8,128)(2,1)}, bf16[2,2,512,768]{3,2,1,0:T(8,128)(2,1)}) custom-call(s32[1]{0:T(128)} %bitcast.14.refs_0_, bf16[2,512,768]{2,1,0:T(8,128)(2,1)S(1)} %bitcast.218, bf16[2,2,512,1536]{3,2,1,0:T(8,128)(2,1)} %bitcast.231, bf16[2,2,512,1536]{3,2,1,0:T(8,128)(2,1)} %bitcast.232, ...), custom_call_target="tpu_custom_call" | custom-call | tf_op jit(solution)/shard_map/pallas_call | solution.py:229
  668.8 5.2 convolution_convert_fusion.3
  676.8 10.8 %convolution_convert_fusion.1 = bf16[1536,1536]{1,0:T(8,128)(2,1)S(1)} fusion(bf16[2048,1536]{1,0:T(8,128)(2,1)S(1)} %bitcast.241, bf16[2048,768]{1,0:T(8,128)(2,1)S(1)} %bitcast.259, bf16[2048,768]{1,0:T(8,128)(2,1)S(1)} %bitcast.257), kind=kOutput, calls=%fused_computation.12 | convolution fusion | flops 9678618624 | bytes 17301504 | tf_op jit(solution)/shard_map/dot_general | solution.py:26
  708.6 13.0 %collective-permute-done.34 = bf16[4,96,1536]{2,1,0:T(8,128)(2,1)} collective-permute-done((bf16[4,96,1536]{2,1,0:T(8,128)(2,1)}, bf16[4,96,1536]{2,1,0:T(8,128)(2,1)}, u32[]{:S(2)}, u32[]{:S(2)}) %collective-permute-start.34) | collective-permute-done | bytes 1179680 | tf_op jit(solution)/shard_map/ppermute | solution.py:34
  730.4 6.6 convolution_convert_fusion.6
  737.0 6.7 convolution_convert_fusion.7
  751.5 7.2 fusion.35
  760.0 6.0 convolution_add_fusion.5
  769.1 44.5 %collective-permute-done.40 = bf16[384,768]{1,0:T(8,128)(2,1)S(1)} collective-permute-done((bf16[384,768]{1,0:T(8,128)(2,1)}, bf16[384,768]{1,0:T(8,128)(2,1)S(1)}, u32[]{:S(2)}, u32[]{:S(2)}) %collective-permute-start.40) | collective-permute-done | bytes 589856 | tf_op jit(solution)/shard_map/ppermute | solution.py:34
  821.5 3.7 pad_maximum_fusion.2.refs_0_.refs_1_.own_ref
  825.2 18.1 %collective-permute-done.46 = bf16[4,96,1536]{2,1,0:T(8,128)(2,1)S(1)} collective-permute-done((bf16[4,96,1536]{2,1,0:T(8,128)(2,1)S(1)}, bf16[4,96,1536]{2,1,0:T(8,128)(2,1)S(1)}, u32[]{:S(2)}, u32[]{:S(2)}) %collective-permute-start.46) | collective-permute-done | bytes 1179680 | tf_op jit(solution)/shard_map/ppermute | solution.py:34
  858.6 43.2 %collective-permute-done.49 = bf16[384,768]{1,0:T(8,128)(2,1)S(1)} collective-permute-done((bf16[384,768]{1,0:T(8,128)(2,1)S(1)}, bf16[384,768]{1,0:T(8,128)(2,1)S(1)}, u32[]{:S(2)}, u32[]{:S(2)}) %collective-permute-start.49) | collective-permute-done | bytes 589856 | tf_op jit(solution)/shard_map/ppermute | solution.py:34
  903.3 10.0 %shard_map.340 = f32[1536,1536]{1,0:T(8,128)} custom-call(s32[5]{0:T(128)S(1)} %copy-done.23, bf16[4,384,1536]{2,1,0:T(8,128)(2,1)} %pad_maximum_fusion.2.refs_0_.refs_1_.own_ref, bf16[4,384,1536]{2,1,0:T(8,128)(2,1)} %collective-permute-done.51.refs_2_.refs_3_.other_ref), custom_call_target="tpu_custom_call" | custom-call | bytes 14155776 | tf_op jit(solution)/shard_map/pallas_call | solution.py:566
  913.3 6.5 shard_map.339
  935.4 9.4 collective-permute-done.57
  945.5 3.9 collective-permute-done.58
  950.8 3.3 collective-permute-done.59
  960.3 3.9 collective-permute-done.61
  970.3 3.6 shard_map.342
  973.9 4.0 shard_map.341
  980.2 3.8 collective-permute-done.65.refs_3_.refs_4_.refs_5_.refs_2_
  984.0 3.6 shard_map.344
  987.6 4.0 shard_map.343
  (559 shorter events, 240.2 us)
Async XLA Ops:
  7.2 52.6 %all-gather.8.cloned.1.call-start = ((), (), s32[]{:S(2)}) async-start(), calls=%async_computation.7 | async-start | bytes 2211840 | tf_op jit(solution)/shard_map/all_gather | solution.py:354
  16.6 104.5 %all-gather.10.cloned.1.call-start = ((), (), s32[]{:S(2)}) async-start(), calls=%async_computation.8 | async-start | bytes 3686400 | tf_op jit(solution)/shard_map/all_gather | solution.py:354
  16.7 6.1 collective-permute-start.1
  17.2 44.1 %collective-permute-start = (bf16[512,1536]{1,0:T(8,128)(2,1)S(1)}, bf16[512,1536]{1,0:T(8,128)(2,1)}, u32[]{:S(2)}, u32[]{:S(2)}) collective-permute-start(bf16[512,1536]{1,0:T(8,128)(2,1)S(1)} %bitcast.237), channel_id=1, source_target_pairs={{0,16},{1,17},{2,18},{3,19},{4,20},{5,21},{6,22},{7,23},{8,24},{9,... | collective-permute-start | bytes 4718600 | tf_op jit(solution)/shard_map/ppermute | solution.py:56
  61.3 259.2 %all-gather.6.cloned.1.call-start = ((), (), s32[]{:S(2)}) async-start(), calls=%async_computation.3 | async-start | bytes 10616832 | tf_op jit(solution)/shard_map/all_gather | solution.py:811
  61.4 35.0 %collective-permute-start.4 = (bf16[512,1536]{1,0:T(8,128)(2,1)}, bf16[512,1536]{1,0:T(8,128)(2,1)}, u32[]{:S(2)}, u32[]{:S(2)}) collective-permute-start(bf16[512,1536]{1,0:T(8,128)(2,1)} %collective-permute-done), channel_id=1, source_target_pairs={{0,1},{1,0},{2,3},{3,2},{4,5},{5,4},{6,7},{7,6},{8,9},{9,8},{10,11... | collective-permute-start | bytes 4718600 | tf_op jit(solution)/shard_map/ppermute | solution.py:34
  61.5 32.0 %collective-permute-start.3 = (bf16[3,96,2304]{2,1,0:T(8,128)(2,1)S(1)}, bf16[3,96,2304]{2,1,0:T(8,128)(2,1)S(1)}, u32[]{:S(2)}, u32[]{:S(2)}) collective-permute-start(bf16[3,96,2304]{2,1,0:T(8,128)(2,1)S(1)} %pad_maximum_fusion.29.refs_3_), channel_id=1, source_target_pairs={{0,16},{16,0},{1,17},{17,1},{2,18},{18,2},{3,19},{19,3},{4,20},{20... | collective-permute-start | bytes 3981320 | tf_op jit(solution)/shard_map/ppermute | solution.py:34
  63.0 31.4 %collective-permute-start.2 = (bf16[3,96,2304]{2,1,0:T(8,128)(2,1)S(1)}, bf16[3,96,2304]{2,1,0:T(8,128)(2,1)}, u32[]{:S(2)}, u32[]{:S(2)}) collective-permute-start(bf16[3,96,2304]{2,1,0:T(8,128)(2,1)S(1)} %pad_maximum_fusion.29.refs_3_), channel_id=1, source_target_pairs={{0,2},{2,0},{1,3},{3,1},{4,6},{6,4},{5,7},{7,5},{8,10},{10,8},{9,1... | collective-permute-start | bytes 3981320 | tf_op jit(solution)/shard_map/ppermute | solution.py:34
  65.0 4.5 collective-permute-start.8
  68.3 5.6 collective-permute-start.9
  69.6 57.7 %collective-permute-start.10 = (bf16[512,1536]{1,0:T(8,128)(2,1)}, bf16[512,1536]{1,0:T(8,128)(2,1)}, u32[]{:S(2)}, u32[]{:S(2)}) collective-permute-start(bf16[512,1536]{1,0:T(8,128)(2,1)} %bitcast.244), channel_id=1, source_target_pairs={{0,16},{16,0},{1,17},{17,1},{2,18},{18,2},{3,19},{19,3},{4,20},{20... | collective-permute-start | bytes 4718600 | tf_op jit(solution)/shard_map/ppermute | solution.py:34
  98.7 28.6 %collective-permute-start.5 = (bf16[3,96,1152]{2,1,0:T(8,128)(2,1)}, bf16[3,96,1152]{2,1,0:T(8,128)(2,1)S(1)}, u32[]{:S(2)}, u32[]{:S(2)}) collective-permute-start(bf16[3,96,1152]{2,1,0:T(8,128)(2,1)} %slice.432), channel_id=1, source_target_pairs={{0,2},{2,0},{1,3},{3,1},{4,6},{6,4},{5,7},{7,5},{8,10},{10,8},{9,1... | collective-permute-start | bytes 1990664 | tf_op jit(solution)/shard_map/ppermute | solution.py:34
  100.2 40.8 %collective-permute-start.6 = (bf16[3,96,1152]{2,1,0:T(8,128)(2,1)}, bf16[3,96,1152]{2,1,0:T(8,128)(2,1)}, u32[]{:S(2)}, u32[]{:S(2)}) collective-permute-start(bf16[3,96,1152]{2,1,0:T(8,128)(2,1)} %slice.433), channel_id=1, source_target_pairs={{0,16},{16,0},{1,17},{17,1},{2,18},{18,2},{3,19},{19,3},{4,20},{20... | collective-permute-start | bytes 1990664 | tf_op jit(solution)/shard_map/ppermute | solution.py:34
  141.1 489.2 %reduce-scatter.4.cloned.1.call-start = ((), (), s32[]{:S(2)}) async-start(), calls=%async_computation.4 | async-start | bytes 10616832 | tf_op jit(solution)/shard_map/reduce_scatter | solution.py:878
  141.6 66.4 %collective-permute-start.12 = (bf16[3,96,3840]{2,1,0:T(8,128)(2,1)}, bf16[3,96,3840]{2,1,0:T(8,128)(2,1)S(1)}, u32[]{:S(2)}, u32[]{:S(2)}) collective-permute-start(bf16[3,96,3840]{2,1,0:T(8,128)(2,1)} %pad_maximum_fusion.16.refs_5_), channel_id=1, source_target_pairs={{0,16},{16,0},{1,17},{17,1},{2,18},{18,2},{3,19},{19,3},{4,20},{20... | collective-permute-start | bytes 6635528 | tf_op jit(solution)/shard_map/ppermute | solution.py:34
  143.2 67.1 %collective-permute-start.11 = (bf16[3,96,3840]{2,1,0:T(8,128)(2,1)}, bf16[3,96,3840]{2,1,0:T(8,128)(2,1)}, u32[]{:S(2)}, u32[]{:S(2)}) collective-permute-start(bf16[3,96,3840]{2,1,0:T(8,128)(2,1)} %pad_maximum_fusion.16.refs_5_), channel_id=1, source_target_pairs={{0,2},{2,0},{1,3},{3,1},{4,6},{6,4},{5,7},{7,5},{8,10},{10,8},{9,1... | collective-permute-start | bytes 6635528 | tf_op jit(solution)/shard_map/ppermute | solution.py:34
  211.8 50.1 %collective-permute-start.13 = (bf16[3,96,1920]{2,1,0:T(8,128)(2,1)S(1)}, bf16[3,96,1920]{2,1,0:T(8,128)(2,1)S(1)}, u32[]{:S(2)}, u32[]{:S(2)}) collective-permute-start(bf16[3,96,1920]{2,1,0:T(8,128)(2,1)S(1)} %slice.436), channel_id=1, source_target_pairs={{0,2},{2,0},{1,3},{3,1},{4,6},{6,4},{5,7},{7,5},{8,10},{10,8},{9,1... | collective-permute-start | bytes 3317768 | tf_op jit(solution)/shard_map/ppermute | solution.py:34
  214.1 47.8 %collective-permute-start.14 = (bf16[3,96,1920]{2,1,0:T(8,128)(2,1)S(1)}, bf16[3,96,1920]{2,1,0:T(8,128)(2,1)S(1)}, u32[]{:S(2)}, u32[]{:S(2)}) collective-permute-start(bf16[3,96,1920]{2,1,0:T(8,128)(2,1)S(1)} %slice.437), channel_id=1, source_target_pairs={{0,16},{16,0},{1,17},{17,1},{2,18},{18,2},{3,19},{19,3},{4,20},{20... | collective-permute-start | bytes 3317768 | tf_op jit(solution)/shard_map/ppermute | solution.py:34
  291.5 4.5 collective-permute-start.16
  325.5 12.6 %collective-permute-start.22 = (bf16[512,1536]{1,0:T(8,128)(2,1)S(1)}, bf16[512,1536]{1,0:T(8,128)(2,1)S(1)}, u32[]{:S(2)}, u32[]{:S(2)}) collective-permute-start(bf16[512,1536]{1,0:T(8,128)(2,1)S(1)} %bitcast.245), channel_id=1, source_target_pairs={{0,1},{1,0},{2,3},{3,2},{4,5},{5,4},{6,7},{7,6},{8,9},{9,8},{10,11... | collective-permute-start | bytes 4718600 | tf_op jit(solution)/shard_map/ppermute | solution.py:34
  325.9 38.3 %collective-permute-start.19 = (bf16[512,1536]{1,0:T(8,128)(2,1)}, bf16[512,1536]{1,0:T(8,128)(2,1)S(1)}, u32[]{:S(2)}, u32[]{:S(2)}) collective-permute-start(bf16[512,1536]{1,0:T(8,128)(2,1)} %collective-permute-done.10), channel_id=1, source_target_pairs={{0,1},{1,0},{2,3},{3,2},{4,5},{5,4},{6,7},{7,6},{8,9},{9,8},{10,11... | collective-permute-start | bytes 4718600 | tf_op jit(solution)/shard_map/ppermute | solution.py:34
  326.0 36.7 %collective-permute-start.20 = (bf16[512,1536]{1,0:T(8,128)(2,1)S(1)}, bf16[512,1536]{1,0:T(8,128)(2,1)S(1)}, u32[]{:S(2)}, u32[]{:S(2)}) collective-permute-start(bf16[512,1536]{1,0:T(8,128)(2,1)S(1)} %add_convert_fusion.5), channel_id=1, source_target_pairs={{0,16},{16,0},{1,17},{17,1},{2,18},{18,2},{3,19},{19,3},{4,20},{20... | collective-permute-start | bytes 4718600 | tf_op jit(solution)/shard_map/ppermute | solution.py:34
  362.7 4.4 collective-permute-start.23
  387.5 5.9 collective-permute-start.24
  398.2 46.2 %collective-permute-start.25 = (bf16[512,1536]{1,0:T(8,128)(2,1)}, bf16[512,1536]{1,0:T(8,128)(2,1)}, u32[]{:S(2)}, u32[]{:S(2)}) collective-permute-start(bf16[512,1536]{1,0:T(8,128)(2,1)} %fusion.34), channel_id=1, source_target_pairs={{0,16},{16,0},{1,17},{17,1},{2,18},{18,2},{3,19},{19,3},{4,20},{20... | collective-permute-start | bytes 4718600 | tf_op jit(solution)/shard_map/ppermute | solution.py:34
  442.3 406.5 %reduce-scatter.6.cloned.1.call-start = ((), (), s32[]{:S(2)}) async-start(), calls=%async_computation.5 | async-start | bytes 2949120 | tf_op jit(solution)/shard_map/reduce_scatter | solution.py:459
  451.9 9.5 collective-permute-start.26
  461.1 42.3 %collective-permute-start.32 = (bf16[1024,1536]{1,0:T(8,128)(2,1)S(1)}, bf16[1024,1536]{1,0:T(8,128)(2,1)}, u32[]{:S(2)}, u32[]{:S(2)}) collective-permute-start(bf16[1024,1536]{1,0:T(8,128)(2,1)S(1)} %pad_maximum_fusion.11), channel_id=1, source_target_pairs={{0,1},{1,0},{2,3},{3,2},{4,5},{5,4},{6,7},{7,6},{8,9},{9,8},{10,11... | collective-permute-start | bytes 9437192 | tf_op jit(solution)/shard_map/ppermute | solution.py:34
  480.7 13.1 %collective-permute-start.27 = (bf16[2,64,1536]{2,1,0:T(8,128)(2,1)S(1)}, bf16[2,64,1536]{2,1,0:T(8,128)(2,1)S(1)}, u32[]{:S(2)}, u32[]{:S(2)}) collective-permute-start(bf16[2,64,1536]{2,1,0:T(8,128)(2,1)S(1)} %maximum_bitcast_fusion.3), channel_id=1, source_target_pairs={{0,16},{16,0},{1,17},{17,1},{2,18},{18,2},{3,19},{19,3},{4,20},{20... | collective-permute-start | bytes 1179656 | tf_op jit(solution)/shard_map/ppermute | solution.py:34
  503.4 9.6 collective-permute-start.30
  512.8 37.4 %collective-permute-start.33 = (bf16[512,1536]{1,0:T(8,128)(2,1)}, bf16[512,1536]{1,0:T(8,128)(2,1)S(1)}, u32[]{:S(2)}, u32[]{:S(2)}) collective-permute-start(bf16[512,1536]{1,0:T(8,128)(2,1)} %fusion.32), channel_id=1, source_target_pairs={{0,16},{16,0},{1,17},{17,1},{2,18},{18,2},{3,19},{19,3},{4,20},{20... | collective-permute-start | bytes 4718600 | tf_op jit(solution)/shard_map/ppermute | solution.py:34
  518.0 39.0 %collective-permute-start.31 = (bf16[512,1536]{1,0:T(8,128)(2,1)S(1)}, bf16[512,1536]{1,0:T(8,128)(2,1)S(1)}, u32[]{:S(2)}, u32[]{:S(2)}) collective-permute-start(bf16[512,1536]{1,0:T(8,128)(2,1)S(1)} %get-tuple-element.309), channel_id=1, source_target_pairs={{0,1},{1,0},{2,3},{3,2},{4,5},{5,4},{6,7},{7,6},{8,9},{9,8},{10,11... | collective-permute-start | bytes 4718600 | tf_op jit(solution)/shard_map/ppermute | solution.py:34
  520.7 79.8 %collective-permute-start.28 = (bf16[4,2,96,1536]{3,2,0,1:T(8,128)(2,1)S(1)}, bf16[4,2,96,1536]{3,2,0,1:T(8,128)(2,1)}, u32[]{:S(2)}, u32[]{:S(2)}) collective-permute-start(bf16[4,2,96,1536]{3,2,0,1:T(8,128)(2,1)S(1)} %maximum_maximum_fusion.2), channel_id=1, source_target_pairs={{0,16},{16,0},{1,17},{17,1},{2,18},{18,2},{3,19},{19,3},{4,20},{20... | collective-permute-start | bytes 7077896 | tf_op jit(solution)/shard_map/ppermute | solution.py:34
  522.5 84.2 %collective-permute-start.29 = (bf16[4,2,96,1536]{3,2,0,1:T(8,128)(2,1)S(1)}, bf16[4,2,96,1536]{3,2,0,1:T(8,128)(2,1)}, u32[]{:S(2)}, u32[]{:S(2)}) collective-permute-start(bf16[4,2,96,1536]{3,2,0,1:T(8,128)(2,1)S(1)} %maximum_maximum_fusion.3), channel_id=1, source_target_pairs={{0,2},{2,0},{1,3},{3,1},{4,6},{6,4},{5,7},{7,5},{8,10},{10,8},{9,1... | collective-permute-start | bytes 7077896 | tf_op jit(solution)/shard_map/ppermute | solution.py:34
  630.3 92.9 %collective-permute-start.37 = (bf16[384,1536]{1,0:T(8,128)(2,1)}, bf16[384,1536]{1,0:T(8,128)(2,1)}, u32[]{:S(2)}, u32[]{:S(2)}) collective-permute-start(bf16[384,1536]{1,0:T(8,128)(2,1)} %reduce-scatter.4.cloned.1.call-done), channel_id=1, source_target_pairs={{0,16},{16,0},{1,17},{17,1},{2,18},{18,2},{3,19},{19,3},{4,20},{20... | collective-permute-start | bytes 3538952 | tf_op jit(solution)/shard_map/ppermute | solution.py:34
  631.7 96.7 %collective-permute-start.36 = (bf16[384,1536]{1,0:T(8,128)(2,1)}, bf16[384,1536]{1,0:T(8,128)(2,1)}, u32[]{:S(2)}, u32[]{:S(2)}) collective-permute-start(bf16[384,1536]{1,0:T(8,128)(2,1)} %reduce-scatter.4.cloned.1.call-done), channel_id=1, source_target_pairs={{0,2},{2,0},{1,3},{3,1},{4,6},{6,4},{5,7},{7,5},{8,10},{10,8},{9,1... | collective-permute-start | bytes 3538952 | tf_op jit(solution)/shard_map/ppermute | solution.py:34
  694.3 27.3 %collective-permute-start.34 = (bf16[4,96,1536]{2,1,0:T(8,128)(2,1)}, bf16[4,96,1536]{2,1,0:T(8,128)(2,1)}, u32[]{:S(2)}, u32[]{:S(2)}) collective-permute-start(bf16[4,96,1536]{2,1,0:T(8,128)(2,1)} %dynamic-slice_bitcast_fusion.3), channel_id=1, source_target_pairs={{0,2},{2,0},{1,3},{3,1},{4,6},{6,4},{5,7},{7,5},{8,10},{10,8},{9,1... | collective-permute-start | bytes 3538952 | tf_op jit(solution)/shard_map/ppermute | solution.py:34
  698.2 27.0 %collective-permute-start.35 = (bf16[4,96,1536]{2,1,0:T(8,128)(2,1)S(1)}, bf16[4,96,1536]{2,1,0:T(8,128)(2,1)}, u32[]{:S(2)}, u32[]{:S(2)}) collective-permute-start(bf16[4,96,1536]{2,1,0:T(8,128)(2,1)S(1)} %dynamic-slice_bitcast_fusion.2), channel_id=1, source_target_pairs={{0,16},{16,0},{1,17},{17,1},{2,18},{18,2},{3,19},{19,3},{4,20},{20... | collective-permute-start | bytes 3538952 | tf_op jit(solution)/shard_map/ppermute | solution.py:34
  737.0 13.6 %collective-permute-start.44 = (bf16[512,1536]{1,0:T(8,128)(2,1)}, bf16[512,1536]{1,0:T(8,128)(2,1)}, u32[]{:S(2)}, u32[]{:S(2)}) collective-permute-start(bf16[512,1536]{1,0:T(8,128)(2,1)} %convolution_convert_fusion.6), channel_id=1, source_target_pairs={{0,1},{1,0},{2,3},{3,2},{4,5},{5,4},{6,7},{7,6},{8,9},{9,8},{10,11... | collective-permute-start | bytes 4718600 | tf_op jit(solution)/shard_map/ppermute | solution.py:34
  743.7 15.0 %collective-permute-start.43 = (bf16[512,1536]{1,0:T(8,128)(2,1)}, bf16[512,1536]{1,0:T(8,128)(2,1)}, u32[]{:S(2)}, u32[]{:S(2)}) collective-permute-start(bf16[512,1536]{1,0:T(8,128)(2,1)} %convolution_convert_fusion.7), channel_id=1, source_target_pairs={{0,1},{1,0},{2,3},{3,2},{4,5},{5,4},{6,7},{7,6},{8,9},{9,8},{10,11... | collective-permute-start | bytes 4718600 | tf_op jit(solution)/shard_map/ppermute | solution.py:34
  746.7 19.3 %collective-permute-start.42 = (bf16[512,1536]{1,0:T(8,128)(2,1)}, bf16[512,1536]{1,0:T(8,128)(2,1)S(1)}, u32[]{:S(2)}, u32[]{:S(2)}) collective-permute-start(bf16[512,1536]{1,0:T(8,128)(2,1)} %convolution_convert_fusion.8), channel_id=1, source_target_pairs={{0,1},{1,0},{2,3},{3,2},{4,5},{5,4},{6,7},{7,6},{8,9},{9,8},{10,11... | collective-permute-start | bytes 4718600 | tf_op jit(solution)/shard_map/ppermute | solution.py:34
  746.8 66.8 %collective-permute-start.38 = (bf16[4,2,96,1536]{3,2,0,1:T(8,128)(2,1)}, bf16[4,2,96,1536]{3,2,0,1:T(8,128)(2,1)}, u32[]{:S(2)}, u32[]{:S(2)}) collective-permute-start(bf16[4,2,96,1536]{3,2,0,1:T(8,128)(2,1)} %maximum_maximum_fusion.6), channel_id=1, source_target_pairs={{0,16},{16,0},{1,17},{17,1},{2,18},{18,2},{3,19},{19,3},{4,20},{20... | collective-permute-start | bytes 7077896 | tf_op jit(solution)/shard_map/ppermute | solution.py:34
  747.6 66.1 %collective-permute-start.39 = (bf16[4,2,96,1536]{3,2,0,1:T(8,128)(2,1)}, bf16[4,2,96,1536]{3,2,0,1:T(8,128)(2,1)}, u32[]{:S(2)}, u32[]{:S(2)}) collective-permute-start(bf16[4,2,96,1536]{3,2,0,1:T(8,128)(2,1)} %maximum_maximum_fusion.7), channel_id=1, source_target_pairs={{0,2},{2,0},{1,3},{3,1},{4,6},{6,4},{5,7},{7,5},{8,10},{10,8},{9,1... | collective-permute-start | bytes 7077896 | tf_op jit(solution)/shard_map/ppermute | solution.py:34
  750.4 173.8 %reduce-scatter.8.cloned.1.call-start = ((), (), s32[]{:S(2)}) async-start(), calls=%async_computation.6 | async-start | bytes 2949120 | tf_op jit(solution)/shard_map/reduce_scatter | solution.py:459
  750.6 63.0 %collective-permute-start.40 = (bf16[384,768]{1,0:T(8,128)(2,1)}, bf16[384,768]{1,0:T(8,128)(2,1)S(1)}, u32[]{:S(2)}, u32[]{:S(2)}) collective-permute-start(bf16[384,768]{1,0:T(8,128)(2,1)} %slice.476), channel_id=1, source_target_pairs={{0,2},{2,0},{1,3},{3,1},{4,6},{6,4},{5,7},{7,5},{8,10},{10,8},{9,1... | collective-permute-start | bytes 1769480 | tf_op jit(solution)/shard_map/ppermute | solution.py:34
  758.7 54.9 %collective-permute-start.41 = (bf16[384,768]{1,0:T(8,128)(2,1)S(1)}, bf16[384,768]{1,0:T(8,128)(2,1)S(1)}, u32[]{:S(2)}, u32[]{:S(2)}) collective-permute-start(bf16[384,768]{1,0:T(8,128)(2,1)S(1)} %copy-done.77), channel_id=1, source_target_pairs={{0,16},{16,0},{1,17},{17,1},{2,18},{18,2},{3,19},{19,3},{4,20},{20... | collective-permute-start | bytes 1769480 | tf_op jit(solution)/shard_map/ppermute | solution.py:34
  816.1 27.2 %collective-permute-start.46 = (bf16[4,96,1536]{2,1,0:T(8,128)(2,1)S(1)}, bf16[4,96,1536]{2,1,0:T(8,128)(2,1)S(1)}, u32[]{:S(2)}, u32[]{:S(2)}) collective-permute-start(bf16[4,96,1536]{2,1,0:T(8,128)(2,1)S(1)} %dynamic-slice_bitcast_fusion.1), channel_id=1, source_target_pairs={{0,2},{2,0},{1,3},{3,1},{4,6},{6,4},{5,7},{7,5},{8,10},{10,8},{9,1... | collective-permute-start | bytes 3538952 | tf_op jit(solution)/shard_map/ppermute | solution.py:34
  819.8 26.9 %collective-permute-start.47 = (bf16[4,96,1536]{2,1,0:T(8,128)(2,1)S(1)}, bf16[4,96,1536]{2,1,0:T(8,128)(2,1)S(1)}, u32[]{:S(2)}, u32[]{:S(2)}) collective-permute-start(bf16[4,96,1536]{2,1,0:T(8,128)(2,1)S(1)} %dynamic-slice_bitcast_fusion), channel_id=1, source_target_pairs={{0,16},{16,0},{1,17},{17,1},{2,18},{18,2},{3,19},{19,3},{4,20},{20... | collective-permute-start | bytes 3538952 | tf_op jit(solution)/shard_map/ppermute | solution.py:34
  825.2 78.1 %collective-permute-start.51 = (bf16[4,384,1536]{2,1,0:T(8,128)(2,1)}, bf16[4,384,1536]{2,1,0:T(8,128)(2,1)}, u32[]{:S(2)}, u32[]{:S(2)}) collective-permute-start(bf16[4,384,1536]{2,1,0:T(8,128)(2,1)} %pad_maximum_fusion.2.refs_0_.refs_1_.own_ref), channel_id=1, source_target_pairs={{0,1},{1,0},{2,3},{3,2},{4,5},{5,4},{6,7},{7,6},{8,9},{9,8},{10,11... | collective-permute-start | bytes 14155784 | tf_op jit(solution)/shard_map/ppermute | solution.py:34
  852.7 67.1 %collective-permute-start.50 = (bf16[512,1536]{1,0:T(8,128)(2,1)}, bf16[512,1536]{1,0:T(8,128)(2,1)S(1)}, u32[]{:S(2)}, u32[]{:S(2)}) collective-permute-start(bf16[512,1536]{1,0:T(8,128)(2,1)} %fusion.35), channel_id=1, source_target_pairs={{16,0},{17,1},{18,2},{19,3},{20,4},{21,5},{22,6},{23,7},{24,8},{25... | collective-permute-start | bytes 4718600 | tf_op jit(solution)/shard_map/ppermute | solution.py:56
  854.5 47.3 %collective-permute-start.49 = (bf16[384,768]{1,0:T(8,128)(2,1)S(1)}, bf16[384,768]{1,0:T(8,128)(2,1)S(1)}, u32[]{:S(2)}, u32[]{:S(2)}) collective-permute-start(bf16[384,768]{1,0:T(8,128)(2,1)S(1)} %maximum_dynamic-update-slice_fusion.2), channel_id=1, source_target_pairs={{0,16},{16,0},{1,17},{17,1},{2,18},{18,2},{3,19},{19,3},{4,20},{20... | collective-permute-start | bytes 1769480 | tf_op jit(solution)/shard_map/ppermute | solution.py:34
  857.3 45.3 %collective-permute-start.48 = (bf16[384,768]{1,0:T(8,128)(2,1)S(1)}, bf16[384,768]{1,0:T(8,128)(2,1)S(1)}, u32[]{:S(2)}, u32[]{:S(2)}) collective-permute-start(bf16[384,768]{1,0:T(8,128)(2,1)S(1)} %maximum_dynamic-update-slice_fusion.2), channel_id=1, source_target_pairs={{0,2},{2,0},{1,3},{3,1},{4,6},{6,4},{5,7},{7,5},{8,10},{10,8},{9,1... | collective-permute-start | bytes 1769480 | tf_op jit(solution)/shard_map/ppermute | solution.py:34
  931.1 33.1 %collective-permute-start.53 = (bf16[384,768]{1,0:T(8,128)(2,1)}, bf16[384,768]{1,0:T(8,128)(2,1)S(1)}, u32[]{:S(2)}, u32[]{:S(2)}) collective-permute-start(bf16[384,768]{1,0:T(8,128)(2,1)} %maximum_dynamic-update-slice_fusion.4), channel_id=1, source_target_pairs={{0,16},{16,0},{1,17},{17,1},{2,18},{18,2},{3,19},{19,3},{4,20},{20... | collective-permute-start | bytes 1769480 | tf_op jit(solution)/shard_map/ppermute | solution.py:34
  931.1 33.1 %collective-permute-start.52 = (bf16[384,768]{1,0:T(8,128)(2,1)}, bf16[384,768]{1,0:T(8,128)(2,1)S(1)}, u32[]{:S(2)}, u32[]{:S(2)}) collective-permute-start(bf16[384,768]{1,0:T(8,128)(2,1)} %maximum_dynamic-update-slice_fusion.4), channel_id=1, source_target_pairs={{0,2},{2,0},{1,3},{3,1},{4,6},{6,4},{5,7},{7,5},{8,10},{10,8},{9,1... | collective-permute-start | bytes 1769480 | tf_op jit(solution)/shard_map/ppermute | solution.py:34
  933.3 11.4 %collective-permute-start.57 = (f32[6,1536]{1,0:T(8,128)S(1)}, f32[6,1536]{1,0:T(8,128)S(1)}, u32[]{:S(2)}, u32[]{:S(2)}) collective-permute-start(f32[6,1536]{1,0:T(8,128)S(1)} %add.343), channel_id=1, source_target_pairs={{0,16},{16,0},{1,17},{17,1},{2,18},{18,2},{3,19},{19,3},{4,20},{20... | collective-permute-start | bytes 110600 | tf_op jit(solution)/shard_map/ppermute | solution.py:34
  944.8 4.7 collective-permute-start.58
  949.5 14.8 %collective-permute-start.54 = (bf16[384,384]{1,0:T(8,128)(2,1)}, bf16[384,384]{1,0:T(8,128)(2,1)}, u32[]{:S(2)}, u32[]{:S(2)}) collective-permute-start(bf16[384,384]{1,0:T(8,128)(2,1)} %slice.488), channel_id=1, source_target_pairs={{0,2},{2,0},{1,3},{3,1},{4,6},{6,4},{5,7},{7,5},{8,10},{10,8},{9,1... | collective-permute-start | bytes 884744 | tf_op jit(solution)/shard_map/ppermute | solution.py:34
  950.2 14.1 %collective-permute-start.55 = (bf16[384,384]{1,0:T(8,128)(2,1)}, bf16[384,384]{1,0:T(8,128)(2,1)}, u32[]{:S(2)}, u32[]{:S(2)}) collective-permute-start(bf16[384,384]{1,0:T(8,128)(2,1)} %slice.489), channel_id=1, source_target_pairs={{0,16},{16,0},{1,17},{17,1},{2,18},{18,2},{3,19},{19,3},{4,20},{20... | collective-permute-start | bytes 884744 | tf_op jit(solution)/shard_map/ppermute | solution.py:34
  954.1 4.6 collective-permute-start.60
  958.7 5.5 collective-permute-start.61
  965.7 4.6 collective-permute-start.64
  965.8 12.2 %collective-permute-start.62 = (bf16[384,384]{1,0:T(8,128)(2,1)S(1)}, bf16[384,384]{1,0:T(8,128)(2,1)S(1)}, u32[]{:S(2)}, u32[]{:S(2)}) collective-permute-start(bf16[384,384]{1,0:T(8,128)(2,1)S(1)} %slice.498), channel_id=1, source_target_pairs={{0,2},{2,0},{1,3},{3,1},{4,6},{6,4},{5,7},{7,5},{8,10},{10,8},{9,1... | collective-permute-start | bytes 884744 | tf_op jit(solution)/shard_map/ppermute | solution.py:34
  967.2 10.8 %collective-permute-start.63 = (bf16[384,384]{1,0:T(8,128)(2,1)S(1)}, bf16[384,384]{1,0:T(8,128)(2,1)S(1)}, u32[]{:S(2)}, u32[]{:S(2)}) collective-permute-start(bf16[384,384]{1,0:T(8,128)(2,1)S(1)} %slice.499), channel_id=1, source_target_pairs={{0,16},{16,0},{1,17},{17,1},{2,18},{18,2},{3,19},{19,3},{4,20},{20... | collective-permute-start | bytes 884744 | tf_op jit(solution)/shard_map/ppermute | solution.py:34
  979.4 4.6 collective-permute-start.65
  (123 other events, 1759.5 us)
Sparse Core Ops, SparseCore 0:
  16.7 42.9 all-gather.7
  61.9 59.1 all-gather.9
  141.2 166.9 all-gather.5
  442.5 187.7 reduce-scatter.3
  750.5 46.2 reduce-scatter.5
  852.8 46.1 reduce-scatter.7

commit v5 on v4

--- a/solution.py
+++ b/solution.py
@@ -545,7 +545,6 @@
                 out_specs=pl.BlockSpec((piece, 4 * columns), lambda y, at: (y, 0)),
             ),
             out_shape=jax.ShapeDtypeStruct((2 * piece, 4 * columns), F32),
-            cost_estimate=pl.CostEstimate(flops=0, bytes_accessed=6 * own.size, transcendentals=0),
             compiler_params=pltpu.CompilerParams(vmem_limit_bytes=VMEM_LIMIT),
         )(self.spot, own, own, other, other)
 
@@ -574,7 +573,6 @@
                 out_specs=pl.BlockSpec((piece, columns), lambda c, p, at: (c * 4 + p, 0)),
             ),
             out_shape=jax.ShapeDtypeStruct((8 * piece, columns), F32),
-            cost_estimate=pl.CostEstimate(flops=0, bytes_accessed=6 * own.size, transcendentals=0),
             compiler_params=pltpu.CompilerParams(vmem_limit_bytes=VMEM_LIMIT),
         )(self.spot, own, other)
 
@@ -965,7 +963,6 @@
         early, late = tied(place.packed(early), place.second_sum(late))
         early, late = place.spread_sides(early), place.shard_sum(late)
         total_up, total_down = place.finish_up(*feed), place.finish_down(*feed)
-        returned, total_up, total_down = tied(returned, total_up, total_down)
     grad_hid, grad_gain_one, grad_shift_one = norm_backward(
         hidden_zero, gain_one, grad_normed + returned.astype(F32)
     )
@@ -978,7 +975,9 @@
     if staged:
         early, late, grad_frames = tied(place.spread_parts(early), place.packed(late), grad_frames)
         late, early = place.spread_sides(late), place.spread_corners(early)
-        late, early, small = tied(place.spread_parts(late), early, small)
+        late, early, total_up, total_down, small = tied(
+            place.spread_parts(late), early, total_up, total_down, small
+        )
         late, early = place.spread_corners(late), place.spread_cores(early)
         total_cross_query, total_cross_key, total_cross_value = place.finish_columns(*early, 3)
         total_cross_out = place.finish_rows(*early)

time: 1010 us -> 1000 us (0.990)
    ppermute x64, waiting for transfers between devices: 335 us -> 295 us  [xor_permute(): lax.ppermute(array, axis, [(i, i ^ bit) for i in range(lax.axis_size(axis...]
    ppermute x2, waiting for transfers between devices: 0.01 us -> 30 us  [shifted(): return lax.ppermute(block, axis, route)]
    unnamed x260 -> x270, local copies, waits for them, and re-layouts: 27.8 us -> 27.4 us
  transfers between devices with their start and end apart: 72 -> 72, of which waited for: 32 -> 32; matrix products, arithmetic and copies ran while one was open for 26% -> 27% of each run, Pallas kernels for 18% -> 18%
where the time goes in v5:
time: 1000 us; the launch traced here: 994 us
  waiting for transfers between devices  393 us (39%)
  Pallas kernels  191 us (19%)
  matrix products  187 us (19%)
  other arithmetic  86.9 us (9%)
  local copies, waits for them, and re-layouts  63.8 us (6%)
  starting transfers between devices  56.7 us (6%)
  between operations  16.6 us (2%)
    ppermute x64, waiting for transfers between devices, xor_permute(): lax.ppermute(array, axis, [(i, i ^ bit) for i in range(lax.axis_size(axis...  295 us
    dot_general x18, matrix products, against(): lax.dot_general(left, right, (((1,), (1,)), ((), ())), preferred_element_...  85 us
    dot_general x14, matrix products, product(): return jnp.dot(left, right, preferred_element_type=F32)  74.1 us
    pallas_call x2, Pallas kernels, attend_back(): pl.pallas_call(lambda *refs: attend_back_kernel(causal, *refs), grid=(cli...  50 us
    ppermute x64, starting transfers between devices, xor_permute(): lax.ppermute(array, axis, [(i, i ^ bit) for i in range(lax.axis_size(axis...  48.8 us
    all_gather x2, waiting for transfers between devices, exchange_z(): return lax.all_gather(mine, 'shard', axis=0, tiled=False)  43.6 us
    pallas_call x2, Pallas kernels, attend(): pl.pallas_call(lambda *refs: attend_kernel(causal, *refs), grid=(clips, p...  41.1 us
    pallas_call x2, Pallas kernels, feed_gradient(): pl.pallas_call(kernel, grid=(4, 2), in_specs=[pl.BlockSpec((each.shape[0]...  35.3 us
  transfers between devices with their start and end apart: 72, of which 32 were waited for; matrix products, arithmetic and copies ran while one was open for 27% of the time, Pallas kernels for 18%

profile of v5, /device:TPU:0, one launch (start us, length us, event | category | flops | bytes accessed | tf_op | source)
XLA Modules:
  0.0 994.4 jit_solution(139818625263828006)
XLA Ops:
  11.1 4.4 shard_map.330
  17.2 5.6 collective-permute-start
  22.8 3.3 pad_maximum_fusion.3
  26.1 33.7 %all-gather.8.cloned.1.call-done = bf16[384,2304]{1,0:T(8,128)(2,1)} async-done(((bf16[96,2304]{1,0:T(8,128)(2,1)}), bf16[384,2304]{1,0:T(8,128)(2,1)}) %all-gather.8.cloned.1.call-update) | async-done | bytes 1769488 | tf_op jit(solution)/shard_map/all_gather | solution.py:354
  70.1 3.8 collective-permute-done.9
  74.1 19.4 %collective-permute-done.3.refs_5_ = bf16[3,96,2304]{2,1,0:T(8,128)(2,1)S(1)} collective-permute-done((bf16[3,96,2304]{2,1,0:T(8,128)(2,1)S(1)}, bf16[3,96,2304]{2,1,0:T(8,128)(2,1)S(1)}, u32[]{:S(2)}, u32[]{:S(2)}) %collective-permute-start.3) | collective-permute-done | bytes 1327136 | tf_op jit(solution)/shard_map/ppermute | solution.py:34
  105.4 5.8 fusion.5
  111.2 9.9 all-gather.10.cloned.1.call-done
  127.3 13.8 %collective-permute-done.6.refs_7_ = bf16[3,96,1152]{2,1,0:T(8,128)(2,1)} collective-permute-done((bf16[3,96,1152]{2,1,0:T(8,128)(2,1)}, bf16[3,96,1152]{2,1,0:T(8,128)(2,1)}, u32[]{:S(2)}, u32[]{:S(2)}) %collective-permute-start.6) | collective-permute-done | bytes 663584 | tf_op jit(solution)/shard_map/ppermute | solution.py:34
  147.0 12.4 %shard_map.331 = (bf16[1536,768]{1,0:T(8,128)(2,1)}, bf16[1536,1536]{1,0:T(8,128)(2,1)}) custom-call(s32[5]{0:T(128)S(1)} %stack.122.at, bf16[384,1536]{1,0:T(8,128)(2,1)S(1)} %copy-done.5, bf16[384,1536]{1,0:T(8,128)(2,1)S(1)} %copy-done.7, bf16[384,1536]{1,0:T(8,128)(2,1)S(1)} %copy-done.9, bf16[3,96,2304]{2,1,0:T(8,128)(2,1)S(1)} %pad_maximum_fusion.29.refs_3_, ...), custom_call_target="tpu_custom_call" | custom-call | tf_op jit(solution)/shard_map/pallas_call | solution.py:411
  159.3 4.4 fusion.71
  163.8 11.8 %convolution_convert_fusion = bf16[2048,1536]{1,0:T(8,128)(2,1)} fusion(bf16[2048,1536]{1,0:T(8,128)(2,1)S(1)} %copy-done.47, bf16[1536,1536]{1,0:T(8,128)(2,1)S(1)} %copy-done.99), kind=kOutput, calls=%fused_computation.11 | convolution fusion | flops 9666822144 | bytes 17301504 | tf_op jit(solution)/shard_map/dot_general | solution.py:22
  175.6 31.6 %shard_map.332 = (bf16[2,512,768]{2,1,0:T(8,128)(2,1)S(1)}, f32[2,6,2,512]{3,2,1,0:T(2,128)S(1)}) custom-call(s32[1]{0:T(128)} %bitcast.14.refs_0_, bf16[2,512,768]{2,1,0:T(8,128)(2,1)S(1)} %bitcast.217, bf16[2,2,512,1536]{3,2,1,0:T(8,128)(2,1)} %bitcast.229, bf16[2,2,512,1536]{3,2,1,0:T(8,128)(2,1)} %bitcast.230), custom_call_target="tpu_custom_call" | custom-call | tf_op jit(solution)/shard_map/pallas_call | solution.py:200
  213.7 47.9 %collective-permute-done.13.refs_8_ = bf16[3,96,1920]{2,1,0:T(8,128)(2,1)S(1)} collective-permute-done((bf16[3,96,1920]{2,1,0:T(8,128)(2,1)S(1)}, bf16[3,96,1920]{2,1,0:T(8,128)(2,1)S(1)}, u32[]{:S(2)}, u32[]{:S(2)}) %collective-permute-start.13) | collective-permute-done | bytes 1105952 | tf_op jit(solution)/shard_map/ppermute | solution.py:34
  261.7 16.3 %shard_map.333 = (bf16[768,1536]{1,0:T(8,128)(2,1)}, bf16[768,1536]{1,0:T(8,128)(2,1)}, bf16[1536,768]{1,0:T(8,128)(2,1)}, bf16[1536,1536]{1,0:T(8,128)(2,1)}) custom-call(s32[5]{0:T(128)S(1)} %stack.122.at, bf16[384,1536]{1,0:T(8,128)(2,1)S(1)} %copy-done.10, bf16[384,1536]{1,0:T(8,128)(2,1)S(1)} %copy-done.11, bf16[384,1536]{1,0:T(8,128)(2,1)S(1)} %copy-done.12, ...), custom_call_target="tpu_custom_call" | custom-call | tf_op jit(solution)/shard_map/pallas_call | solution.py:411
  277.9 4.3 convolution_convert_fusion.15
  282.3 3.7 collective-permute-done.15
  286.0 3.8 fusion.132
  298.7 9.5 shard_map.334
  314.5 6.1 fusion.23
  328.8 9.3 multiply_convert_fusion.1
  338.2 9.6 fusion.11.refs_2_
  347.8 15.0 %collective-permute-done.20 = bf16[512,1536]{1,0:T(8,128)(2,1)S(1)} collective-permute-done((bf16[512,1536]{1,0:T(8,128)(2,1)S(1)}, bf16[512,1536]{1,0:T(8,128)(2,1)S(1)}, u32[]{:S(2)}, u32[]{:S(2)}) %collective-permute-start.20) | collective-permute-done | bytes 1572896 | tf_op jit(solution)/shard_map/ppermute | solution.py:34
  367.3 7.5 multiply_convert_fusion
  374.8 9.9 fusion.17.refs_3_
  394.3 4.2 fusion.34
  400.8 17.3 %shard_map.335.refs_4_ = bf16[4,2,384,1536]{3,2,1,0:T(8,128)(2,1)} custom-call(bf16[1024,1536]{1,0:T(8,128)(2,1)S(1)} %copy-done.13, bf16[1024,1536]{1,0:T(8,128)(2,1)} %get-tuple-element.197.refs_1_, bf16[1024,1536]{1,0:T(8,128)(2,1)} %pad_maximum_fusion.7.refs_2_, bf16[1024,1536]{1,0:T(8,128)(2,1)} %copy-done.45), custom_call_target="tpu_custom_call" | custom-call | tf_op jit(solution)/shard_map/pallas_call | solution.py:507
  418.1 18.0 %shard_map.336 = bf16[4,2,384,1536]{3,2,1,0:T(8,128)(2,1)} custom-call(bf16[1024,1536]{1,0:T(8,128)(2,1)S(1)} %pad_maximum_fusion.6.refs_0_, bf16[1024,1536]{1,0:T(8,128)(2,1)} %copy-done.46, bf16[1024,1536]{1,0:T(8,128)(2,1)} %copy-done.57, bf16[1024,1536]{1,0:T(8,128)(2,1)} %copy-done.59, ...), custom_call_target="tpu_custom_call", output_to_operand_aliasing={{}: (4, {})} | custom-call | tf_op jit(solution)/shard_map/pallas_call | solution.py:507
  436.2 6.6 convolution_add_fusion.6
  444.9 4.5 multiply_reduce_fusion
  452.5 6.2 convolution_convert_fusion.10
  463.0 4.7 fusion.69
  467.7 13.5 %shard_map.337 = (bf16[2,512,768]{2,1,0:T(8,128)(2,1)S(1)}, bf16[1,2,64,768]{3,2,1,0:T(8,128)(2,1)S(1)}, bf16[1,2,64,768]{3,2,1,0:T(8,128)(2,1)S(1)}) custom-call(s32[1]{0:T(128)} %bitcast.14.refs_0_, bf16[2,512,768]{2,1,0:T(8,128)(2,1)S(1)} %bitcast.216, bf16[1,2,64,1536]{3,2,1,0:T(8,128)(2,1)S(1)} %bitcast.213, bf16[1,2,64,1536]{3,2,1,0:T(8,128)(2,1)S(1)} %bitcast.214, ...), custom_call_target="tpu_custom_call" | custom-call | tf_op jit(solution)/shard_map/pallas_call | solution.py:229
  482.9 4.6 convolution_convert_fusion.5
  506.6 5.2 fusion.32
  525.9 23.2 %collective-permute-done.33 = bf16[512,1536]{1,0:T(8,128)(2,1)S(1)} collective-permute-done((bf16[512,1536]{1,0:T(8,128)(2,1)S(1)}, bf16[512,1536]{1,0:T(8,128)(2,1)S(1)}, u32[]{:S(2)}, u32[]{:S(2)}) %collective-permute-start.33) | collective-permute-done | bytes 1572896 | tf_op jit(solution)/shard_map/ppermute | solution.py:34
  549.1 6.9 fusion.33
  563.0 4.7 fusion.70
  567.7 31.6 %collective-permute-done.28 = bf16[4,2,96,1536]{3,2,0,1:T(8,128)(2,1)} collective-permute-done((bf16[4,2,96,1536]{3,2,0,1:T(8,128)(2,1)S(1)}, bf16[4,2,96,1536]{3,2,0,1:T(8,128)(2,1)}, u32[]{:S(2)}, u32[]{:S(2)}) %collective-permute-start.28) | collective-permute-done | bytes 2359328 | tf_op jit(solution)/shard_map/ppermute | solution.py:34
  599.3 6.8 collective-permute-done.29
  606.1 24.3 %reduce-scatter.4.cloned.1.call-done = bf16[384,1536]{1,0:T(8,128)(2,1)} async-done(((bf16[3072,1536]{1,0:T(8,128)(2,1)}), bf16[384,1536]{1,0:T(8,128)(2,1)}) %reduce-scatter.4.cloned.1.call-update) | async-done | bytes 1179664 | tf_op jit(solution)/shard_map/reduce_scatter | solution.py:876
  633.0 36.6 %shard_map.338 = (bf16[2,512,768]{2,1,0:T(8,128)(2,1)S(1)}, bf16[2,2,512,768]{3,2,1,0:T(8,128)(2,1)}, bf16[2,2,512,768]{3,2,1,0:T(8,128)(2,1)}) custom-call(s32[1]{0:T(128)} %bitcast.14.refs_0_, bf16[2,512,768]{2,1,0:T(8,128)(2,1)S(1)} %bitcast.218, bf16[2,2,512,1536]{3,2,1,0:T(8,128)(2,1)} %bitcast.231, bf16[2,2,512,1536]{3,2,1,0:T(8,128)(2,1)} %bitcast.232, ...), custom_call_target="tpu_custom_call" | custom-call | tf_op jit(solution)/shard_map/pallas_call | solution.py:229
  669.6 5.2 convolution_convert_fusion.3
  677.6 10.6 %convolution_convert_fusion.1 = bf16[1536,1536]{1,0:T(8,128)(2,1)S(1)} fusion(bf16[2048,1536]{1,0:T(8,128)(2,1)S(1)} %bitcast.241, bf16[2048,768]{1,0:T(8,128)(2,1)S(1)} %bitcast.259, bf16[2048,768]{1,0:T(8,128)(2,1)S(1)} %bitcast.257), kind=kOutput, calls=%fused_computation.12 | convolution fusion | flops 9678618624 | bytes 17301504 | tf_op jit(solution)/shard_map/dot_general | solution.py:26
  705.6 3.2 pad_maximum_fusion.1
  708.8 13.6 %collective-permute-done.34 = bf16[4,96,1536]{2,1,0:T(8,128)(2,1)} collective-permute-done((bf16[4,96,1536]{2,1,0:T(8,128)(2,1)}, bf16[4,96,1536]{2,1,0:T(8,128)(2,1)}, u32[]{:S(2)}, u32[]{:S(2)}) %collective-permute-start.34) | collective-permute-done | bytes 1179680 | tf_op jit(solution)/shard_map/ppermute | solution.py:34
  731.1 6.6 convolution_convert_fusion.6
  737.7 6.7 convolution_convert_fusion.7
  752.1 7.1 fusion.35
  760.7 6.0 convolution_add_fusion.5
  769.8 44.4 %collective-permute-done.40 = bf16[384,768]{1,0:T(8,128)(2,1)S(1)} collective-permute-done((bf16[384,768]{1,0:T(8,128)(2,1)}, bf16[384,768]{1,0:T(8,128)(2,1)S(1)}, u32[]{:S(2)}, u32[]{:S(2)}) %collective-permute-start.40) | collective-permute-done | bytes 589856 | tf_op jit(solution)/shard_map/ppermute | solution.py:34
  821.9 22.3 %collective-permute-done.46 = bf16[4,96,1536]{2,1,0:T(8,128)(2,1)S(1)} collective-permute-done((bf16[4,96,1536]{2,1,0:T(8,128)(2,1)S(1)}, bf16[4,96,1536]{2,1,0:T(8,128)(2,1)S(1)}, u32[]{:S(2)}, u32[]{:S(2)}) %collective-permute-start.46) | collective-permute-done | bytes 1179680 | tf_op jit(solution)/shard_map/ppermute | solution.py:34
  855.0 3.9 pad_maximum_fusion.2.refs_0_.refs_1_.own_ref
  859.7 30.0 %collective-permute-done.50 = bf16[512,1536]{1,0:T(8,128)(2,1)S(1)} collective-permute-done((bf16[512,1536]{1,0:T(8,128)(2,1)}, bf16[512,1536]{1,0:T(8,128)(2,1)S(1)}, u32[]{:S(2)}, u32[]{:S(2)}) %collective-permute-start.50) | collective-permute-done | bytes 1572896 | tf_op jit(solution)/shard_map/ppermute | solution.py:56
  895.6 8.7 collective-permute-done.49
  928.1 3.6 collective-permute-done.58
  939.0 3.2 collective-permute-done.61
  944.7 10.0 %shard_map.340 = f32[1536,1536]{1,0:T(8,128)} custom-call(s32[5]{0:T(128)S(1)} %copy-done.23, bf16[4,384,1536]{2,1,0:T(8,128)(2,1)} %pad_maximum_fusion.2.refs_0_.refs_1_.own_ref, bf16[4,384,1536]{2,1,0:T(8,128)(2,1)} %collective-permute-done.55.refs_2_.refs_3_.other_ref), custom_call_target="tpu_custom_call" | custom-call | tf_op jit(solution)/shard_map/pallas_call | solution.py:565
  954.7 6.2 shard_map.339
  967.1 3.6 shard_map.342
  970.7 4.0 shard_map.341
  975.9 3.8 collective-permute-done.65.refs_3_.refs_4_.refs_5_.refs_2_
  979.7 3.6 shard_map.344
  983.3 4.0 shard_map.343
  (569 shorter events, 246.1 us)
Async XLA Ops:
  7.2 52.6 %all-gather.8.cloned.1.call-start = ((), (), s32[]{:S(2)}) async-start(), calls=%async_computation.7 | async-start | bytes 2211840 | tf_op jit(solution)/shard_map/all_gather | solution.py:354
  16.6 104.5 %all-gather.10.cloned.1.call-start = ((), (), s32[]{:S(2)}) async-start(), calls=%async_computation.8 | async-start | bytes 3686400 | tf_op jit(solution)/shard_map/all_gather | solution.py:354
  16.7 6.1 collective-permute-start.1
  17.2 44.1 %collective-permute-start = (bf16[512,1536]{1,0:T(8,128)(2,1)S(1)}, bf16[512,1536]{1,0:T(8,128)(2,1)}, u32[]{:S(2)}, u32[]{:S(2)}) collective-permute-start(bf16[512,1536]{1,0:T(8,128)(2,1)S(1)} %bitcast.237), channel_id=1, source_target_pairs={{0,16},{1,17},{2,18},{3,19},{4,20},{5,21},{6,22},{7,23},{8,24},{9,... | collective-permute-start | bytes 4718600 | tf_op jit(solution)/shard_map/ppermute | solution.py:56
  61.3 259.3 %all-gather.6.cloned.1.call-start = ((), (), s32[]{:S(2)}) async-start(), calls=%async_computation.3 | async-start | bytes 10616832 | tf_op jit(solution)/shard_map/all_gather | solution.py:809
  61.4 35.0 %collective-permute-start.4 = (bf16[512,1536]{1,0:T(8,128)(2,1)}, bf16[512,1536]{1,0:T(8,128)(2,1)}, u32[]{:S(2)}, u32[]{:S(2)}) collective-permute-start(bf16[512,1536]{1,0:T(8,128)(2,1)} %collective-permute-done), channel_id=1, source_target_pairs={{0,1},{1,0},{2,3},{3,2},{4,5},{5,4},{6,7},{7,6},{8,9},{9,8},{10,11... | collective-permute-start | bytes 4718600 | tf_op jit(solution)/shard_map/ppermute | solution.py:34
  61.5 32.0 %collective-permute-start.3 = (bf16[3,96,2304]{2,1,0:T(8,128)(2,1)S(1)}, bf16[3,96,2304]{2,1,0:T(8,128)(2,1)S(1)}, u32[]{:S(2)}, u32[]{:S(2)}) collective-permute-start(bf16[3,96,2304]{2,1,0:T(8,128)(2,1)S(1)} %pad_maximum_fusion.29.refs_3_), channel_id=1, source_target_pairs={{0,16},{16,0},{1,17},{17,1},{2,18},{18,2},{3,19},{19,3},{4,20},{20... | collective-permute-start | bytes 3981320 | tf_op jit(solution)/shard_map/ppermute | solution.py:34
  63.0 31.4 %collective-permute-start.2 = (bf16[3,96,2304]{2,1,0:T(8,128)(2,1)S(1)}, bf16[3,96,2304]{2,1,0:T(8,128)(2,1)}, u32[]{:S(2)}, u32[]{:S(2)}) collective-permute-start(bf16[3,96,2304]{2,1,0:T(8,128)(2,1)S(1)} %pad_maximum_fusion.29.refs_3_), channel_id=1, source_target_pairs={{0,2},{2,0},{1,3},{3,1},{4,6},{6,4},{5,7},{7,5},{8,10},{10,8},{9,1... | collective-permute-start | bytes 3981320 | tf_op jit(solution)/shard_map/ppermute | solution.py:34
  65.0 4.5 collective-permute-start.8
  68.3 5.6 collective-permute-start.9
  69.6 57.7 %collective-permute-start.10 = (bf16[512,1536]{1,0:T(8,128)(2,1)}, bf16[512,1536]{1,0:T(8,128)(2,1)}, u32[]{:S(2)}, u32[]{:S(2)}) collective-permute-start(bf16[512,1536]{1,0:T(8,128)(2,1)} %bitcast.244), channel_id=1, source_target_pairs={{0,16},{16,0},{1,17},{17,1},{2,18},{18,2},{3,19},{19,3},{4,20},{20... | collective-permute-start | bytes 4718600 | tf_op jit(solution)/shard_map/ppermute | solution.py:34
  98.7 28.6 %collective-permute-start.5 = (bf16[3,96,1152]{2,1,0:T(8,128)(2,1)}, bf16[3,96,1152]{2,1,0:T(8,128)(2,1)S(1)}, u32[]{:S(2)}, u32[]{:S(2)}) collective-permute-start(bf16[3,96,1152]{2,1,0:T(8,128)(2,1)} %slice.432), channel_id=1, source_target_pairs={{0,2},{2,0},{1,3},{3,1},{4,6},{6,4},{5,7},{7,5},{8,10},{10,8},{9,1... | collective-permute-start | bytes 1990664 | tf_op jit(solution)/shard_map/ppermute | solution.py:34
  100.2 40.8 %collective-permute-start.6 = (bf16[3,96,1152]{2,1,0:T(8,128)(2,1)}, bf16[3,96,1152]{2,1,0:T(8,128)(2,1)}, u32[]{:S(2)}, u32[]{:S(2)}) collective-permute-start(bf16[3,96,1152]{2,1,0:T(8,128)(2,1)} %slice.433), channel_id=1, source_target_pairs={{0,16},{16,0},{1,17},{17,1},{2,18},{18,2},{3,19},{19,3},{4,20},{20... | collective-permute-start | bytes 1990664 | tf_op jit(solution)/shard_map/ppermute | solution.py:34
  141.1 489.4 %reduce-scatter.4.cloned.1.call-start = ((), (), s32[]{:S(2)}) async-start(), calls=%async_computation.4 | async-start | bytes 10616832 | tf_op jit(solution)/shard_map/reduce_scatter | solution.py:876
  141.4 66.5 %collective-permute-start.12 = (bf16[3,96,3840]{2,1,0:T(8,128)(2,1)}, bf16[3,96,3840]{2,1,0:T(8,128)(2,1)S(1)}, u32[]{:S(2)}, u32[]{:S(2)}) collective-permute-start(bf16[3,96,3840]{2,1,0:T(8,128)(2,1)} %pad_maximum_fusion.16.refs_5_), channel_id=1, source_target_pairs={{0,16},{16,0},{1,17},{17,1},{2,18},{18,2},{3,19},{19,3},{4,20},{20... | collective-permute-start | bytes 6635528 | tf_op jit(solution)/shard_map/ppermute | solution.py:34
  142.9 66.9 %collective-permute-start.11 = (bf16[3,96,3840]{2,1,0:T(8,128)(2,1)}, bf16[3,96,3840]{2,1,0:T(8,128)(2,1)}, u32[]{:S(2)}, u32[]{:S(2)}) collective-permute-start(bf16[3,96,3840]{2,1,0:T(8,128)(2,1)} %pad_maximum_fusion.16.refs_5_), channel_id=1, source_target_pairs={{0,2},{2,0},{1,3},{3,1},{4,6},{6,4},{5,7},{7,5},{8,10},{10,8},{9,1... | collective-permute-start | bytes 6635528 | tf_op jit(solution)/shard_map/ppermute | solution.py:34
  211.6 50.0 %collective-permute-start.13 = (bf16[3,96,1920]{2,1,0:T(8,128)(2,1)S(1)}, bf16[3,96,1920]{2,1,0:T(8,128)(2,1)S(1)}, u32[]{:S(2)}, u32[]{:S(2)}) collective-permute-start(bf16[3,96,1920]{2,1,0:T(8,128)(2,1)S(1)} %slice.436), channel_id=1, source_target_pairs={{0,2},{2,0},{1,3},{3,1},{4,6},{6,4},{5,7},{7,5},{8,10},{10,8},{9,1... | collective-permute-start | bytes 3317768 | tf_op jit(solution)/shard_map/ppermute | solution.py:34
  213.7 47.9 %collective-permute-start.14 = (bf16[3,96,1920]{2,1,0:T(8,128)(2,1)S(1)}, bf16[3,96,1920]{2,1,0:T(8,128)(2,1)S(1)}, u32[]{:S(2)}, u32[]{:S(2)}) collective-permute-start(bf16[3,96,1920]{2,1,0:T(8,128)(2,1)S(1)} %slice.437), channel_id=1, source_target_pairs={{0,16},{16,0},{1,17},{17,1},{2,18},{18,2},{3,19},{19,3},{4,20},{20... | collective-permute-start | bytes 3317768 | tf_op jit(solution)/shard_map/ppermute | solution.py:34
  291.5 4.5 collective-permute-start.16
  325.6 12.6 %collective-permute-start.22 = (bf16[512,1536]{1,0:T(8,128)(2,1)S(1)}, bf16[512,1536]{1,0:T(8,128)(2,1)S(1)}, u32[]{:S(2)}, u32[]{:S(2)}) collective-permute-start(bf16[512,1536]{1,0:T(8,128)(2,1)S(1)} %bitcast.245), channel_id=1, source_target_pairs={{0,1},{1,0},{2,3},{3,2},{4,5},{5,4},{6,7},{7,6},{8,9},{9,8},{10,11... | collective-permute-start | bytes 4718600 | tf_op jit(solution)/shard_map/ppermute | solution.py:34
  325.9 38.3 %collective-permute-start.19 = (bf16[512,1536]{1,0:T(8,128)(2,1)}, bf16[512,1536]{1,0:T(8,128)(2,1)S(1)}, u32[]{:S(2)}, u32[]{:S(2)}) collective-permute-start(bf16[512,1536]{1,0:T(8,128)(2,1)} %collective-permute-done.10), channel_id=1, source_target_pairs={{0,1},{1,0},{2,3},{3,2},{4,5},{5,4},{6,7},{7,6},{8,9},{9,8},{10,11... | collective-permute-start | bytes 4718600 | tf_op jit(solution)/shard_map/ppermute | solution.py:34
  326.1 36.7 %collective-permute-start.20 = (bf16[512,1536]{1,0:T(8,128)(2,1)S(1)}, bf16[512,1536]{1,0:T(8,128)(2,1)S(1)}, u32[]{:S(2)}, u32[]{:S(2)}) collective-permute-start(bf16[512,1536]{1,0:T(8,128)(2,1)S(1)} %add_convert_fusion.5), channel_id=1, source_target_pairs={{0,16},{16,0},{1,17},{17,1},{2,18},{18,2},{3,19},{19,3},{4,20},{20... | collective-permute-start | bytes 4718600 | tf_op jit(solution)/shard_map/ppermute | solution.py:34
  362.8 4.4 collective-permute-start.23
  387.6 5.9 collective-permute-start.24
  398.5 46.3 %collective-permute-start.25 = (bf16[512,1536]{1,0:T(8,128)(2,1)}, bf16[512,1536]{1,0:T(8,128)(2,1)}, u32[]{:S(2)}, u32[]{:S(2)}) collective-permute-start(bf16[512,1536]{1,0:T(8,128)(2,1)} %fusion.34), channel_id=1, source_target_pairs={{0,16},{16,0},{1,17},{17,1},{2,18},{18,2},{3,19},{19,3},{4,20},{20... | collective-permute-start | bytes 4718600 | tf_op jit(solution)/shard_map/ppermute | solution.py:34
  442.8 406.6 %reduce-scatter.6.cloned.1.call-start = ((), (), s32[]{:S(2)}) async-start(), calls=%async_computation.5 | async-start | bytes 2949120 | tf_op jit(solution)/shard_map/reduce_scatter | solution.py:459
  452.3 9.5 collective-permute-start.26
  461.6 42.0 %collective-permute-start.32 = (bf16[1024,1536]{1,0:T(8,128)(2,1)S(1)}, bf16[1024,1536]{1,0:T(8,128)(2,1)}, u32[]{:S(2)}, u32[]{:S(2)}) collective-permute-start(bf16[1024,1536]{1,0:T(8,128)(2,1)S(1)} %pad_maximum_fusion.11), channel_id=1, source_target_pairs={{0,1},{1,0},{2,3},{3,2},{4,5},{5,4},{6,7},{7,6},{8,9},{9,8},{10,11... | collective-permute-start | bytes 9437192 | tf_op jit(solution)/shard_map/ppermute | solution.py:34
  481.2 12.8 %collective-permute-start.27 = (bf16[2,64,1536]{2,1,0:T(8,128)(2,1)S(1)}, bf16[2,64,1536]{2,1,0:T(8,128)(2,1)S(1)}, u32[]{:S(2)}, u32[]{:S(2)}) collective-permute-start(bf16[2,64,1536]{2,1,0:T(8,128)(2,1)S(1)} %maximum_bitcast_fusion.3), channel_id=1, source_target_pairs={{0,16},{16,0},{1,17},{17,1},{2,18},{18,2},{3,19},{19,3},{4,20},{20... | collective-permute-start | bytes 1179656 | tf_op jit(solution)/shard_map/ppermute | solution.py:34
  503.5 8.5 collective-permute-start.30
  511.8 37.3 %collective-permute-start.33 = (bf16[512,1536]{1,0:T(8,128)(2,1)S(1)}, bf16[512,1536]{1,0:T(8,128)(2,1)S(1)}, u32[]{:S(2)}, u32[]{:S(2)}) collective-permute-start(bf16[512,1536]{1,0:T(8,128)(2,1)S(1)} %fusion.32), channel_id=1, source_target_pairs={{0,16},{16,0},{1,17},{17,1},{2,18},{18,2},{3,19},{19,3},{4,20},{20... | collective-permute-start | bytes 4718600 | tf_op jit(solution)/shard_map/ppermute | solution.py:34
  517.5 38.4 %collective-permute-start.31 = (bf16[512,1536]{1,0:T(8,128)(2,1)S(1)}, bf16[512,1536]{1,0:T(8,128)(2,1)S(1)}, u32[]{:S(2)}, u32[]{:S(2)}) collective-permute-start(bf16[512,1536]{1,0:T(8,128)(2,1)S(1)} %get-tuple-element.307), channel_id=1, source_target_pairs={{0,1},{1,0},{2,3},{3,2},{4,5},{5,4},{6,7},{7,6},{8,9},{9,8},{10,11... | collective-permute-start | bytes 4718600 | tf_op jit(solution)/shard_map/ppermute | solution.py:34
  520.3 79.0 %collective-permute-start.28 = (bf16[4,2,96,1536]{3,2,0,1:T(8,128)(2,1)S(1)}, bf16[4,2,96,1536]{3,2,0,1:T(8,128)(2,1)}, u32[]{:S(2)}, u32[]{:S(2)}) collective-permute-start(bf16[4,2,96,1536]{3,2,0,1:T(8,128)(2,1)S(1)} %maximum_maximum_fusion.2), channel_id=1, source_target_pairs={{0,16},{16,0},{1,17},{17,1},{2,18},{18,2},{3,19},{19,3},{4,20},{20... | collective-permute-start | bytes 7077896 | tf_op jit(solution)/shard_map/ppermute | solution.py:34
  522.0 84.1 %collective-permute-start.29 = (bf16[4,2,96,1536]{3,2,0,1:T(8,128)(2,1)S(1)}, bf16[4,2,96,1536]{3,2,0,1:T(8,128)(2,1)}, u32[]{:S(2)}, u32[]{:S(2)}) collective-permute-start(bf16[4,2,96,1536]{3,2,0,1:T(8,128)(2,1)S(1)} %maximum_maximum_fusion.3), channel_id=1, source_target_pairs={{0,2},{2,0},{1,3},{3,1},{4,6},{6,4},{5,7},{7,5},{8,10},{10,8},{9,1... | collective-permute-start | bytes 7077896 | tf_op jit(solution)/shard_map/ppermute | solution.py:34
  630.4 93.5 %collective-permute-start.37 = (bf16[384,1536]{1,0:T(8,128)(2,1)}, bf16[384,1536]{1,0:T(8,128)(2,1)}, u32[]{:S(2)}, u32[]{:S(2)}) collective-permute-start(bf16[384,1536]{1,0:T(8,128)(2,1)} %reduce-scatter.4.cloned.1.call-done), channel_id=1, source_target_pairs={{0,16},{16,0},{1,17},{17,1},{2,18},{18,2},{3,19},{19,3},{4,20},{20... | collective-permute-start | bytes 3538952 | tf_op jit(solution)/shard_map/ppermute | solution.py:34
  631.9 97.3 %collective-permute-start.36 = (bf16[384,1536]{1,0:T(8,128)(2,1)}, bf16[384,1536]{1,0:T(8,128)(2,1)}, u32[]{:S(2)}, u32[]{:S(2)}) collective-permute-start(bf16[384,1536]{1,0:T(8,128)(2,1)} %reduce-scatter.4.cloned.1.call-done), channel_id=1, source_target_pairs={{0,2},{2,0},{1,3},{3,1},{4,6},{6,4},{5,7},{7,5},{8,10},{10,8},{9,1... | collective-permute-start | bytes 3538952 | tf_op jit(solution)/shard_map/ppermute | solution.py:34
  694.9 27.5 %collective-permute-start.34 = (bf16[4,96,1536]{2,1,0:T(8,128)(2,1)}, bf16[4,96,1536]{2,1,0:T(8,128)(2,1)}, u32[]{:S(2)}, u32[]{:S(2)}) collective-permute-start(bf16[4,96,1536]{2,1,0:T(8,128)(2,1)} %dynamic-slice_bitcast_fusion.3), channel_id=1, source_target_pairs={{0,2},{2,0},{1,3},{3,1},{4,6},{6,4},{5,7},{7,5},{8,10},{10,8},{9,1... | collective-permute-start | bytes 3538952 | tf_op jit(solution)/shard_map/ppermute | solution.py:34
  698.3 27.5 %collective-permute-start.35 = (bf16[4,96,1536]{2,1,0:T(8,128)(2,1)S(1)}, bf16[4,96,1536]{2,1,0:T(8,128)(2,1)}, u32[]{:S(2)}, u32[]{:S(2)}) collective-permute-start(bf16[4,96,1536]{2,1,0:T(8,128)(2,1)S(1)} %dynamic-slice_bitcast_fusion.2), channel_id=1, source_target_pairs={{0,16},{16,0},{1,17},{17,1},{2,18},{18,2},{3,19},{19,3},{4,20},{20... | collective-permute-start | bytes 3538952 | tf_op jit(solution)/shard_map/ppermute | solution.py:34
  737.7 13.1 %collective-permute-start.44 = (bf16[512,1536]{1,0:T(8,128)(2,1)}, bf16[512,1536]{1,0:T(8,128)(2,1)}, u32[]{:S(2)}, u32[]{:S(2)}) collective-permute-start(bf16[512,1536]{1,0:T(8,128)(2,1)} %convolution_convert_fusion.6), channel_id=1, source_target_pairs={{0,1},{1,0},{2,3},{3,2},{4,5},{5,4},{6,7},{7,6},{8,9},{9,8},{10,11... | collective-permute-start | bytes 4718600 | tf_op jit(solution)/shard_map/ppermute | solution.py:34
  744.4 14.7 %collective-permute-start.43 = (bf16[512,1536]{1,0:T(8,128)(2,1)}, bf16[512,1536]{1,0:T(8,128)(2,1)}, u32[]{:S(2)}, u32[]{:S(2)}) collective-permute-start(bf16[512,1536]{1,0:T(8,128)(2,1)} %convolution_convert_fusion.7), channel_id=1, source_target_pairs={{0,1},{1,0},{2,3},{3,2},{4,5},{5,4},{6,7},{7,6},{8,9},{9,8},{10,11... | collective-permute-start | bytes 4718600 | tf_op jit(solution)/shard_map/ppermute | solution.py:34
  747.4 19.3 %collective-permute-start.42 = (bf16[512,1536]{1,0:T(8,128)(2,1)}, bf16[512,1536]{1,0:T(8,128)(2,1)S(1)}, u32[]{:S(2)}, u32[]{:S(2)}) collective-permute-start(bf16[512,1536]{1,0:T(8,128)(2,1)} %convolution_convert_fusion.8), channel_id=1, source_target_pairs={{0,1},{1,0},{2,3},{3,2},{4,5},{5,4},{6,7},{7,6},{8,9},{9,8},{10,11... | collective-permute-start | bytes 4718600 | tf_op jit(solution)/shard_map/ppermute | solution.py:34
  747.5 66.7 %collective-permute-start.38 = (bf16[4,2,96,1536]{3,2,0,1:T(8,128)(2,1)}, bf16[4,2,96,1536]{3,2,0,1:T(8,128)(2,1)}, u32[]{:S(2)}, u32[]{:S(2)}) collective-permute-start(bf16[4,2,96,1536]{3,2,0,1:T(8,128)(2,1)} %maximum_maximum_fusion.6), channel_id=1, source_target_pairs={{0,16},{16,0},{1,17},{17,1},{2,18},{18,2},{3,19},{19,3},{4,20},{20... | collective-permute-start | bytes 7077896 | tf_op jit(solution)/shard_map/ppermute | solution.py:34
  748.1 66.1 %collective-permute-start.39 = (bf16[4,2,96,1536]{3,2,0,1:T(8,128)(2,1)}, bf16[4,2,96,1536]{3,2,0,1:T(8,128)(2,1)}, u32[]{:S(2)}, u32[]{:S(2)}) collective-permute-start(bf16[4,2,96,1536]{3,2,0,1:T(8,128)(2,1)} %maximum_maximum_fusion.7), channel_id=1, source_target_pairs={{0,2},{2,0},{1,3},{3,1},{4,6},{6,4},{5,7},{7,5},{8,10},{10,8},{9,1... | collective-permute-start | bytes 7077896 | tf_op jit(solution)/shard_map/ppermute | solution.py:34
  750.5 155.3 %reduce-scatter.8.cloned.1.call-start = ((), (), s32[]{:S(2)}) async-start(), calls=%async_computation.6 | async-start | bytes 2949120 | tf_op jit(solution)/shard_map/reduce_scatter | solution.py:459
  750.8 63.4 %collective-permute-start.40 = (bf16[384,768]{1,0:T(8,128)(2,1)}, bf16[384,768]{1,0:T(8,128)(2,1)S(1)}, u32[]{:S(2)}, u32[]{:S(2)}) collective-permute-start(bf16[384,768]{1,0:T(8,128)(2,1)} %slice.476), channel_id=1, source_target_pairs={{0,2},{2,0},{1,3},{3,1},{4,6},{6,4},{5,7},{7,5},{8,10},{10,8},{9,1... | collective-permute-start | bytes 1769480 | tf_op jit(solution)/shard_map/ppermute | solution.py:34
  759.1 55.0 %collective-permute-start.41 = (bf16[384,768]{1,0:T(8,128)(2,1)S(1)}, bf16[384,768]{1,0:T(8,128)(2,1)S(1)}, u32[]{:S(2)}, u32[]{:S(2)}) collective-permute-start(bf16[384,768]{1,0:T(8,128)(2,1)S(1)} %copy-done.77), channel_id=1, source_target_pairs={{0,16},{16,0},{1,17},{17,1},{2,18},{18,2},{3,19},{19,3},{4,20},{20... | collective-permute-start | bytes 1769480 | tf_op jit(solution)/shard_map/ppermute | solution.py:34
  817.1 27.2 %collective-permute-start.46 = (bf16[4,96,1536]{2,1,0:T(8,128)(2,1)S(1)}, bf16[4,96,1536]{2,1,0:T(8,128)(2,1)S(1)}, u32[]{:S(2)}, u32[]{:S(2)}) collective-permute-start(bf16[4,96,1536]{2,1,0:T(8,128)(2,1)S(1)} %dynamic-slice_bitcast_fusion.1), channel_id=1, source_target_pairs={{0,2},{2,0},{1,3},{3,1},{4,6},{6,4},{5,7},{7,5},{8,10},{10,8},{9,1... | collective-permute-start | bytes 3538952 | tf_op jit(solution)/shard_map/ppermute | solution.py:34
  820.4 26.9 %collective-permute-start.47 = (bf16[4,96,1536]{2,1,0:T(8,128)(2,1)S(1)}, bf16[4,96,1536]{2,1,0:T(8,128)(2,1)S(1)}, u32[]{:S(2)}, u32[]{:S(2)}) collective-permute-start(bf16[4,96,1536]{2,1,0:T(8,128)(2,1)S(1)} %dynamic-slice_bitcast_fusion), channel_id=1, source_target_pairs={{0,16},{16,0},{1,17},{17,1},{2,18},{18,2},{3,19},{19,3},{4,20},{20... | collective-permute-start | bytes 3538952 | tf_op jit(solution)/shard_map/ppermute | solution.py:34
  853.3 36.4 %collective-permute-start.50 = (bf16[512,1536]{1,0:T(8,128)(2,1)}, bf16[512,1536]{1,0:T(8,128)(2,1)S(1)}, u32[]{:S(2)}, u32[]{:S(2)}) collective-permute-start(bf16[512,1536]{1,0:T(8,128)(2,1)} %fusion.35), channel_id=1, source_target_pairs={{16,0},{17,1},{18,2},{19,3},{20,4},{21,5},{22,6},{23,7},{24,8},{25... | collective-permute-start | bytes 4718600 | tf_op jit(solution)/shard_map/ppermute | solution.py:56
  858.8 85.8 %collective-permute-start.55 = (bf16[4,384,1536]{2,1,0:T(8,128)(2,1)}, bf16[4,384,1536]{2,1,0:T(8,128)(2,1)}, u32[]{:S(2)}, u32[]{:S(2)}) collective-permute-start(bf16[4,384,1536]{2,1,0:T(8,128)(2,1)} %pad_maximum_fusion.2.refs_0_.refs_1_.own_ref), channel_id=1, source_target_pairs={{0,1},{1,0},{2,3},{3,2},{4,5},{5,4},{6,7},{7,6},{8,9},{9,8},{10,11... | collective-permute-start | bytes 14155784 | tf_op jit(solution)/shard_map/ppermute | solution.py:34
  891.8 12.4 %collective-permute-start.49 = (bf16[384,768]{1,0:T(8,128)(2,1)S(1)}, bf16[384,768]{1,0:T(8,128)(2,1)S(1)}, u32[]{:S(2)}, u32[]{:S(2)}) collective-permute-start(bf16[384,768]{1,0:T(8,128)(2,1)S(1)} %maximum_dynamic-update-slice_fusion.2), channel_id=1, source_target_pairs={{0,16},{16,0},{1,17},{17,1},{2,18},{18,2},{3,19},{19,3},{4,20},{20... | collective-permute-start | bytes 1769480 | tf_op jit(solution)/shard_map/ppermute | solution.py:34
  891.8 13.2 %collective-permute-start.48 = (bf16[384,768]{1,0:T(8,128)(2,1)S(1)}, bf16[384,768]{1,0:T(8,128)(2,1)S(1)}, u32[]{:S(2)}, u32[]{:S(2)}) collective-permute-start(bf16[384,768]{1,0:T(8,128)(2,1)S(1)} %maximum_dynamic-update-slice_fusion.2), channel_id=1, source_target_pairs={{0,2},{2,0},{1,3},{3,1},{4,6},{6,4},{5,7},{7,5},{8,10},{10,8},{9,1... | collective-permute-start | bytes 1769480 | tf_op jit(solution)/shard_map/ppermute | solution.py:34
  909.5 51.5 %collective-permute-start.52 = (bf16[384,768]{1,0:T(8,128)(2,1)S(1)}, bf16[384,768]{1,0:T(8,128)(2,1)S(1)}, u32[]{:S(2)}, u32[]{:S(2)}) collective-permute-start(bf16[384,768]{1,0:T(8,128)(2,1)S(1)} %maximum_dynamic-update-slice_fusion.4), channel_id=1, source_target_pairs={{0,16},{16,0},{1,17},{17,1},{2,18},{18,2},{3,19},{19,3},{4,20},{20... | collective-permute-start | bytes 1769480 | tf_op jit(solution)/shard_map/ppermute | solution.py:34
  910.5 50.4 %collective-permute-start.51 = (bf16[384,768]{1,0:T(8,128)(2,1)S(1)}, bf16[384,768]{1,0:T(8,128)(2,1)S(1)}, u32[]{:S(2)}, u32[]{:S(2)}) collective-permute-start(bf16[384,768]{1,0:T(8,128)(2,1)S(1)} %maximum_dynamic-update-slice_fusion.4), channel_id=1, source_target_pairs={{0,2},{2,0},{1,3},{3,1},{4,6},{6,4},{5,7},{7,5},{8,10},{10,8},{9,1... | collective-permute-start | bytes 1769480 | tf_op jit(solution)/shard_map/ppermute | solution.py:34
  922.5 4.1 collective-permute-start.57
  927.2 4.4 collective-permute-start.58
  933.1 5.1 collective-permute-start.60
  936.8 5.5 collective-permute-start.61
  938.1 22.9 %collective-permute-start.53 = (bf16[384,384]{1,0:T(8,128)(2,1)}, bf16[384,384]{1,0:T(8,128)(2,1)}, u32[]{:S(2)}, u32[]{:S(2)}) collective-permute-start(bf16[384,384]{1,0:T(8,128)(2,1)} %slice.488), channel_id=1, source_target_pairs={{0,2},{2,0},{1,3},{3,1},{4,6},{6,4},{5,7},{7,5},{8,10},{10,8},{9,1... | collective-permute-start | bytes 884744 | tf_op jit(solution)/shard_map/ppermute | solution.py:34
  942.9 18.2 %collective-permute-start.54 = (bf16[384,384]{1,0:T(8,128)(2,1)}, bf16[384,384]{1,0:T(8,128)(2,1)}, u32[]{:S(2)}, u32[]{:S(2)}) collective-permute-start(bf16[384,384]{1,0:T(8,128)(2,1)} %slice.489), channel_id=1, source_target_pairs={{0,16},{16,0},{1,17},{17,1},{2,18},{18,2},{3,19},{19,3},{4,20},{20... | collective-permute-start | bytes 884744 | tf_op jit(solution)/shard_map/ppermute | solution.py:34
  962.5 4.6 collective-permute-start.64
  962.5 12.2 %collective-permute-start.62 = (bf16[384,384]{1,0:T(8,128)(2,1)S(1)}, bf16[384,384]{1,0:T(8,128)(2,1)S(1)}, u32[]{:S(2)}, u32[]{:S(2)}) collective-permute-start(bf16[384,384]{1,0:T(8,128)(2,1)S(1)} %slice.498), channel_id=1, source_target_pairs={{0,2},{2,0},{1,3},{3,1},{4,6},{6,4},{5,7},{7,5},{8,10},{10,8},{9,1... | collective-permute-start | bytes 884744 | tf_op jit(solution)/shard_map/ppermute | solution.py:34
  963.4 11.3 %collective-permute-start.63 = (bf16[384,384]{1,0:T(8,128)(2,1)S(1)}, bf16[384,384]{1,0:T(8,128)(2,1)S(1)}, u32[]{:S(2)}, u32[]{:S(2)}) collective-permute-start(bf16[384,384]{1,0:T(8,128)(2,1)S(1)} %slice.499), channel_id=1, source_target_pairs={{0,16},{16,0},{1,17},{17,1},{2,18},{18,2},{3,19},{19,3},{4,20},{20... | collective-permute-start | bytes 884744 | tf_op jit(solution)/shard_map/ppermute | solution.py:34
  975.1 4.6 collective-permute-start.65
  (128 other events, 1837.8 us)
Sparse Core Ops, SparseCore 0:
  16.7 42.9 all-gather.7
  61.9 59.1 all-gather.9
  141.2 166.7 all-gather.5
  442.9 187.4 reduce-scatter.3
  750.6 46.9 reduce-scatter.5
  853.4 46.9 reduce-scatter.7
